TPU v7x, 256 devices: a whole 4x4x8 slice. The times are simulated.
256 devices in a mesh: sky: 32 (over z, y), grp: 8 (over x, core).
Axes of the slice: x: 4, y: 4, z: 8, core: 2. Of those that a mesh axis runs over, the one named last changes fastest.
Arguments:
- pixels: float32 [8, 2048, 16, 512], P('grp', 'sky'), may hold values from -6 to 6
- mask_bits: int32 [8, 2048, 512], P('grp', 'sky'), may hold values from 0 to 7, as said below
- owner: int32 [8, 2048], P('grp', 'sky'), may hold values from 0 to 31, as said below
- row_offset: int32 [8, 2048], P('grp', 'sky'), may hold values from 0 to 48
- seg_weight: float32 [8, 2048], P('grp', 'sky'), may hold values from 0.01 to 0.2
- psf_bank: float32 [8, 2, 21], replicated, may hold values from -1.25 to 1.25
- basis_index: int32 [8, 3], P('grp'), may hold values from 0 to 7
- basis_coeff: float32 [8, 3], P('grp'), may hold values from -3 to 3
- row_base: int32 [8, 16], P('grp'), may hold values from 0 to 14
- row_frac: float32 [8, 16], P('grp'), may hold values from 0 to 1
- col_base: int32 [8, 512], P('grp'), may hold values from 0 to 510
- col_frac: float32 [8, 512], P('grp'), may hold values from 0 to 1
Outputs:
- coadd: float32 [2048, 512], P(('sky', 'grp'))
Inputs may be any that keep to these rules, and one draw needn't show every extreme that they name: Each device of an exposure group holds at most 8 segments of one owner; in each exposure one owner holds exactly 8 segments in every aligned block of 64 segments. `mask_bits`: bit 0 marks bad columns, bit 1 saturated ones, bit 2 cosmic-ray hits.
All inputs are finite; a program needn't handle non-finite values.
Results may differ from a plain program's by a relative error of at most 0.00012.
Values sent between devices are 32-bit elements; how exact they have to be, the bound alone decides.
No kernel may reach another device: no remote copies, remote signals or barrier semaphores. Data moves between devices by JAX's collectives and lax.ppermute only.
A program may use at most 128 MiB of HBM per device.

v0:
```python
import jax
import jax.numpy as jnp
from jax import lax
from jax.sharding import PartitionSpec as P

PATCH = 64
CAP = 8


highest = lax.Precision.HIGHEST


def taps_matrix(profile, offsets):
    result = jnp.zeros(offsets.shape, jnp.float32)
    for tap_index in range(profile.shape[0]):
        result = result + profile[tap_index] * (offsets == tap_index).astype(jnp.float32)
    return result


def warp_matrix(base_index, fraction, length):
    source = jnp.arange(length, dtype=jnp.int32)[:, None]
    lower = (source == base_index[None, :]).astype(jnp.float32)
    higher = (source == base_index[None, :] + 1).astype(jnp.float32)
    return (1.0 - fraction)[None, :] * lower + fraction[None, :] * higher


def column_factor(mask_bits):
    bad_flag = (mask_bits % 2).astype(jnp.float32)
    full_flag = (mask_bits // 2 % 2).astype(jnp.float32)
    cosmic_flag = (mask_bits // 4 % 2).astype(jnp.float32)
    return (1.0 - bad_flag) * (1.0 - 0.75 * full_flag) * (1.0 - 0.5 * cosmic_flag)


def exposure_tables(
    psf_bank, basis_index, row_base, row_frac, col_base, col_frac, strip_rows, strip_width
):
    bank_lead = jnp.arange(psf_bank.shape[0], dtype=jnp.int32)
    picker = (basis_index[:, None] == bank_lead[None, :]).astype(jnp.float32)
    profiles = jnp.einsum("kb,bst->kst", picker, psf_bank, precision=highest)
    reach = (psf_bank.shape[2] - 1) // 2
    row_lead = jnp.arange(strip_rows, dtype=jnp.int32)
    col_lead = jnp.arange(strip_width, dtype=jnp.int32)
    column_warp = warp_matrix(col_base, col_frac, strip_width)
    row_warp = warp_matrix(row_base, row_frac, strip_rows).T
    row_list = []
    col_list = []
    for basis_term in range(profiles.shape[0]):
        row_list.append(
            taps_matrix(profiles[basis_term, 0], row_lead[None, :] - row_lead[:, None] + reach)
        )
        banded = taps_matrix(profiles[basis_term, 1], col_lead[:, None] - col_lead[None, :] + reach)
        col_list.append(jnp.dot(banded, column_warp, precision=highest))
    return (jnp.stack(row_list), jnp.stack(col_list), column_warp, row_warp)


def match_psf(images, factors, row_mats, col_mats, coeffs, column_warp):
    result = jnp.zeros(images.shape, jnp.float32)
    for basis_term in range(row_mats.shape[0]):
        row_pass = jnp.einsum("ia,naw->niw", row_mats[basis_term], images, precision=highest)
        result = result + coeffs[basis_term] * jnp.einsum(
            "niw,wj->nij", row_pass, col_mats[basis_term], precision=highest
        )
    coverage = jnp.dot(factors, column_warp, precision=highest)
    return (result, coverage)


def cover_rows(coverage, weights, starts, length, row_warp):
    strip_rows = row_warp.shape[0]
    spread = jnp.sum(row_warp, axis=1)
    target = starts[None, :, None] + jnp.arange(strip_rows, dtype=jnp.int32)[None, None, :]
    put_matrix = (jnp.arange(length, dtype=jnp.int32)[:, None, None] == target).astype(jnp.float32)
    shares = jnp.einsum("lni,i->ln", put_matrix, spread, precision=highest) * weights[None, :]
    return jnp.dot(shares, coverage, precision=highest)


def place(matched, coverage, weights, starts, length, row_warp):
    strip_rows = row_warp.shape[0]
    lifted = (
        jnp.einsum("ia,naw->niw", row_warp, matched, precision=highest) * weights[:, None, None]
    )
    target = starts[None, :, None] + jnp.arange(strip_rows, dtype=jnp.int32)[None, None, :]
    put_matrix = (jnp.arange(length, dtype=jnp.int32)[:, None, None] == target).astype(jnp.float32)
    numer = jnp.einsum("lni,niw->lw", put_matrix, lifted, precision=highest)
    denom = cover_rows(coverage, weights, starts, length, row_warp)
    return (numer, denom)


def dispatch(owners, sky_count):
    segment_count = owners.shape[0]
    order_index = jnp.arange(segment_count, dtype=jnp.int32)
    same_owner = owners[:, None] == owners[None, :]
    earlier = order_index[:, None] < order_index[None, :]
    ranking = jnp.sum((same_owner & earlier).astype(jnp.int32), axis=0)
    slot_index = owners * CAP + ranking
    chosen = (jnp.arange(sky_count * CAP, dtype=jnp.int32)[:, None] == slot_index[None, :]).astype(
        jnp.int32
    )
    source_rows = jnp.sum(chosen * order_index[None, :], axis=1)
    live_slots = jnp.sum(chosen, axis=1)
    return (source_rows, live_slots)


def per_device(
    pixels,
    mask_bits,
    owner,
    row_offset,
    seg_weight,
    psf_bank,
    basis_index,
    basis_coeff,
    row_base,
    row_frac,
    col_base,
    col_frac,
):
    sky_count = lax.axis_size("sky")
    strip_rows = pixels.shape[2]
    strip_width = pixels.shape[3]
    row_mats, col_mats, column_warp, row_warp = exposure_tables(
        psf_bank,
        basis_index[0],
        row_base[0],
        row_frac[0],
        col_base[0],
        col_frac[0],
        strip_rows,
        strip_width,
    )
    coeffs = basis_coeff[0]
    factors = column_factor(mask_bits[0])
    masked = pixels[0] * factors[:, None, :]
    owners = owner[0]
    offsets = row_offset[0]
    weights = seg_weight[0]
    source_rows, live_slots = dispatch(owners, sky_count)
    live_float = live_slots.astype(jnp.float32)
    slot_weight = (jnp.take(weights, source_rows) * live_float).reshape(sky_count, CAP)
    slot_offset = (
        (jnp.take(offsets, source_rows) * live_slots).astype(jnp.float32).reshape(sky_count, CAP)
    )
    slot_total = sky_count * CAP
    slot_image = (jnp.take(masked, source_rows, axis=0) * live_float[:, None, None]).reshape(
        sky_count, CAP, strip_rows, strip_width
    )
    slot_factor = (jnp.take(factors, source_rows, axis=0) * live_float[:, None]).reshape(
        sky_count, CAP, strip_width
    )
    image_part = lax.all_to_all(slot_image, "sky", split_axis=0, concat_axis=0, tiled=True)
    factor_part = lax.all_to_all(slot_factor, "sky", split_axis=0, concat_axis=0, tiled=True)
    weight_part = lax.all_to_all(slot_weight, "sky", split_axis=0, concat_axis=0, tiled=True)
    offset_part = lax.all_to_all(slot_offset, "sky", split_axis=0, concat_axis=0, tiled=True)
    lead_count = image_part.shape[0]
    item_count = image_part.shape[1]
    matched, coverage = match_psf(
        image_part.reshape(lead_count * item_count, strip_rows, strip_width),
        factor_part.reshape(lead_count * item_count, strip_width),
        row_mats,
        col_mats,
        coeffs,
        column_warp,
    )
    got_image = matched.reshape(lead_count, item_count, strip_rows, strip_width)
    got_cover = coverage.reshape(lead_count, item_count, strip_width)
    numer, denom = place(
        got_image.reshape(slot_total, strip_rows, strip_width),
        got_cover.reshape(slot_total, strip_width),
        weight_part.reshape(slot_total),
        offset_part.reshape(slot_total).astype(jnp.int32),
        PATCH,
        row_warp,
    )
    numer, denom = (
        lax.psum_scatter(numer, "grp", scatter_dimension=0, tiled=True),
        lax.psum_scatter(denom, "grp", scatter_dimension=0, tiled=True),
    )
    return numer / jnp.maximum(denom, 1.0)


def solution(mesh):
    placed = (
        P("grp", "sky", None, None),
        P("grp", "sky", None),
        P("grp", "sky"),
        P("grp", "sky"),
        P("grp", "sky"),
        P(),
        P("grp", None),
        P("grp", None),
        P("grp", None),
        P("grp", None),
        P("grp", None),
        P("grp", None),
    )
    return jax.shard_map(
        per_device, mesh=mesh, in_specs=placed, out_specs=P(("sky", "grp"), None), check_vma=False
    )
```

profile of v0, /device:TPU:8, one launch (start us, length us, event | category | flops | bytes accessed | tf_op | source)
XLA Modules:
  0.0 444.1 jit_solution(1906922742338459541)
XLA Ops:
  8.2 1.9 gather_fusion
  10.3 1.9 gather_fusion.2
  13.5 11.7 %all-to-all-start.2 = ((f32[32,1,8]{2,1,0:T(1,128)}), f32[32,1,8]{2,1,0:T(1,128)S(1)}, u32[]{:S(2)}, u32[]{:S(2)}) async-start(f32[32,1,8]{2,1,0:T(1,128)} %bitcast.161), calls=%async_computation.2 | async-start | bytes 32768 | tf_op jit(solution)/shard_map/all_to_all | solution.py:151
  25.3 1.2 fusion.383
  26.6 1.0 gather_fusion.3
  27.6 6.1 %all-to-all-done.2 = f32[32,1,8]{2,1,0:T(1,128)S(1)} async-done(((f32[32,1,8]{2,1,0:T(1,128)}), f32[32,1,8]{2,1,0:T(1,128)S(1)}, u32[]{:S(2)}, u32[]{:S(2)}) %all-to-all-start.2) | async-done | bytes 1056 | tf_op jit(solution)/shard_map/all_to_all | solution.py:151
  33.8 4.8 %all-to-all-start = ((f32[32,1,8]{2,1,0:T(1,128)}), f32[32,1,8]{2,1,0:T(1,128)S(1)}, u32[]{:S(2)}, u32[]{:S(2)}) async-start(f32[32,1,8]{2,1,0:T(1,128)} %bitcast.6), calls=%async_computation | async-start | bytes 32768 | tf_op jit(solution)/shard_map/all_to_all | solution.py:152
  38.5 0.9 fusion.233
  39.5 7.6 %all-to-all-done = f32[32,1,8]{2,1,0:T(1,128)S(1)} async-done(((f32[32,1,8]{2,1,0:T(1,128)}), f32[32,1,8]{2,1,0:T(1,128)S(1)}, u32[]{:S(2)}, u32[]{:S(2)}) %all-to-all-start) | async-done | bytes 1056 | tf_op jit(solution)/shard_map/all_to_all | solution.py:152
  47.7 5.0 %all-to-all-start.3 = ((f32[32,8,512]{2,1,0:T(8,128)}), f32[32,8,512]{2,1,0:T(8,128)S(1)}, u32[]{:S(2)}, u32[]{:S(2)}) async-start(f32[32,8,512]{2,1,0:T(8,128)} %fusion.233), calls=%async_computation.4 | async-start | bytes 1048576 | tf_op jit(solution)/shard_map/all_to_all | solution.py:150
  52.7 1.9 bitcast_multiply_fusion
  54.7 4.4 gather_fusion.1
  59.0 5.9 %select_multiply_fusion = f32[32,8,16,512]{3,2,1,0:T(8,128)} fusion(f32[32,8,16,512]{3,2,1,0:T(8,128)} %bitcast.235, f32[32,8]{1,0:T(8,128)S(1)} %convert_element_type.73, pred[32,8]{1,0:T(8,128)(4,1)S(1)} %compare_and_fusion), kind=kLoop, calls=%fused_computation.19 | loop fusion | flops 4194304 | bytes 16778496 | tf_op jit(solution)/shard_map/mul | solution.py:143
  64.9 2.5 all-to-all-done.3
  67.5 7.6 %all-to-all-start.1 = ((f32[32,8,16,512]{3,2,1,0:T(8,128)}), f32[32,8,16,512]{3,2,1,0:T(8,128)}, u32[]{:S(2)}, u32[]{:S(2)}) async-start(f32[32,8,16,512]{3,2,1,0:T(8,128)} %select_multiply_fusion), calls=%async_computation.1 | async-start | bytes 16777216 | tf_op jit(solution)/shard_map/all_to_all | solution.py:149
  81.7 15.9 %convolution_bitcast_fusion.1 = f32[512,512,1]{1,0,2:T(8,128)S(1)} fusion(f32[]{:T(128)} %bitcast.107, f32[]{:T(128)} %bitcast.106, f32[]{:T(128)} %bitcast.105, f32[]{:T(128)} %bitcast.104, f32[]{:T(128)} %bitcast.103, f32[]{:T(128)} %bitcast.102, f32[]{:T(128)} %bitcast.101, f32[]{:T(128)} %bitcast.100, f32[]{:T(128)} %bitcast.99, f32[]{:T(128)} %bitcast.98, ...), kind=kOutput, calls=%fused_computation.25 | convolution fusion | flops 1628700672 | bytes 1056852 | tf_op jit(solution)/shard_map/dot_general | solution.py:52
  97.6 16.7 %convolution_bitcast_fusion.2 = f32[512,512,1]{1,0,2:T(8,128)} fusion(f32[512]{0:T(512)S(1)} %bitcast.243, s32[512]{0:T(512)S(1)} %bitcast.255, f32[512]{0:T(512)S(1)} %bitcast.251, s32[512]{0:T(512)S(1)} %bitcast.247, f32[]{:T(128)} %bitcast.57, f32[]{:T(128)} %bitcast.56, f32[]{:T(128)} %bitcast.55, f32[]{:T(128)} %bitcast.54, f32[]{:T(128)} %bitcast.53, ...), kind=kOutput, calls=%fused_computation.26 | convolution fusion | flops 1628700672 | bytes 1056852 | tf_op jit(solution)/shard_map/dot_general | solution.py:52
  114.3 15.8 %convolution_bitcast_fusion = f32[512,512,1]{1,0,2:T(8,128)S(1)} fusion(f32[]{:T(128)} %bitcast.153, f32[]{:T(128)} %bitcast.152, f32[]{:T(128)} %bitcast.151, f32[]{:T(128)} %bitcast.150, f32[]{:T(128)} %bitcast.149, f32[]{:T(128)} %bitcast.148, f32[]{:T(128)} %bitcast.147, f32[]{:T(128)} %bitcast.146, f32[]{:T(128)} %bitcast.145, f32[]{:T(128)} %bitcast.144, ...), kind=kOutput, calls=%fused_computation.24 | convolution fusion | flops 1628700672 | bytes 1056852 | tf_op jit(solution)/shard_map/dot_general | solution.py:52
  132.6 1.2 fusion.104
  133.9 1.1 fusion.396
  135.0 11.6 %reduce-scatter.3.cloned.1.call-start = ((), (), s32[]{:S(2)}) async-start(), calls=%async_computation.6 | async-start | bytes 147456 | tf_op jit(solution)/shard_map/reduce_scatter | solution.py:174
  146.6 110.8 %all-to-all-done.1 = f32[32,8,16,512]{3,2,1,0:T(8,128)} async-done(((f32[32,8,16,512]{3,2,1,0:T(8,128)}), f32[32,8,16,512]{3,2,1,0:T(8,128)}, u32[]{:S(2)}, u32[]{:S(2)}) %all-to-all-start.1) | async-done | bytes 8388640 | tf_op jit(solution)/shard_map/all_to_all | solution.py:149
  257.4 24.4 %fusion.403 = f32[256,512,16]{1,2,0:T(8,128)S(1)} fusion(f32[256,16,512]{2,1,0:T(8,128)} %bitcast.11, f32[]{:T(128)} %bitcast.84, f32[]{:T(128)} %bitcast.83, f32[]{:T(128)} %bitcast.82, f32[]{:T(128)} %bitcast.81, f32[]{:T(128)} %bitcast.80, f32[]{:T(128)} %bitcast.79, f32[]{:T(128)} %bitcast.78, f32[]{:T(128)} %bitcast.77, f32[]{:T(128)} %bitcast.76, ...), kind=kOutput, calls=%fused_computation.383 | convolution fusion | flops 402669568 | bytes 16777300 | tf_op jit(solution)/shard_map/ia,naw->niw/dot_general | solution.py:59
  281.8 15.9 %fusion.2 = f32[256,16,512]{2,1,0:T(8,128)S(1)} fusion(f32[512,512,1]{1,0,2:T(8,128)S(1)} %convolution_bitcast_fusion.1, f32[256,512,16]{1,2,0:T(8,128)S(1)} %fusion.403), kind=kOutput, calls=%fused_computation.6 | convolution fusion | flops 12884901888 | bytes 17825792 | tf_op jit(solution)/shard_map/niw,wj->nij/dot_general | solution.py:60
  297.8 24.4 %fusion.405 = f32[256,512,16]{1,2,0:T(8,128)S(1)} fusion(f32[256,16,512]{2,1,0:T(8,128)} %bitcast.11, f32[]{:T(128)} %bitcast.34, f32[]{:T(128)} %bitcast.33, f32[]{:T(128)} %bitcast.32, f32[]{:T(128)} %bitcast.31, f32[]{:T(128)} %bitcast.30, f32[]{:T(128)} %bitcast.29, f32[]{:T(128)} %bitcast.28, f32[]{:T(128)} %bitcast.27, f32[]{:T(128)} %bitcast.26, ...), kind=kOutput, calls=%fused_computation.385 | convolution fusion | flops 402669568 | bytes 16777300 | tf_op jit(solution)/shard_map/ia,naw->niw/dot_general | solution.py:59
  322.2 15.7 %fusion.4 = f32[256,16,512]{2,1,0:T(8,128)S(1)} fusion(f32[512,512,1]{1,0,2:T(8,128)S(1)} %copy-done.2, f32[256,512,16]{1,2,0:T(8,128)S(1)} %fusion.405), kind=kOutput, calls=%fused_computation.8 | convolution fusion | flops 12884901888 | bytes 17825792 | tf_op jit(solution)/shard_map/niw,wj->nij/dot_general | solution.py:60
  337.9 24.4 %fusion.401 = f32[256,512,16]{1,2,0:T(8,128)S(1)} fusion(f32[256,16,512]{2,1,0:T(8,128)} %bitcast.11, f32[]{:T(128)} %bitcast.130, f32[]{:T(128)} %bitcast.129, f32[]{:T(128)} %bitcast.128, f32[]{:T(128)} %bitcast.127, f32[]{:T(128)} %bitcast.126, f32[]{:T(128)} %bitcast.125, f32[]{:T(128)} %bitcast.124, f32[]{:T(128)} %bitcast.123, f32[]{:T(128)} %bitcast.122, ...), kind=kOutput, calls=%fused_computation.381 | convolution fusion | flops 402669568 | bytes 16777300 | tf_op jit(solution)/shard_map/ia,naw->niw/dot_general | solution.py:59
  362.3 15.8 %fusion = f32[256,16,512]{2,1,0:T(8,128)} fusion(f32[512,512,1]{1,0,2:T(8,128)S(1)} %convolution_bitcast_fusion, f32[256,512,16]{1,2,0:T(8,128)S(1)} %fusion.401), kind=kOutput, calls=%fused_computation.4 | convolution fusion | flops 12884901888 | bytes 17825792 | tf_op jit(solution)/shard_map/niw,wj->nij/dot_general | solution.py:60
  378.1 15.4 %multiply_bitcast_fusion = f32[256,16,512]{2,1,0:T(8,128)} fusion(f32[256]{0:T(256)S(1)} %mul.1218, f32[256,16,512]{2,1,0:T(8,128)} %fusion, f32[256,16,512]{2,1,0:T(8,128)S(1)} %fusion.2, f32[256,16,512]{2,1,0:T(8,128)S(1)} %fusion.4, f32[]{:T(128)} %bitcast.109, f32[]{:T(128)} %bitcast.63, f32[]{:T(128)} %bitcast.7, f32[16]{0:T(128)} %bitcast.238, ...), kind=kOutput, calls=%fused_computation.12 | convolution fusion | flops 415237376 | bytes 33555724 | tf_op jit(solution)/shard_map/ia,naw->niw/dot_general | solution.py:79
  393.6 11.5 %fusion.19 = f32[64,512]{1,0:T(8,128)} fusion(f32[256,16,512]{2,1,0:T(8,128)} %multiply_bitcast_fusion, s32[256,16]{0,1:T(8,128)S(1)} %copy-done.6), kind=kOutput, calls=%fused_computation.27 | convolution fusion | flops 1610874880 | bytes 8536064 | tf_op jit(solution)/shard_map/lni,niw->lw/dot_general | solution.py:83
  405.1 30.5 %reduce-scatter.3.cloned.1.call-done = f32[8,512]{1,0:T(8,128)} async-done(((f32[64,512]{1,0:T(8,128)}), f32[8,512]{1,0:T(8,128)}) %reduce-scatter.3.cloned.1.call-update) | async-done | bytes 16400 | tf_op jit(solution)/shard_map/reduce_scatter | solution.py:174
  435.7 1.3 maximum_divide_fusion
  (79 shorter events, 13.1 us)
Async XLA Ops:
  6.5 69.6 %copy-start = (f32[8,2,21]{2,1,0:T(2,128)S(1)}, f32[8,2,21]{2,1,0:T(2,128)}, u32[]{:S(2)}) copy-start(f32[8,2,21]{2,1,0:T(2,128)} %param.17) | copy-start | bytes 4036
  13.5 20.2 %all-to-all-start.2 = ((f32[32,1,8]{2,1,0:T(1,128)}), f32[32,1,8]{2,1,0:T(1,128)S(1)}, u32[]{:S(2)}, u32[]{:S(2)}) async-start(f32[32,1,8]{2,1,0:T(1,128)} %bitcast.161), calls=%async_computation.2 | async-start | bytes 32768 | tf_op jit(solution)/shard_map/all_to_all | solution.py:151
  33.8 13.4 %copy-start.7 = (f32[32,1,8]{2,1,0:T(1,128)}, f32[32,1,8]{2,1,0:T(1,128)S(1)}, u32[]{:S(2)}) copy-start(f32[32,1,8]{2,1,0:T(1,128)S(1)} %all-to-all-done.2) | copy-start | bytes 3076
  33.8 13.3 %all-to-all-start = ((f32[32,1,8]{2,1,0:T(1,128)}), f32[32,1,8]{2,1,0:T(1,128)S(1)}, u32[]{:S(2)}, u32[]{:S(2)}) async-start(f32[32,1,8]{2,1,0:T(1,128)} %bitcast.6), calls=%async_computation | async-start | bytes 32768 | tf_op jit(solution)/shard_map/all_to_all | solution.py:152
  47.1 0.6 copy-start.9
  47.7 19.8 %all-to-all-start.3 = ((f32[32,8,512]{2,1,0:T(8,128)}), f32[32,8,512]{2,1,0:T(8,128)S(1)}, u32[]{:S(2)}, u32[]{:S(2)}) async-start(f32[32,8,512]{2,1,0:T(8,128)} %fusion.233), calls=%async_computation.4 | async-start | bytes 1048576 | tf_op jit(solution)/shard_map/all_to_all | solution.py:150
  64.9 10.6 %copy-start.11 = (f32[1,3]{1,0:T(1,128)S(1)}, f32[1,3]{1,0:T(1,128)}, u32[]{:S(2)}) copy-start(f32[1,3]{1,0:T(1,128)} %param.19) | copy-start | bytes 40
  64.9 11.2 %copy-start.18 = (s32[1,3]{1,0:T(1,128)S(1)}, s32[1,3]{1,0:T(1,128)}, u32[]{:S(2)}) copy-start(s32[1,3]{1,0:T(1,128)} %param.18) | copy-start | bytes 40
  64.9 16.5 %copy-start.13 = (s32[1,16]{1,0:T(1,128)S(1)}, s32[1,16]{1,0:T(1,128)}, u32[]{:S(2)}) copy-start(s32[1,16]{1,0:T(1,128)} %param.20) | copy-start | bytes 196
  64.9 16.5 %copy-start.12 = (f32[1,16]{1,0:T(1,128)S(1)}, f32[1,16]{1,0:T(1,128)}, u32[]{:S(2)}) copy-start(f32[1,16]{1,0:T(1,128)} %param.21) | copy-start | bytes 196
  64.9 16.7 %copy-start.16 = (f32[1,512]{1,0:T(1,128)S(1)}, f32[1,512]{1,0:T(1,128)}, u32[]{:S(2)}) copy-start(f32[1,512]{1,0:T(1,128)} %param.23) | copy-start | bytes 6148
  64.9 16.7 %copy-start.17 = (s32[1,512]{1,0:T(1,128)S(1)}, s32[1,512]{1,0:T(1,128)}, u32[]{:S(2)}) copy-start(s32[1,512]{1,0:T(1,128)} %param.22) | copy-start | bytes 6148
  67.5 8.7 %copy-start.3 = (f32[32,8,512]{2,1,0:T(8,128)}, f32[32,8,512]{2,1,0:T(8,128)S(1)}, u32[]{:S(2)}) copy-start(f32[32,8,512]{2,1,0:T(8,128)S(1)} %all-to-all-done.3) | copy-start | bytes 1572868
  67.5 190.0 %all-to-all-start.1 = ((f32[32,8,16,512]{3,2,1,0:T(8,128)}), f32[32,8,16,512]{3,2,1,0:T(8,128)}, u32[]{:S(2)}, u32[]{:S(2)}) async-start(f32[32,8,16,512]{3,2,1,0:T(8,128)} %select_multiply_fusion), calls=%async_computation.1 | async-start | bytes 16777216 | tf_op jit(solution)/shard_map/all_to_all | solution.py:149
  75.1 330.1 %reduce-scatter.5.cloned.1.call-start = ((), (), s32[]{:S(2)}) async-start(), calls=%async_computation.7 | async-start | bytes 147456 | tf_op jit(solution)/shard_map/reduce_scatter | solution.py:175
  81.4 16.1 %copy-start.14 = (s32[16]{0:T(128)}, s32[16]{0:T(128)S(1)}, u32[]{:S(2)}) copy-start(s32[16]{0:T(128)S(1)} %add_bitcast_fusion) | copy-start | bytes 196
  81.4 16.1 %copy-start.15 = (f32[16]{0:T(128)}, f32[16]{0:T(128)S(1)}, u32[]{:S(2)}) copy-start(f32[16]{0:T(128)S(1)} %subtract_bitcast_fusion) | copy-start | bytes 196
  114.3 16.3 %copy-start.8 = (f32[32,1,8]{2,1,0:T(1,128)S(1)}, f32[32,1,8]{2,1,0:T(1,128)}, u32[]{:S(2)}) copy-start(f32[32,1,8]{2,1,0:T(1,128)} %copy-done.7) | copy-start | bytes 3076
  114.3 17.0 %copy-start.10 = (f32[32,1,8]{2,1,0:T(1,128)S(1)}, f32[32,1,8]{2,1,0:T(1,128)}, u32[]{:S(2)}) copy-start(f32[32,1,8]{2,1,0:T(1,128)} %copy-done.9) | copy-start | bytes 3076
  114.3 18.4 %copy-start.4 = (f32[32,8,512]{2,1,0:T(8,128)S(1)}, f32[32,8,512]{2,1,0:T(8,128)}, u32[]{:S(2)}) copy-start(f32[32,8,512]{2,1,0:T(8,128)} %copy-done.3) | copy-start | bytes 1572868
  131.4 0.6 copy-start.5
  135.0 300.7 %reduce-scatter.3.cloned.1.call-start = ((), (), s32[]{:S(2)}) async-start(), calls=%async_computation.6 | async-start | bytes 147456 | tf_op jit(solution)/shard_map/reduce_scatter | solution.py:174
  297.7 24.4 %copy-start.2 = (f32[512,512,1]{1,0,2:T(8,128)S(1)}, f32[512,512,1]{1,0,2:T(8,128)}, u32[]{:S(2)}) copy-start(f32[512,512,1]{1,0,2:T(8,128)} %convolution_bitcast_fusion.2) | copy-start | bytes 3145732
  378.1 15.5 %copy-start.6 = (s32[256,16]{0,1:T(8,128)S(1)}, s32[256,16]{0,1:T(8,128)}, u32[]{:S(2)}) copy-start(s32[256,16]{0,1:T(8,128)} %copy-done.5) | copy-start | bytes 49156
  378.1 58.9 %copy-start.1 = (f32[8,2,21]{2,1,0:T(2,128)S(1)}, f32[8,2,21]{2,1,0:T(2,128)}, u32[]{:S(2)}) copy-start(f32[8,2,21]{2,1,0:T(2,128)} %param.17) | copy-start | bytes 4036
Sparse Core Ops, SparseCore 0:
  135.1 34.6 reduce-scatter.4
  405.2 30.3 reduce-scatter.2
where the time goes:
time: 450 us; the launch traced here: 444 us
  matrix products  199 us (44%)
  waiting for transfers between devices  158 us (35%)
  starting transfers between devices  41 us (9%)
  local copies, waits for them, and re-layouts  17.1 us (4%)
  other arithmetic  15.2 us (3%)
  between operations  14 us (3%)
    all_to_all x1, waiting for transfers between devices, per_device(): lax.all_to_all(slot_image, 'sky', split_axis=0, concat_axis=0, tiled=True)  111 us
    dot_general x3, matrix products, match_psf(): jnp.einsum('ia,naw->niw', row_mats[basis_term], images, precision=highest)  73.2 us
    dot_general x3, matrix products, exposure_tables(): col_list.append(jnp.dot(banded, column_warp, precision=highest))  48.4 us
    dot_general x3, matrix products, match_psf(): jnp.einsum('niw,wj->nij', row_pass, col_mats[basis_term], precision=highest)  47.4 us
    reduce_scatter x1, waiting for transfers between devices, per_device(): lax.psum_scatter(numer, 'grp', scatter_dimension=0, tiled=True)  30.5 us
    dot_general x1, matrix products, place(): jnp.einsum('ia,naw->niw', row_warp, matched, precision=highest)  15.4 us
    all_to_all x1, starting transfers between devices, per_device(): lax.all_to_all(slot_weight, 'sky', split_axis=0, concat_axis=0, tiled=True)  11.7 us
    reduce_scatter x1, starting transfers between devices, per_device(): lax.psum_scatter(numer, 'grp', scatter_dimension=0, tiled=True)  11.6 us
  transfers between devices with their start and end apart: 6, of which 5 were waited for; matrix products, arithmetic and copies ran while one was open for 50% of the time, Pallas kernels for 0%

commit v1 on v0

v1 whole, which is shorter than its diff:
```python
import functools

import jax
import jax.numpy as jnp
from jax import lax
from jax.experimental import pallas as pl
from jax.experimental.pallas import tpu as pltpu
from jax.sharding import PartitionSpec as P

F32 = jnp.float32
BF16 = jnp.bfloat16
NX, NY, NZ = 4, 4, 8
SEGS = 64
ROWS = 16
WIDTH = 512
TAPS = 21
REACH = 10
NBASIS = 3
LANES = 128
BLOCKS = WIDTH // LANES
BLOCK_SEGS = 16
BLOCK_ROWS = BLOCK_SEGS * ROWS


def split(value):
    high = value.astype(BF16)
    return high, (value - high.astype(F32)).astype(BF16)


def column_factor(bits):
    bad = (bits & 1).astype(F32)
    full = ((bits >> 1) & 1).astype(F32)
    cosmic = ((bits >> 2) & 1).astype(F32)
    return (1.0 - bad) * (1.0 - 0.75 * full) * (1.0 - 0.5 * cosmic)


def column_warp(base_ref, frac_ref):
    source = lax.broadcasted_iota(jnp.int32, (WIDTH, WIDTH), 0)
    base = base_ref[...]
    frac = frac_ref[...]
    return jnp.where(source == base, 1.0 - frac, 0.0) + jnp.where(source == base + 1, frac, 0.0)


def column_of(ref, shape):
    row = lax.broadcasted_iota(jnp.int32, shape, 0)
    result = jnp.full(shape, ref[0, 0])
    for i in range(1, ROWS):
        result = jnp.where(row == i, ref[0, i], result)
    return result


def relative_patch(place_ref, owner):
    ry = (owner % NY - place_ref[2] + NY) % NY
    rz = (owner // NY - place_ref[3] + NZ) % NZ
    return ry, rz


def write_out(place_ref, sums, outs, sems):
    keep_x, send_x, keep_y, send_y = outs
    copies = []
    for rc, (to_x, to_y) in enumerate(((keep_x, keep_y), (send_x, send_y))):
        core = (place_ref[0] + rc) % 2
        for rx in range(NX):
            tile = ((place_ref[1] + rx) % NX) * 2 + core
            rows = pl.ds(pl.multiple_of(tile * 8, 8), 8)
            for block in range(2):
                copies.append((sums.at[block, :, :, rows, :], to_x.at[rx, block]))
                copies.append((sums.at[2 + block, :, :, rows, :], to_y.at[:, rx, block]))
    started = [pltpu.make_async_copy(src, dst, sems.at[i]) for i, (src, dst) in enumerate(copies)]
    for copy in started:
        copy.start()
    for copy in started:
        copy.wait()


def denom_kernel(
    place_ref, owner_ref, offset_ref, weight_ref, frac_ref, bits_ref, col_base_ref, col_frac_ref,
    keep_x, send_x, keep_y, send_y, sums, cover, sems,
):
    factor = column_factor(bits_ref[0]).astype(BF16)
    warp_high, warp_low = split(column_warp(col_base_ref, col_frac_ref))
    coverage = jnp.dot(factor, warp_high, preferred_element_type=F32) + jnp.dot(
        factor, warp_low, preferred_element_type=F32
    )
    for block in range(BLOCKS):
        cover[block] = coverage[:, block * LANES : (block + 1) * LANES]
    frac = column_of(frac_ref, (ROWS, LANES))
    spread = (1.0 - frac) + frac
    sums[...] = jnp.zeros(sums.shape, F32)

    def one(s, carry):
        ry, rz = relative_patch(place_ref, owner_ref[0, s])
        rows = pl.ds(offset_ref[0, s], ROWS)
        share = spread * weight_ref[0, s]
        for block in range(BLOCKS):
            sums[block, ry, rz, rows, :] += share * cover[block, pl.ds(s, 1), :]
        return carry

    lax.fori_loop(0, SEGS, one, 0, unroll=2)
    write_out(place_ref, sums, (keep_x, send_x, keep_y, send_y), sems)


def row_tables(bank_ref, index_ref, coeff_ref, base_ref, frac_ref, k):
    shape = (ROWS, BLOCK_ROWS)
    delta = lax.broadcasted_iota(jnp.int32, shape, 1) % ROWS - column_of(base_ref, shape) + REACH
    frac = column_of(frac_ref, shape)
    term = index_ref[0, k]
    lower = jnp.zeros(shape, F32)
    higher = jnp.zeros(shape, F32)
    for tap in range(TAPS):
        value = bank_ref[term, 0, tap]
        lower = jnp.where(delta == tap, value, lower)
        higher = jnp.where(delta == tap + 1, value, higher)
    return ((1.0 - frac) * lower + frac * higher) * coeff_ref[0, k]


def band_tables(bank_ref, index_ref, k):
    lane = lax.broadcasted_iota(jnp.int32, (LANES, WIDTH), 1)
    term = index_ref[0, k]
    base = jnp.zeros((LANES, WIDTH), F32)
    for tap in range(TAPS):
        base = jnp.where(lane == LANES + REACH - tap, bank_ref[term, 1, tap], base)
    return pltpu.roll(base, 0, 1, stride=1, stride_axis=0)[:, : 3 * LANES]


def rows_kernel(
    bank_ref, index_ref, coeff_ref, base_ref, frac_ref, bits_ref, pixels_ref, u_high, u_low, blockdiag
):
    same = (
        lax.broadcasted_iota(jnp.int32, (BLOCK_ROWS, BLOCK_ROWS), 0) // ROWS
        == lax.broadcasted_iota(jnp.int32, (BLOCK_ROWS, BLOCK_ROWS), 1) // ROWS
    )
    for k in range(NBASIS):
        table = row_tables(bank_ref, index_ref, coeff_ref, base_ref, frac_ref, k)
        whole = jnp.where(same, jnp.concatenate([table] * BLOCK_SEGS, axis=0), 0.0)
        high, low = split(whole)
        rows = slice(k * BLOCK_ROWS, (k + 1) * BLOCK_ROWS)
        blockdiag[rows, 0:BLOCK_ROWS] = high
        blockdiag[rows, BLOCK_ROWS : 2 * BLOCK_ROWS] = high
        blockdiag[rows, 2 * BLOCK_ROWS :] = low

    def one(b, carry):
        segs = pl.ds(b * BLOCK_SEGS, BLOCK_SEGS)
        factor = column_factor(bits_ref[0, segs, :])
        masked = (pixels_ref[0, segs] * factor[:, None, :]).reshape(BLOCK_ROWS, WIDTH)
        high, low = split(masked)
        product = jnp.dot(
            blockdiag[...], jnp.concatenate([high, low, high], axis=0), preferred_element_type=F32
        )
        rows = pl.ds(pl.multiple_of(b * BLOCK_ROWS, BLOCK_ROWS), BLOCK_ROWS)
        for k in range(NBASIS):
            part_high, part_low = split(product[k * BLOCK_ROWS : (k + 1) * BLOCK_ROWS])
            u_high[rows, k * WIDTH : (k + 1) * WIDTH] = part_high
            u_low[rows, k * WIDTH : (k + 1) * WIDTH] = part_low
        return carry

    lax.fori_loop(0, SEGS // BLOCK_SEGS, one, 0)


def numer_kernel(
    place_ref, owner_ref, offset_ref, weight_ref, bank_ref, index_ref, col_base_ref, col_frac_ref, u_high, u_low,
    keep_x, send_x, keep_y, send_y, sums, lifted, band_high, band_low, warp_high, warp_low, sems,
):
    band_high[...] = jnp.zeros(band_high.shape, BF16)
    band_low[...] = jnp.zeros(band_low.shape, BF16)
    for k in range(NBASIS):
        high, low = split(band_tables(bank_ref, index_ref, k))
        for block in range(BLOCKS):
            first = max(block - 1, 0)
            last = min(block + 1, BLOCKS - 1)
            rows = slice(k * WIDTH + block * LANES, k * WIDTH + (block + 1) * LANES)
            to = slice(first * LANES, (last + 1) * LANES)
            of = slice((first - block + 1) * LANES, (last - block + 2) * LANES)
            band_high[rows, to] = high[:, of]
            band_low[rows, to] = low[:, of]
    high, low = split(column_warp(col_base_ref, col_frac_ref))
    warp_high[...] = high
    warp_low[...] = low
    sums[...] = jnp.zeros(sums.shape, F32)
    dot = functools.partial(jnp.dot, preferred_element_type=F32)

    def one(b, carry):
        rows = pl.ds(pl.multiple_of(b * BLOCK_ROWS, BLOCK_ROWS), BLOCK_ROWS)
        part_high = u_high[rows, :]
        part_low = u_low[rows, :]
        wide = dot(part_high, band_high[...]) + dot(part_high, band_low[...]) + dot(part_low, band_high[...])
        high, low = split(wide)
        warped = dot(high, warp_high[...]) + dot(high, warp_low[...]) + dot(low, warp_high[...])
        for block in range(BLOCKS):
            lifted[block, rows, :] = warped[:, block * LANES : (block + 1) * LANES]
        return carry

    lax.fori_loop(0, SEGS * ROWS // BLOCK_ROWS, one, 0)

    def place(s, carry):
        ry, rz = relative_patch(place_ref, owner_ref[0, s])
        rows = pl.ds(offset_ref[0, s], ROWS)
        weight = weight_ref[0, s]
        of = pl.ds(pl.multiple_of(s * ROWS, ROWS), ROWS)
        for block in range(BLOCKS):
            sums[block, ry, rz, rows, :] += weight * lifted[block, of, :]
        return carry

    lax.fori_loop(0, SEGS, place, 0, unroll=2)
    write_out(place_ref, sums, (keep_x, send_x, keep_y, send_y), sems)


SMEM = pl.BlockSpec(memory_space=pltpu.SMEM)
VMEM = pl.BlockSpec(memory_space=pltpu.VMEM)
ANY = pl.BlockSpec(memory_space=pl.ANY)
PARTS_X = jax.ShapeDtypeStruct((NX, 2, NY, NZ, 8, LANES), F32)
PARTS_Y = jax.ShapeDtypeStruct((NY, NX, 2, NZ, 8, LANES), F32)
PARAMS = pltpu.CompilerParams(vmem_limit_bytes=40 * 1024 * 1024)
SUMS = pltpu.VMEM((BLOCKS, NY, NZ, 64, LANES), F32)


def denom_sums(place, owner, offset, weight, row_frac, bits, col_base, col_frac):
    return pl.pallas_call(
        denom_kernel,
        out_shape=(PARTS_X, PARTS_X, PARTS_Y, PARTS_Y),
        in_specs=[SMEM] * 5 + [VMEM] * 3,
        out_specs=(ANY,) * 4,
        scratch_shapes=[SUMS, pltpu.VMEM((BLOCKS, SEGS, LANES), F32), pltpu.SemaphoreType.DMA((32,))],
        compiler_params=PARAMS,
        cost_estimate=pl.CostEstimate(flops=10**8, bytes_accessed=4 * 10**6, transcendentals=0),
        name="denom_sums",
    )(place, owner, offset, weight, row_frac, bits, col_base, col_frac)


def row_pass(bank, index, coeff, row_base, row_frac, bits, pixels):
    wide = jax.ShapeDtypeStruct((SEGS * ROWS, NBASIS * WIDTH), BF16)
    return pl.pallas_call(
        rows_kernel,
        out_shape=(wide, wide),
        in_specs=[SMEM] * 5 + [VMEM] * 2,
        out_specs=(VMEM, VMEM),
        scratch_shapes=[pltpu.VMEM((NBASIS * BLOCK_ROWS, 3 * BLOCK_ROWS), BF16)],
        compiler_params=PARAMS,
        cost_estimate=pl.CostEstimate(flops=5 * 10**9, bytes_accessed=8 * 10**6, transcendentals=0),
        name="row_pass",
    )(bank, index, coeff, row_base, row_frac, bits, pixels)


def numer_sums(place, owner, offset, weight, bank, index, col_base, col_frac, u_high, u_low):
    band = pltpu.VMEM((NBASIS * WIDTH, WIDTH), BF16)
    warp = pltpu.VMEM((WIDTH, WIDTH), BF16)
    return pl.pallas_call(
        numer_kernel,
        out_shape=(PARTS_X, PARTS_X, PARTS_Y, PARTS_Y),
        in_specs=[SMEM] * 6 + [VMEM] * 4,
        out_specs=(ANY,) * 4,
        scratch_shapes=[
            SUMS, pltpu.VMEM((BLOCKS, SEGS * ROWS, LANES), F32), band, band, warp, warp,
            pltpu.SemaphoreType.DMA((32,)),
        ],
        compiler_params=PARAMS,
        cost_estimate=pl.CostEstimate(flops=10**10, bytes_accessed=10**7, transcendentals=0),
        name="numer_sums",
    )(place, owner, offset, weight, bank, index, col_base, col_frac, u_high, u_low)


def shift_core(value):
    return lax.ppermute(value, "grp", [(i, i ^ 1) for i in range(2 * NX)])


def shift_x(value, d):
    return lax.ppermute(value, "grp", [(i, (i // 2 + d) % NX * 2 + i % 2) for i in range(2 * NX)])


def shift_y(value, d):
    return lax.ppermute(value, "sky", [(i, i // NY * NY + (i + d) % NY) for i in range(NY * NZ)])


def shift_z(value, d):
    return lax.ppermute(value, "sky", [(i, (i // NY + d) % NZ * NY + i % NY) for i in range(NY * NZ)])


def exchange(parts, shift):
    return [parts[0]] + [shift(parts[d], d) for d in range(1, len(parts))]


def total(terms, take):
    result = take(terms[0])
    for term in terms[1:]:
        result = result + take(term)
    return result


def travel(keep_x, send_x, keep_y, send_y):
    own_x = [keep_x, shift_core(send_x)]
    own_y = [keep_y, shift_core(send_y)]
    by_x = exchange([total(own_x, lambda t: t[d]) for d in range(NX)], shift_x)
    by_y = exchange([total(own_y, lambda t: t[d]) for d in range(NY)], shift_y)
    by_xy = exchange([total(by_x, lambda t: t[:, d]) for d in range(NY)], shift_y)
    by_yx = exchange([total(by_y, lambda t: t[d]) for d in range(NX)], shift_x)
    last = exchange(
        [
            jnp.concatenate([total(by_xy, lambda t: t[:, d]), total(by_yx, lambda t: t[:, d])])
            for d in range(NZ)
        ],
        shift_z,
    )
    return total(last, lambda t: t)


def per_device(
    pixels, mask_bits, owner, row_offset, seg_weight, psf_bank, basis_index, basis_coeff,
    row_base, row_frac, col_base, col_frac,
):
    sky = lax.axis_index("sky").astype(jnp.int32)
    grp = lax.axis_index("grp").astype(jnp.int32)
    place = jnp.stack([grp % 2, grp // 2, sky % NY, sky // NY])
    denom_parts = denom_sums(place, owner, row_offset, seg_weight, row_frac, mask_bits, col_base, col_frac)
    u_high, u_low = row_pass(psf_bank, basis_index, basis_coeff, row_base, row_frac, mask_bits, pixels)
    numer_parts = numer_sums(
        place, owner, row_offset, seg_weight, psf_bank, basis_index, col_base, col_frac, u_high, u_low
    )
    denom = travel(*denom_parts)
    numer = travel(*numer_parts)
    coadd = numer / jnp.maximum(denom, 1.0)
    return jnp.swapaxes(coadd, 0, 1).reshape(8, WIDTH)


def solution(mesh):
    placed = (
        P("grp", "sky", None, None),
        P("grp", "sky", None),
        P("grp", "sky"),
        P("grp", "sky"),
        P("grp", "sky"),
        P(),
        P("grp", None),
        P("grp", None),
        P("grp", None),
        P("grp", None),
        P("grp", None),
        P("grp", None),
    )
    return jax.shard_map(
        per_device, mesh=mesh, in_specs=placed, out_specs=P(("sky", "grp"), None), check_vma=False
    )
```

time: 450 us -> 112 us (0.25)
  the two profiles are of different devices: /device:TPU:8 before, /device:TPU:6 now
where the time goes in v1:
time: 112 us; the launch traced here: 110 us
  starting transfers between devices  64.4 us (58%)
  Pallas kernels  19 us (17%)
  waiting for transfers between devices  18.4 us (16%)
  local copies, waits for them, and re-layouts  6.14 us (5%)
  other arithmetic  1.78 us (2%)
    ppermute x14, starting transfers between devices, shift_z(): lax.ppermute(value, 'sky', [(i, (i // NY + d) % NZ * NY + i % NY) for i i...  31.9 us
    ppermute x12, starting transfers between devices, shift_x(): lax.ppermute(value, 'grp', [(i, (i // 2 + d) % NX * 2 + i % 2) for i in r...  16.9 us
    ppermute x12, starting transfers between devices, shift_y(): lax.ppermute(value, 'sky', [(i, i // NY * NY + (i + d) % NY) for i in ran...  14.4 us
    pallas_call x1, Pallas kernels, numer_sums(): pl.pallas_call(numer_kernel, out_shape=(PARTS_X, PARTS_X, PARTS_Y, PARTS_...  11.4 us
    ppermute x12, waiting for transfers between devices, shift_x(): lax.ppermute(value, 'grp', [(i, (i // 2 + d) % NX * 2 + i % 2) for i in r...  11 us
    unnamed x30, local copies, waits for them, and re-layouts  5.88 us
    ppermute x12, waiting for transfers between devices, shift_y(): lax.ppermute(value, 'sky', [(i, i // NY * NY + (i + d) % NY) for i in ran...  5.17 us
    pallas_call x1, Pallas kernels, row_pass(): pl.pallas_call(rows_kernel, out_shape=(wide, wide), in_specs=[SMEM] * 5 +...  4.26 us
  transfers between devices with their start and end apart: 42, of which 8 were waited for; matrix products, arithmetic and copies ran while one was open for 1% of the time, Pallas kernels for 3%

profile of v1, /device:TPU:6, one launch (start us, length us, event | category | flops | bytes accessed | tf_op | source)
XLA Modules:
  0.0 110.3 jit_solution(16165560703806755662)
XLA Ops:
  0.1 1.6 %copy-done = f32[1,64,16,512]{3,2,1,0:T(8,128)S(1)} copy-done((f32[1,64,16,512]{3,2,1,0:T(8,128)S(1)}, f32[1,64,16,512]{3,2,1,0:T(8,128)}, u32[]{:S(2)}) %copy-start) | copy-done | bytes 2097176
  5.9 4.3 %row_pass.1 = (bf16[1024,1536]{1,0:T(8,128)(2,1)S(1)}, bf16[1024,1536]{1,0:T(8,128)(2,1)S(1)}) custom-call(f32[8,2,21]{2,1,0:T(2,128)S(1)} %copy-done.3, s32[1,3]{1,0:T(1,128)S(1)} %copy-done.9, f32[1,3]{1,0:T(1,128)S(1)} %copy-done.7, s32[1,16]{1,0:T(1,128)S(1)} %copy-done.8, f32[1,16]{1,0:T(1,128)S(1)} %copy-done.14, s32[1,64,512]{2,1,0:T(8,128)S(1)} %copy-done.1, ...), custom_call_target="tpu_custom_call" | custom-call | flops 5000000000 | bytes 8000000 | tf_op jit(solution)/shard_map/row_pass/pallas_call | solution.py:232
  10.3 11.4 %numer_sums.1 = (f32[4,2,4,8,8,128]{5,4,3,2,1,0:T(8,128)S(1)}, f32[4,2,4,8,8,128]{5,4,3,2,1,0:T(8,128)S(1)}, f32[4,4,2,8,8,128]{5,4,3,2,1,0:T(8,128)S(1)}, f32[4,4,2,8,8,128]{5,4,3,2,1,0:T(8,128)S(1)}) custom-call(s32[4]{0:T(128)S(1)} %pad_add_fusion.place_ref, s32[1,64]{1,0:T(1,128)S(1)} %copy-done.11, s32[1,64]{1,0:T(1,128)S(1)} %copy-done.12, ...), custom_call_target="tpu_custom_call" | custom-call | flops 10000000000 | bytes 10000000 | tf_op jit(solution)/shard_map/numer_sums/pallas_call | solution.py:247
  22.6 3.3 %denom_sums.1 = (f32[4,2,4,8,8,128]{5,4,3,2,1,0:T(8,128)S(1)}, f32[4,2,4,8,8,128]{5,4,3,2,1,0:T(8,128)S(1)}, f32[4,4,2,8,8,128]{5,4,3,2,1,0:T(8,128)S(1)}, f32[4,4,2,8,8,128]{5,4,3,2,1,0:T(8,128)S(1)}) custom-call(s32[4]{0:T(128)S(1)} %pad_add_fusion.place_ref, s32[1,64]{1,0:T(1,128)S(1)} %copy-done.11, s32[1,64]{1,0:T(1,128)S(1)} %copy-done.12, ...), custom_call_target="tpu_custom_call" | custom-call | flops 100000000 | bytes 4000000 | tf_op jit(solution)/shard_map/denom_sums/pallas_call | solution.py:218
  26.8 2.3 %collective-permute-start.1 = (f32[2,4,8,8,128]{4,3,0,2,1:T(8,128)S(1)}, f32[2,4,8,8,128]{4,3,0,2,1:T(8,128)S(1)}, u32[]{:S(2)}, u32[]{:S(2)}) collective-permute-start(f32[2,4,8,8,128]{4,3,0,2,1:T(8,128)S(1)} %get-tuple-element.28), channel_id=1, source_target_pairs={{0,2},{1,3},{2,4},{3,5},{4,6},{5,7},{6,0},{7,1},{8,10},{9,11},{10,... | collective-permute-start | bytes 786440 | tf_op jit(solution)/shard_map/ppermute | solution.py:267
  30.1 2.8 %collective-permute-start.10 = (f32[4,2,8,8,128]{4,3,1,2,0:T(8,128)S(1)}, f32[4,2,8,8,128]{4,3,1,2,0:T(8,128)S(1)}, u32[]{:S(2)}, u32[]{:S(2)}) collective-permute-start(f32[4,2,8,8,128]{4,3,1,2,0:T(8,128)S(1)} %get-tuple-element.30), channel_id=1, source_target_pairs={{0,24},{8,0},{16,8},{24,16},{32,56},{40,32},{48,40},{56,48},{64,88... | collective-permute-start | bytes 786440 | tf_op jit(solution)/shard_map/ppermute | solution.py:271
  33.5 7.0 %collective-permute-done.1 = f32[2,4,8,8,128]{4,3,0,2,1:T(8,128)S(1)} collective-permute-done((f32[2,4,8,8,128]{4,3,0,2,1:T(8,128)S(1)}, f32[2,4,8,8,128]{4,3,0,2,1:T(8,128)S(1)}, u32[]{:S(2)}, u32[]{:S(2)}) %collective-permute-start.1) | collective-permute-done | bytes 262176 | tf_op jit(solution)/shard_map/ppermute | solution.py:267
  40.6 3.7 %collective-permute-start.22 = (f32[2,4,8,8,128]{4,3,0,2,1:T(8,128)S(1)}, f32[2,4,8,8,128]{4,3,0,2,1:T(8,128)S(1)}, u32[]{:S(2)}, u32[]{:S(2)}) collective-permute-start(f32[2,4,8,8,128]{4,3,0,2,1:T(8,128)S(1)} %get-tuple-element.36), channel_id=1, source_target_pairs={{0,2},{1,3},{2,4},{3,5},{4,6},{5,7},{6,0},{7,1},{8,10},{9,11},{10,... | collective-permute-start | bytes 786440 | tf_op jit(solution)/shard_map/ppermute | solution.py:267
  44.4 2.1 %collective-permute-start.31 = (f32[4,2,8,8,128]{4,3,2,1,0:T(8,128)S(1)}, f32[4,2,8,8,128]{4,3,2,1,0:T(8,128)S(1)}, u32[]{:S(2)}, u32[]{:S(2)}) collective-permute-start(f32[4,2,8,8,128]{4,3,2,1,0:T(8,128)S(1)} %get-tuple-element.54), channel_id=1, source_target_pairs={{0,24},{8,0},{16,8},{24,16},{32,56},{40,32},{48,40},{56,48},{64,88... | collective-permute-start | bytes 786440 | tf_op jit(solution)/shard_map/ppermute | solution.py:271
  48.7 3.8 %collective-permute-done.31 = f32[4,2,8,8,128]{4,3,2,1,0:T(8,128)S(1)} collective-permute-done((f32[4,2,8,8,128]{4,3,2,1,0:T(8,128)S(1)}, f32[4,2,8,8,128]{4,3,2,1,0:T(8,128)S(1)}, u32[]{:S(2)}, u32[]{:S(2)}) %collective-permute-start.31) | collective-permute-done | bytes 262176 | tf_op jit(solution)/shard_map/ppermute | solution.py:271
  52.4 1.9 %collective-permute-start.30 = (f32[4,2,8,8,128]{4,3,1,2,0:T(8,128)S(1)}, f32[4,2,8,8,128]{4,3,1,2,0:T(8,128)S(1)}, u32[]{:S(2)}, u32[]{:S(2)}) collective-permute-start(f32[4,2,8,8,128]{4,3,1,2,0:T(8,128)S(1)} %get-tuple-element.50), channel_id=1, source_target_pairs={{0,16},{8,24},{16,0},{24,8},{32,48},{40,56},{48,32},{56,40},{64,80... | collective-permute-start | bytes 786440 | tf_op jit(solution)/shard_map/ppermute | solution.py:271
  54.3 1.6 %collective-permute-start.4 = (f32[2,8,8,128]{3,2,0,1:T(8,128)S(1)}, f32[2,8,8,128]{3,2,0,1:T(8,128)S(1)}, u32[]{:S(2)}, u32[]{:S(2)}) collective-permute-start(f32[2,8,8,128]{3,2,0,1:T(8,128)S(1)} %get-tuple-element.40), channel_id=1, source_target_pairs={{0,8},{8,16},{16,24},{24,0},{32,40},{40,48},{48,56},{56,32},{64,72... | collective-permute-start | bytes 196616 | tf_op jit(solution)/shard_map/ppermute | solution.py:271
  55.9 1.5 %collective-permute-done.23 = f32[2,4,8,8,128]{4,3,0,2,1:T(8,128)S(1)} collective-permute-done((f32[2,4,8,8,128]{4,3,0,2,1:T(8,128)S(1)}, f32[2,4,8,8,128]{4,3,0,2,1:T(8,128)S(1)}, u32[]{:S(2)}, u32[]{:S(2)}) %collective-permute-start.23) | collective-permute-done | bytes 262176 | tf_op jit(solution)/shard_map/ppermute | solution.py:267
  57.4 1.2 %collective-permute-start.5 = (f32[2,8,8,128]{3,2,0,1:T(8,128)S(1)}, f32[2,8,8,128]{3,2,0,1:T(8,128)S(1)}, u32[]{:S(2)}, u32[]{:S(2)}) collective-permute-start(f32[2,8,8,128]{3,2,0,1:T(8,128)S(1)} %get-tuple-element.39), channel_id=1, source_target_pairs={{0,16},{8,24},{16,0},{24,8},{32,48},{40,56},{48,32},{56,40},{64,80... | collective-permute-start | bytes 196616 | tf_op jit(solution)/shard_map/ppermute | solution.py:271
  58.6 2.1 %collective-permute-done.24 = f32[2,4,8,8,128]{4,3,0,2,1:T(8,128)S(1)} collective-permute-done((f32[2,4,8,8,128]{4,3,0,2,1:T(8,128)S(1)}, f32[2,4,8,8,128]{4,3,0,2,1:T(8,128)S(1)}, u32[]{:S(2)}, u32[]{:S(2)}) %collective-permute-start.24) | collective-permute-done | bytes 262176 | tf_op jit(solution)/shard_map/ppermute | solution.py:267
  61.6 2.2 %collective-permute-start.11 = (f32[2,8,8,128]{3,2,0,1:T(8,128)S(1)}, f32[2,8,8,128]{3,2,0,1:T(8,128)S(1)}, u32[]{:S(2)}, u32[]{:S(2)}) collective-permute-start(f32[2,8,8,128]{3,2,0,1:T(8,128)S(1)} %get-tuple-element.44), channel_id=1, source_target_pairs={{0,2},{1,3},{2,4},{3,5},{4,6},{5,7},{6,0},{7,1},{8,10},{9,11},{10,... | collective-permute-start | bytes 196616 | tf_op jit(solution)/shard_map/ppermute | solution.py:267
  63.7 1.4 %collective-permute-done.30 = f32[4,2,8,8,128]{4,3,1,2,0:T(8,128)S(1)} collective-permute-done((f32[4,2,8,8,128]{4,3,1,2,0:T(8,128)S(1)}, f32[4,2,8,8,128]{4,3,1,2,0:T(8,128)S(1)}, u32[]{:S(2)}, u32[]{:S(2)}) %collective-permute-start.30) | collective-permute-done | bytes 262176 | tf_op jit(solution)/shard_map/ppermute | solution.py:271
  65.1 1.7 %collective-permute-start.12 = (f32[2,8,8,128]{3,2,0,1:T(8,128)S(1)}, f32[2,8,8,128]{3,2,0,1:T(8,128)S(1)}, u32[]{:S(2)}, u32[]{:S(2)}) collective-permute-start(f32[2,8,8,128]{3,2,0,1:T(8,128)S(1)} %get-tuple-element.43), channel_id=1, source_target_pairs={{0,4},{1,5},{2,6},{3,7},{4,0},{5,1},{6,2},{7,3},{8,12},{9,13},{10,... | collective-permute-start | bytes 196616 | tf_op jit(solution)/shard_map/ppermute | solution.py:267
  67.2 1.2 %collective-permute-start.26 = (f32[2,8,8,128]{3,2,0,1:T(8,128)S(1)}, f32[2,8,8,128]{3,2,0,1:T(8,128)S(1)}, u32[]{:S(2)}, u32[]{:S(2)}) collective-permute-start(f32[2,8,8,128]{3,2,0,1:T(8,128)S(1)} %get-tuple-element.47), channel_id=1, source_target_pairs={{0,16},{8,24},{16,0},{24,8},{32,48},{40,56},{48,32},{56,40},{64,80... | collective-permute-start | bytes 196616 | tf_op jit(solution)/shard_map/ppermute | solution.py:271
  68.4 2.5 %collective-permute-start.27 = (f32[2,8,8,128]{3,2,0,1:T(8,128)S(1)}, f32[2,8,8,128]{3,2,0,1:T(8,128)S(1)}, u32[]{:S(2)}, u32[]{:S(2)}) collective-permute-start(f32[2,8,8,128]{3,2,0,1:T(8,128)S(1)} %get-tuple-element.46), channel_id=1, source_target_pairs={{0,24},{8,0},{16,8},{24,16},{32,56},{40,32},{48,40},{56,48},{64,88... | collective-permute-start | bytes 196616 | tf_op jit(solution)/shard_map/ppermute | solution.py:271
  72.5 1.7 %collective-permute-start.32 = (f32[2,8,8,128]{3,2,0,1:T(8,128)S(1)}, f32[2,8,8,128]{3,2,0,1:T(8,128)S(1)}, u32[]{:S(2)}, u32[]{:S(2)}) collective-permute-start(f32[2,8,8,128]{3,2,0,1:T(8,128)S(1)} %get-tuple-element.59), channel_id=1, source_target_pairs={{0,2},{1,3},{2,4},{3,5},{4,6},{5,7},{6,0},{7,1},{8,10},{9,11},{10,... | collective-permute-start | bytes 196616 | tf_op jit(solution)/shard_map/ppermute | solution.py:267
  75.3 2.7 %collective-permute-start.14 = (f32[4,8,128]{2,1,0:T(8,128)S(1)}, f32[4,8,128]{2,1,0:T(8,128)S(1)}, u32[]{:S(2)}, u32[]{:S(2)}) collective-permute-start(f32[4,8,128]{2,1,0:T(8,128)S(1)} %pad_maximum_fusion), channel_id=1, source_target_pairs={{0,32},{8,40},{16,48},{24,56},{32,64},{40,72},{48,80},{56,88},{64,... | collective-permute-start | bytes 49160 | tf_op jit(solution)/shard_map/ppermute | solution.py:275
  78.0 3.3 %collective-permute-start.15 = (f32[4,8,128]{2,1,0:T(8,128)S(1)}, f32[4,8,128]{2,1,0:T(8,128)S(1)}, u32[]{:S(2)}, u32[]{:S(2)}) collective-permute-start(f32[4,8,128]{2,1,0:T(8,128)S(1)} %pad_maximum_fusion.1), channel_id=1, source_target_pairs={{0,64},{8,72},{16,80},{24,88},{32,96},{40,104},{48,112},{56,120},{... | collective-permute-start | bytes 49160 | tf_op jit(solution)/shard_map/ppermute | solution.py:275
  81.3 4.1 %collective-permute-start.16 = (f32[4,8,128]{2,1,0:T(8,128)S(1)}, f32[4,8,128]{2,1,0:T(8,128)S(1)}, u32[]{:S(2)}, u32[]{:S(2)}) collective-permute-start(f32[4,8,128]{2,1,0:T(8,128)S(1)} %pad_maximum_fusion.2), channel_id=1, source_target_pairs={{0,96},{8,104},{16,112},{24,120},{32,128},{40,136},{48,144},{56,15... | collective-permute-start | bytes 49160 | tf_op jit(solution)/shard_map/ppermute | solution.py:275
  86.0 4.9 %collective-permute-start.18 = (f32[4,8,128]{2,1,0:T(8,128)S(1)}, f32[4,8,128]{2,1,0:T(8,128)S(1)}, u32[]{:S(2)}, u32[]{:S(2)}) collective-permute-start(f32[4,8,128]{2,1,0:T(8,128)S(1)} %pad_maximum_fusion.4), channel_id=1, source_target_pairs={{0,160},{8,168},{16,176},{24,184},{32,192},{40,200},{48,208},{56,2... | collective-permute-start | bytes 49160 | tf_op jit(solution)/shard_map/ppermute | solution.py:275
  91.0 2.7 %collective-permute-start.19 = (f32[4,8,128]{2,1,0:T(8,128)S(1)}, f32[4,8,128]{2,1,0:T(8,128)S(1)}, u32[]{:S(2)}, u32[]{:S(2)}) collective-permute-start(f32[4,8,128]{2,1,0:T(8,128)S(1)} %pad_maximum_fusion.5), channel_id=1, source_target_pairs={{0,192},{8,200},{16,208},{24,216},{32,224},{40,232},{48,240},{56,2... | collective-permute-start | bytes 49160 | tf_op jit(solution)/shard_map/ppermute | solution.py:275
  96.1 1.8 %collective-permute-start.37 = (f32[4,8,128]{2,1,0:T(8,128)S(1)}, f32[4,8,128]{2,1,0:T(8,128)S(1)}, u32[]{:S(2)}, u32[]{:S(2)}) collective-permute-start(f32[4,8,128]{2,1,0:T(8,128)S(1)} %pad_maximum_fusion.9), channel_id=1, source_target_pairs={{0,96},{8,104},{16,112},{24,120},{32,128},{40,136},{48,144},{56,15... | collective-permute-start | bytes 49160 | tf_op jit(solution)/shard_map/ppermute | solution.py:275
  97.8 4.0 %collective-permute-start.38 = (f32[4,8,128]{2,1,0:T(8,128)S(1)}, f32[4,8,128]{2,1,0:T(8,128)S(1)}, u32[]{:S(2)}, u32[]{:S(2)}) collective-permute-start(f32[4,8,128]{2,1,0:T(8,128)S(1)} %pad_maximum_fusion.10), channel_id=1, source_target_pairs={{0,128},{8,136},{16,144},{24,152},{32,160},{40,168},{48,176},{56,1... | collective-permute-start | bytes 49160 | tf_op jit(solution)/shard_map/ppermute | solution.py:275
  101.8 1.9 %collective-permute-start.39 = (f32[4,8,128]{2,1,0:T(8,128)S(1)}, f32[4,8,128]{2,1,0:T(8,128)S(1)}, u32[]{:S(2)}, u32[]{:S(2)}) collective-permute-start(f32[4,8,128]{2,1,0:T(8,128)S(1)} %pad_maximum_fusion.11), channel_id=1, source_target_pairs={{0,160},{8,168},{16,176},{24,184},{32,192},{40,200},{48,208},{56,2... | collective-permute-start | bytes 49160 | tf_op jit(solution)/shard_map/ppermute | solution.py:275
  103.8 2.1 %collective-permute-start.40 = (f32[4,8,128]{2,1,0:T(8,128)S(1)}, f32[4,8,128]{2,1,0:T(8,128)S(1)}, u32[]{:S(2)}, u32[]{:S(2)}) collective-permute-start(f32[4,8,128]{2,1,0:T(8,128)S(1)} %pad_maximum_fusion.12), channel_id=1, source_target_pairs={{0,192},{8,200},{16,208},{24,216},{32,224},{40,232},{48,240},{56,2... | collective-permute-start | bytes 49160 | tf_op jit(solution)/shard_map/ppermute | solution.py:275
  105.9 1.5 %collective-permute-start.41 = (f32[4,8,128]{2,1,0:T(8,128)S(1)}, f32[4,8,128]{2,1,0:T(8,128)S(1)}, u32[]{:S(2)}, u32[]{:S(2)}) collective-permute-start(f32[4,8,128]{2,1,0:T(8,128)S(1)} %pad_maximum_fusion.13), channel_id=1, source_target_pairs={{0,224},{8,232},{16,240},{24,248},{32,0},{40,8},{48,16},{56,24},{6... | collective-permute-start | bytes 49160 | tf_op jit(solution)/shard_map/ppermute | solution.py:275
  107.5 1.8 %collective-permute-done.40 = f32[4,8,128]{2,1,0:T(8,128)S(1)} collective-permute-done((f32[4,8,128]{2,1,0:T(8,128)S(1)}, f32[4,8,128]{2,1,0:T(8,128)S(1)}, u32[]{:S(2)}, u32[]{:S(2)}) %collective-permute-start.40) | collective-permute-done | bytes 16416 | tf_op jit(solution)/shard_map/ppermute | solution.py:275
  (124 shorter events, 17.6 us)
Async XLA Ops:
  22.0 7.8 %collective-permute-start.7 = (f32[4,4,2,8,8,128]{5,4,2,3,1,0:T(8,128)S(1)}, f32[4,4,2,8,8,128]{5,4,2,3,1,0:T(8,128)S(1)}, u32[]{:S(2)}, u32[]{:S(2)}) collective-permute-start(f32[4,4,2,8,8,128]{5,4,2,3,1,0:T(8,128)S(1)} %copy.19), channel_id=1, source_target_pairs={{0,1},{1,0},{2,3},{3,2},{4,5},{5,4},{6,7},{7,6},{8,9},{9,8},{10,11... | collective-permute-start | bytes 3145736 | tf_op jit(solution)/shard_map/ppermute | solution.py:263
  26.1 7.0 %collective-permute-start.28 = (f32[4,4,2,8,8,128]{5,4,3,2,1,0:T(8,128)S(1)}, f32[4,4,2,8,8,128]{5,4,3,2,1,0:T(8,128)S(1)}, u32[]{:S(2)}, u32[]{:S(2)}) collective-permute-start(f32[4,4,2,8,8,128]{5,4,3,2,1,0:T(8,128)S(1)} %get-tuple-element.24), channel_id=1, source_target_pairs={{0,1},{1,0},{2,3},{3,2},{4,5},{5,4},{6,7},{7,6},{8,9},{9,8},{10,11... | collective-permute-start | bytes 3145736 | tf_op jit(solution)/shard_map/ppermute | solution.py:263
  26.8 13.8 %collective-permute-start.1 = (f32[2,4,8,8,128]{4,3,0,2,1:T(8,128)S(1)}, f32[2,4,8,8,128]{4,3,0,2,1:T(8,128)S(1)}, u32[]{:S(2)}, u32[]{:S(2)}) collective-permute-start(f32[2,4,8,8,128]{4,3,0,2,1:T(8,128)S(1)} %get-tuple-element.28), channel_id=1, source_target_pairs={{0,2},{1,3},{2,4},{3,5},{4,6},{5,7},{6,0},{7,1},{8,10},{9,11},{10,... | collective-permute-start | bytes 786440 | tf_op jit(solution)/shard_map/ppermute | solution.py:267
  29.1 11.6 %collective-permute-start.2 = (f32[2,4,8,8,128]{4,3,0,2,1:T(8,128)S(1)}, f32[2,4,8,8,128]{4,3,0,2,1:T(8,128)S(1)}, u32[]{:S(2)}, u32[]{:S(2)}) collective-permute-start(f32[2,4,8,8,128]{4,3,0,2,1:T(8,128)S(1)} %get-tuple-element.27), channel_id=1, source_target_pairs={{0,4},{1,5},{2,6},{3,7},{4,0},{5,1},{6,2},{7,3},{8,12},{9,13},{10,... | collective-permute-start | bytes 786440 | tf_op jit(solution)/shard_map/ppermute | solution.py:267
  29.7 14.6 %collective-permute-start.3 = (f32[2,4,8,8,128]{4,3,0,2,1:T(8,128)S(1)}, f32[2,4,8,8,128]{4,3,0,2,1:T(8,128)S(1)}, u32[]{:S(2)}, u32[]{:S(2)}) collective-permute-start(f32[2,4,8,8,128]{4,3,0,2,1:T(8,128)S(1)} %get-tuple-element.26), channel_id=1, source_target_pairs={{0,6},{1,7},{2,0},{3,1},{4,2},{5,3},{6,4},{7,5},{8,14},{9,15},{10,... | collective-permute-start | bytes 786440 | tf_op jit(solution)/shard_map/ppermute | solution.py:267
  30.1 16.4 %collective-permute-start.10 = (f32[4,2,8,8,128]{4,3,1,2,0:T(8,128)S(1)}, f32[4,2,8,8,128]{4,3,1,2,0:T(8,128)S(1)}, u32[]{:S(2)}, u32[]{:S(2)}) collective-permute-start(f32[4,2,8,8,128]{4,3,1,2,0:T(8,128)S(1)} %get-tuple-element.30), channel_id=1, source_target_pairs={{0,24},{8,0},{16,8},{24,16},{32,56},{40,32},{48,40},{56,48},{64,88... | collective-permute-start | bytes 786440 | tf_op jit(solution)/shard_map/ppermute | solution.py:271
  33.1 14.3 %collective-permute-start.8 = (f32[4,2,8,8,128]{4,3,1,2,0:T(8,128)S(1)}, f32[4,2,8,8,128]{4,3,1,2,0:T(8,128)S(1)}, u32[]{:S(2)}, u32[]{:S(2)}) collective-permute-start(f32[4,2,8,8,128]{4,3,1,2,0:T(8,128)S(1)} %get-tuple-element.32), channel_id=1, source_target_pairs={{0,8},{8,16},{16,24},{24,0},{32,40},{40,48},{48,56},{56,32},{64,72... | collective-permute-start | bytes 786440 | tf_op jit(solution)/shard_map/ppermute | solution.py:271
  40.5 8.0 %collective-permute-start.9 = (f32[4,2,8,8,128]{4,3,1,2,0:T(8,128)S(1)}, f32[4,2,8,8,128]{4,3,1,2,0:T(8,128)S(1)}, u32[]{:S(2)}, u32[]{:S(2)}) collective-permute-start(f32[4,2,8,8,128]{4,3,1,2,0:T(8,128)S(1)} %get-tuple-element.31), channel_id=1, source_target_pairs={{0,16},{8,24},{16,0},{24,8},{32,48},{40,56},{48,32},{56,40},{64,80... | collective-permute-start | bytes 786440 | tf_op jit(solution)/shard_map/ppermute | solution.py:271
  40.6 13.7 %collective-permute-start.22 = (f32[2,4,8,8,128]{4,3,0,2,1:T(8,128)S(1)}, f32[2,4,8,8,128]{4,3,0,2,1:T(8,128)S(1)}, u32[]{:S(2)}, u32[]{:S(2)}) collective-permute-start(f32[2,4,8,8,128]{4,3,0,2,1:T(8,128)S(1)} %get-tuple-element.36), channel_id=1, source_target_pairs={{0,2},{1,3},{2,4},{3,5},{4,6},{5,7},{6,0},{7,1},{8,10},{9,11},{10,... | collective-permute-start | bytes 786440 | tf_op jit(solution)/shard_map/ppermute | solution.py:267
  44.4 8.0 %collective-permute-start.31 = (f32[4,2,8,8,128]{4,3,2,1,0:T(8,128)S(1)}, f32[4,2,8,8,128]{4,3,2,1,0:T(8,128)S(1)}, u32[]{:S(2)}, u32[]{:S(2)}) collective-permute-start(f32[4,2,8,8,128]{4,3,2,1,0:T(8,128)S(1)} %get-tuple-element.54), channel_id=1, source_target_pairs={{0,24},{8,0},{16,8},{24,16},{32,56},{40,32},{48,40},{56,48},{64,88... | collective-permute-start | bytes 786440 | tf_op jit(solution)/shard_map/ppermute | solution.py:271
  46.5 10.8 %collective-permute-start.23 = (f32[2,4,8,8,128]{4,3,0,2,1:T(8,128)S(1)}, f32[2,4,8,8,128]{4,3,0,2,1:T(8,128)S(1)}, u32[]{:S(2)}, u32[]{:S(2)}) collective-permute-start(f32[2,4,8,8,128]{4,3,0,2,1:T(8,128)S(1)} %get-tuple-element.35), channel_id=1, source_target_pairs={{0,4},{1,5},{2,6},{3,7},{4,0},{5,1},{6,2},{7,3},{8,12},{9,13},{10,... | collective-permute-start | bytes 786440 | tf_op jit(solution)/shard_map/ppermute | solution.py:267
  47.4 13.3 %collective-permute-start.24 = (f32[2,4,8,8,128]{4,3,0,2,1:T(8,128)S(1)}, f32[2,4,8,8,128]{4,3,0,2,1:T(8,128)S(1)}, u32[]{:S(2)}, u32[]{:S(2)}) collective-permute-start(f32[2,4,8,8,128]{4,3,0,2,1:T(8,128)S(1)} %get-tuple-element.34), channel_id=1, source_target_pairs={{0,6},{1,7},{2,0},{3,1},{4,2},{5,3},{6,4},{7,5},{8,14},{9,15},{10,... | collective-permute-start | bytes 786440 | tf_op jit(solution)/shard_map/ppermute | solution.py:267
  48.6 13.0 %collective-permute-start.29 = (f32[4,2,8,8,128]{4,3,1,2,0:T(8,128)S(1)}, f32[4,2,8,8,128]{4,3,1,2,0:T(8,128)S(1)}, u32[]{:S(2)}, u32[]{:S(2)}) collective-permute-start(f32[4,2,8,8,128]{4,3,1,2,0:T(8,128)S(1)} %get-tuple-element.51), channel_id=1, source_target_pairs={{0,8},{8,16},{16,24},{24,0},{32,40},{40,48},{48,56},{56,32},{64,72... | collective-permute-start | bytes 786440 | tf_op jit(solution)/shard_map/ppermute | solution.py:271
  52.4 12.7 %collective-permute-start.30 = (f32[4,2,8,8,128]{4,3,1,2,0:T(8,128)S(1)}, f32[4,2,8,8,128]{4,3,1,2,0:T(8,128)S(1)}, u32[]{:S(2)}, u32[]{:S(2)}) collective-permute-start(f32[4,2,8,8,128]{4,3,1,2,0:T(8,128)S(1)} %get-tuple-element.50), channel_id=1, source_target_pairs={{0,16},{8,24},{16,0},{24,8},{32,48},{40,56},{48,32},{56,40},{64,80... | collective-permute-start | bytes 786440 | tf_op jit(solution)/shard_map/ppermute | solution.py:271
  54.3 12.6 %collective-permute-start.4 = (f32[2,8,8,128]{3,2,0,1:T(8,128)S(1)}, f32[2,8,8,128]{3,2,0,1:T(8,128)S(1)}, u32[]{:S(2)}, u32[]{:S(2)}) collective-permute-start(f32[2,8,8,128]{3,2,0,1:T(8,128)S(1)} %get-tuple-element.40), channel_id=1, source_target_pairs={{0,8},{8,16},{16,24},{24,0},{32,40},{40,48},{48,56},{56,32},{64,72... | collective-permute-start | bytes 196616 | tf_op jit(solution)/shard_map/ppermute | solution.py:271
  57.4 9.6 %collective-permute-start.5 = (f32[2,8,8,128]{3,2,0,1:T(8,128)S(1)}, f32[2,8,8,128]{3,2,0,1:T(8,128)S(1)}, u32[]{:S(2)}, u32[]{:S(2)}) collective-permute-start(f32[2,8,8,128]{3,2,0,1:T(8,128)S(1)} %get-tuple-element.39), channel_id=1, source_target_pairs={{0,16},{8,24},{16,0},{24,8},{32,48},{40,56},{48,32},{56,40},{64,80... | collective-permute-start | bytes 196616 | tf_op jit(solution)/shard_map/ppermute | solution.py:271
  67.1 7.3 %collective-permute-start.25 = (f32[2,8,8,128]{3,2,0,1:T(8,128)S(1)}, f32[2,8,8,128]{3,2,0,1:T(8,128)S(1)}, u32[]{:S(2)}, u32[]{:S(2)}) collective-permute-start(f32[2,8,8,128]{3,2,0,1:T(8,128)S(1)} %get-tuple-element.48), channel_id=1, source_target_pairs={{0,8},{8,16},{16,24},{24,0},{32,40},{40,48},{48,56},{56,32},{64,72... | collective-permute-start | bytes 196616 | tf_op jit(solution)/shard_map/ppermute | solution.py:271
  67.2 8.2 %collective-permute-start.26 = (f32[2,8,8,128]{3,2,0,1:T(8,128)S(1)}, f32[2,8,8,128]{3,2,0,1:T(8,128)S(1)}, u32[]{:S(2)}, u32[]{:S(2)}) collective-permute-start(f32[2,8,8,128]{3,2,0,1:T(8,128)S(1)} %get-tuple-element.47), channel_id=1, source_target_pairs={{0,16},{8,24},{16,0},{24,8},{32,48},{40,56},{48,32},{56,40},{64,80... | collective-permute-start | bytes 196616 | tf_op jit(solution)/shard_map/ppermute | solution.py:271
  68.4 9.6 %collective-permute-start.27 = (f32[2,8,8,128]{3,2,0,1:T(8,128)S(1)}, f32[2,8,8,128]{3,2,0,1:T(8,128)S(1)}, u32[]{:S(2)}, u32[]{:S(2)}) collective-permute-start(f32[2,8,8,128]{3,2,0,1:T(8,128)S(1)} %get-tuple-element.46), channel_id=1, source_target_pairs={{0,24},{8,0},{16,8},{24,16},{32,56},{40,32},{48,40},{56,48},{64,88... | collective-permute-start | bytes 196616 | tf_op jit(solution)/shard_map/ppermute | solution.py:271
  71.0 10.3 %collective-permute-start.34 = (f32[2,8,8,128]{3,2,1,0:T(8,128)S(1)}, f32[2,8,8,128]{3,2,1,0:T(8,128)S(1)}, u32[]{:S(2)}, u32[]{:S(2)}) collective-permute-start(f32[2,8,8,128]{3,2,1,0:T(8,128)S(1)} %fusion.14), channel_id=1, source_target_pairs={{0,6},{1,7},{2,0},{3,1},{4,2},{5,3},{6,4},{7,5},{8,14},{9,15},{10,... | collective-permute-start | bytes 196616 | tf_op jit(solution)/shard_map/ppermute | solution.py:267
  72.5 12.9 %collective-permute-start.32 = (f32[2,8,8,128]{3,2,0,1:T(8,128)S(1)}, f32[2,8,8,128]{3,2,0,1:T(8,128)S(1)}, u32[]{:S(2)}, u32[]{:S(2)}) collective-permute-start(f32[2,8,8,128]{3,2,0,1:T(8,128)S(1)} %get-tuple-element.59), channel_id=1, source_target_pairs={{0,2},{1,3},{2,4},{3,5},{4,6},{5,7},{6,0},{7,1},{8,10},{9,11},{10,... | collective-permute-start | bytes 196616 | tf_op jit(solution)/shard_map/ppermute | solution.py:267
  74.3 11.6 %collective-permute-start.33 = (f32[2,8,8,128]{3,2,0,1:T(8,128)S(1)}, f32[2,8,8,128]{3,2,0,1:T(8,128)S(1)}, u32[]{:S(2)}, u32[]{:S(2)}) collective-permute-start(f32[2,8,8,128]{3,2,0,1:T(8,128)S(1)} %get-tuple-element.58), channel_id=1, source_target_pairs={{0,4},{1,5},{2,6},{3,7},{4,0},{5,1},{6,2},{7,3},{8,12},{9,13},{10,... | collective-permute-start | bytes 196616 | tf_op jit(solution)/shard_map/ppermute | solution.py:267
  75.3 15.7 %collective-permute-start.14 = (f32[4,8,128]{2,1,0:T(8,128)S(1)}, f32[4,8,128]{2,1,0:T(8,128)S(1)}, u32[]{:S(2)}, u32[]{:S(2)}) collective-permute-start(f32[4,8,128]{2,1,0:T(8,128)S(1)} %pad_maximum_fusion), channel_id=1, source_target_pairs={{0,32},{8,40},{16,48},{24,56},{32,64},{40,72},{48,80},{56,88},{64,... | collective-permute-start | bytes 49160 | tf_op jit(solution)/shard_map/ppermute | solution.py:275
  78.0 15.8 %collective-permute-start.15 = (f32[4,8,128]{2,1,0:T(8,128)S(1)}, f32[4,8,128]{2,1,0:T(8,128)S(1)}, u32[]{:S(2)}, u32[]{:S(2)}) collective-permute-start(f32[4,8,128]{2,1,0:T(8,128)S(1)} %pad_maximum_fusion.1), channel_id=1, source_target_pairs={{0,64},{8,72},{16,80},{24,88},{32,96},{40,104},{48,112},{56,120},{... | collective-permute-start | bytes 49160 | tf_op jit(solution)/shard_map/ppermute | solution.py:275
  81.3 13.5 %collective-permute-start.16 = (f32[4,8,128]{2,1,0:T(8,128)S(1)}, f32[4,8,128]{2,1,0:T(8,128)S(1)}, u32[]{:S(2)}, u32[]{:S(2)}) collective-permute-start(f32[4,8,128]{2,1,0:T(8,128)S(1)} %pad_maximum_fusion.2), channel_id=1, source_target_pairs={{0,96},{8,104},{16,112},{24,120},{32,128},{40,136},{48,144},{56,15... | collective-permute-start | bytes 49160 | tf_op jit(solution)/shard_map/ppermute | solution.py:275
  85.4 10.4 %collective-permute-start.17 = (f32[4,8,128]{2,1,0:T(8,128)S(1)}, f32[4,8,128]{2,1,0:T(8,128)S(1)}, u32[]{:S(2)}, u32[]{:S(2)}) collective-permute-start(f32[4,8,128]{2,1,0:T(8,128)S(1)} %pad_maximum_fusion.3), channel_id=1, source_target_pairs={{0,128},{8,136},{16,144},{24,152},{32,160},{40,168},{48,176},{56,1... | collective-permute-start | bytes 49160 | tf_op jit(solution)/shard_map/ppermute | solution.py:275
  86.0 10.1 %collective-permute-start.18 = (f32[4,8,128]{2,1,0:T(8,128)S(1)}, f32[4,8,128]{2,1,0:T(8,128)S(1)}, u32[]{:S(2)}, u32[]{:S(2)}) collective-permute-start(f32[4,8,128]{2,1,0:T(8,128)S(1)} %pad_maximum_fusion.4), channel_id=1, source_target_pairs={{0,160},{8,168},{16,176},{24,184},{32,192},{40,200},{48,208},{56,2... | collective-permute-start | bytes 49160 | tf_op jit(solution)/shard_map/ppermute | solution.py:275
  93.8 8.1 %collective-permute-start.20 = (f32[4,8,128]{2,1,0:T(8,128)S(1)}, f32[4,8,128]{2,1,0:T(8,128)S(1)}, u32[]{:S(2)}, u32[]{:S(2)}) collective-permute-start(f32[4,8,128]{2,1,0:T(8,128)S(1)} %pad_maximum_fusion.6), channel_id=1, source_target_pairs={{0,224},{8,232},{16,240},{24,248},{32,0},{40,8},{48,16},{56,24},{6... | collective-permute-start | bytes 49160 | tf_op jit(solution)/shard_map/ppermute | solution.py:275
  94.8 9.0 %collective-permute-start.35 = (f32[4,8,128]{2,1,0:T(8,128)S(1)}, f32[4,8,128]{2,1,0:T(8,128)S(1)}, u32[]{:S(2)}, u32[]{:S(2)}) collective-permute-start(f32[4,8,128]{2,1,0:T(8,128)S(1)} %pad_maximum_fusion.7), channel_id=1, source_target_pairs={{0,32},{8,40},{16,48},{24,56},{32,64},{40,72},{48,80},{56,88},{64,... | collective-permute-start | bytes 49160 | tf_op jit(solution)/shard_map/ppermute | solution.py:275
  95.8 10.1 %collective-permute-start.36 = (f32[4,8,128]{2,1,0:T(8,128)S(1)}, f32[4,8,128]{2,1,0:T(8,128)S(1)}, u32[]{:S(2)}, u32[]{:S(2)}) collective-permute-start(f32[4,8,128]{2,1,0:T(8,128)S(1)} %pad_maximum_fusion.8), channel_id=1, source_target_pairs={{0,64},{8,72},{16,80},{24,88},{32,96},{40,104},{48,112},{56,120},{... | collective-permute-start | bytes 49160 | tf_op jit(solution)/shard_map/ppermute | solution.py:275
  96.1 11.4 %collective-permute-start.37 = (f32[4,8,128]{2,1,0:T(8,128)S(1)}, f32[4,8,128]{2,1,0:T(8,128)S(1)}, u32[]{:S(2)}, u32[]{:S(2)}) collective-permute-start(f32[4,8,128]{2,1,0:T(8,128)S(1)} %pad_maximum_fusion.9), channel_id=1, source_target_pairs={{0,96},{8,104},{16,112},{24,120},{32,128},{40,136},{48,144},{56,15... | collective-permute-start | bytes 49160 | tf_op jit(solution)/shard_map/ppermute | solution.py:275
  97.8 9.6 %collective-permute-start.38 = (f32[4,8,128]{2,1,0:T(8,128)S(1)}, f32[4,8,128]{2,1,0:T(8,128)S(1)}, u32[]{:S(2)}, u32[]{:S(2)}) collective-permute-start(f32[4,8,128]{2,1,0:T(8,128)S(1)} %pad_maximum_fusion.10), channel_id=1, source_target_pairs={{0,128},{8,136},{16,144},{24,152},{32,160},{40,168},{48,176},{56,1... | collective-permute-start | bytes 49160 | tf_op jit(solution)/shard_map/ppermute | solution.py:275
  (25 other events, 92.4 us)

commit v2 on v1

v2 whole, which is shorter than its diff:
```python
import functools

import jax
import jax.numpy as jnp
from jax import lax
from jax.experimental import pallas as pl
from jax.experimental.pallas import tpu as pltpu
from jax.sharding import PartitionSpec as P

F32 = jnp.float32
BF16 = jnp.bfloat16
NX, NY, NZ = 4, 4, 8
SEGS = 64
ROWS = 16
WIDTH = 512
TAPS = 21
REACH = 10
NBASIS = 3
LANES = 128
BLOCKS = WIDTH // LANES
BLOCK_SEGS = 16
BLOCK_ROWS = BLOCK_SEGS * ROWS


def split(value):
    high = value.astype(BF16)
    return high, (value - high.astype(F32)).astype(BF16)


def column_factor(bits):
    bad = (bits & 1).astype(F32)
    full = ((bits >> 1) & 1).astype(F32)
    cosmic = ((bits >> 2) & 1).astype(F32)
    return (1.0 - bad) * (1.0 - 0.75 * full) * (1.0 - 0.5 * cosmic)


def column_warp(base, frac):
    source = lax.broadcasted_iota(jnp.int32, (WIDTH, base.shape[1]), 0)
    return jnp.where(source == base, 1.0 - frac, 0.0) + jnp.where(source == base + 1, frac, 0.0)


def column_of(ref, shape):
    row = lax.broadcasted_iota(jnp.int32, shape, 0)
    result = jnp.full(shape, ref[0, 0])
    for i in range(1, ROWS):
        result = jnp.where(row == i, ref[0, i], result)
    return result


A_FIRST = (0, 3, 1, 2)
B_FIRST = (0, 1, 3, 2)


def relative_patch(place_ref, owner):
    ry = (owner % NY) ^ place_ref[2]
    rz = (owner // NY) ^ place_ref[3]
    return ry, (rz & 1) * 4 + ((rz >> 1) ^ (rz >> 2)) % 2 * 2 + (rz >> 2)


def write_out(place_ref, source, keep, send, sems, order):
    copies = []
    for to, core in ((keep, place_ref[0]), (send, 1 - place_ref[0])):
        for pu, ru in enumerate(order):
            for pv, rv in enumerate(A_FIRST):
                rx = ru + core * (rv - ru)
                ry = rv + core * (ru - rv)
                rows = pl.ds(pl.multiple_of((place_ref[1] ^ rx) * 16, 16), 16)
                copies.append((source(core, ry, rows), to.at[pu, pv]))
    started = [pltpu.make_async_copy(src, dst, sems.at[i]) for i, (src, dst) in enumerate(copies)]
    for copy in started:
        copy.start()
    for copy in started:
        copy.wait()


def denom_kernel(
    place_hbm, owner_hbm, offset_hbm, weight_hbm, frac_hbm, bits_ref, col_base_ref, col_frac_ref,
    keep, send, place_ref, owner_ref, offset_ref, weight_ref, frac_ref, sums, cover, sems,
):
    small = [
        pltpu.make_async_copy(src, dst, sems.at[i])
        for i, (src, dst) in enumerate(
            (
                (place_hbm, place_ref), (owner_hbm, owner_ref), (offset_hbm, offset_ref),
                (weight_hbm, weight_ref), (frac_hbm, frac_ref),
            )
        )
    ]
    for copy in small:
        copy.start()
    factor = column_factor(bits_ref[0]).astype(BF16)
    warp_high, warp_low = split(column_warp(col_base_ref[...], col_frac_ref[...]))
    coverage = jnp.dot(factor, warp_high, preferred_element_type=F32) + jnp.dot(
        factor, warp_low, preferred_element_type=F32
    )
    for block in range(BLOCKS):
        cover[block // 2, block % 2] = coverage[:, block * LANES : (block + 1) * LANES]
    sums[...] = jnp.zeros(sums.shape, F32)
    for copy in small:
        copy.wait()
    frac = column_of(frac_ref, (ROWS, LANES))
    spread = (1.0 - frac) + frac

    def one(s, carry):
        ry, rz = relative_patch(place_ref, owner_ref[0, s])
        rows = pl.ds(offset_ref[0, s], ROWS)
        share = spread * weight_ref[0, s]
        for half in range(2):
            for j in range(2):
                sums[half, j, ry, rz, rows, :] += share * cover[half, j, pl.ds(s, 1), :]
        return carry

    lax.fori_loop(0, SEGS, one, 0, unroll=2)
    write_out(place_ref, lambda core, ry, rows: sums.at[core, :, ry, :, rows, :], keep, send, sems, A_FIRST)


def row_tables(bank_ref, index_ref, coeff_ref, base_ref, frac_ref, k):
    shape = (ROWS, BLOCK_ROWS)
    delta = lax.broadcasted_iota(jnp.int32, shape, 1) % ROWS - column_of(base_ref, shape) + REACH
    frac = column_of(frac_ref, shape)
    term = index_ref[0, k]
    lower = jnp.zeros(shape, F32)
    higher = jnp.zeros(shape, F32)
    for tap in range(TAPS):
        value = bank_ref[term, 0, tap]
        lower = jnp.where(delta == tap, value, lower)
        higher = jnp.where(delta == tap + 1, value, higher)
    return ((1.0 - frac) * lower + frac * higher) * coeff_ref[0, k]


def band_tables(bank_ref, index_ref, k):
    lane = lax.broadcasted_iota(jnp.int32, (LANES, WIDTH), 1)
    term = index_ref[0, k]
    base = jnp.zeros((LANES, WIDTH), F32)
    for tap in range(TAPS):
        base = jnp.where(lane == LANES + REACH - tap, bank_ref[term, 1, tap], base)
    return pltpu.roll(base, 0, 1, stride=1, stride_axis=0)[:, : 3 * LANES]


def rows_kernel(
    bank_ref, index_ref, coeff_ref, base_ref, frac_ref, bits_ref, pixels_ref, after, u_high, u_low, blockdiag
):
    same = (
        lax.broadcasted_iota(jnp.int32, (BLOCK_ROWS, BLOCK_ROWS), 0) // ROWS
        == lax.broadcasted_iota(jnp.int32, (BLOCK_ROWS, BLOCK_ROWS), 1) // ROWS
    )
    for k in range(NBASIS):
        table = row_tables(bank_ref, index_ref, coeff_ref, base_ref, frac_ref, k)
        whole = jnp.where(same, jnp.concatenate([table] * BLOCK_SEGS, axis=0), 0.0)
        high, low = split(whole)
        rows = slice(k * BLOCK_ROWS, (k + 1) * BLOCK_ROWS)
        blockdiag[rows, 0:BLOCK_ROWS] = high
        blockdiag[rows, BLOCK_ROWS : 2 * BLOCK_ROWS] = high
        blockdiag[rows, 2 * BLOCK_ROWS :] = low

    def one(b, carry):
        segs = pl.ds(b * BLOCK_SEGS, BLOCK_SEGS)
        factor = column_factor(bits_ref[0, segs, :])
        masked = (pixels_ref[0, segs] * factor[:, None, :]).reshape(BLOCK_ROWS, WIDTH)
        high, low = split(masked)
        product = jnp.dot(
            blockdiag[...], jnp.concatenate([high, low, high], axis=0), preferred_element_type=F32
        )
        rows = pl.ds(pl.multiple_of(b * BLOCK_ROWS, BLOCK_ROWS), BLOCK_ROWS)
        for k in range(NBASIS):
            part_high, part_low = split(product[k * BLOCK_ROWS : (k + 1) * BLOCK_ROWS])
            u_high[rows, k * WIDTH : (k + 1) * WIDTH] = part_high
            u_low[rows, k * WIDTH : (k + 1) * WIDTH] = part_low
        return carry

    lax.fori_loop(0, SEGS // BLOCK_SEGS, one, 0)


def band_kernel(bank_ref, index_ref, u_high, u_low, after, high_ref, low_ref, band_high, band_low):
    band_high[...] = jnp.zeros(band_high.shape, BF16)
    band_low[...] = jnp.zeros(band_low.shape, BF16)
    for k in range(NBASIS):
        high, low = split(band_tables(bank_ref, index_ref, k))
        for block in range(BLOCKS):
            first = max(block - 1, 0)
            last = min(block + 1, BLOCKS - 1)
            rows = slice(k * WIDTH + block * LANES, k * WIDTH + (block + 1) * LANES)
            to = slice(first * LANES, (last + 1) * LANES)
            of = slice((first - block + 1) * LANES, (last - block + 2) * LANES)
            band_high[rows, to] = high[:, of]
            band_low[rows, to] = low[:, of]
    dot = functools.partial(jnp.dot, preferred_element_type=F32)

    def one(b, carry):
        rows = pl.ds(pl.multiple_of(b * BLOCK_ROWS, BLOCK_ROWS), BLOCK_ROWS)
        part_high = u_high[rows, :]
        part_low = u_low[rows, :]
        wide = dot(part_high, band_high[...]) + dot(part_high, band_low[...]) + dot(part_low, band_high[...])
        high, low = split(wide)
        high_ref[rows, :] = high
        low_ref[rows, :] = low
        return carry

    lax.fori_loop(0, SEGS * ROWS // BLOCK_ROWS, one, 0)


def place_kernel(
    chunk, place_ref, owner_ref, offset_ref, weight_ref, col_base_ref, col_frac_ref, high_ref, low_ref, after,
    keep, send, sums, lifted, sems,
):
    picked = [slice((2 * half + chunk) * LANES, (2 * half + chunk + 1) * LANES) for half in range(2)]
    base = jnp.concatenate([col_base_ref[:, cols] for cols in picked], axis=1)
    frac = jnp.concatenate([col_frac_ref[:, cols] for cols in picked], axis=1)
    warp_high, warp_low = split(column_warp(base, frac))
    dot = functools.partial(jnp.dot, preferred_element_type=F32)
    high = high_ref[...]
    warped = dot(high, warp_high) + dot(high, warp_low) + dot(low_ref[...], warp_high)
    for half in range(2):
        lifted[half] = warped[:, half * LANES : (half + 1) * LANES]
    sums[...] = jnp.zeros(sums.shape, F32)

    def one(s, carry):
        ry, rz = relative_patch(place_ref, owner_ref[0, s])
        rows = pl.ds(offset_ref[0, s], ROWS)
        weight = weight_ref[0, s]
        of = pl.ds(pl.multiple_of(s * ROWS, ROWS), ROWS)
        for half in range(2):
            sums[half, ry, rz, rows, :] += weight * lifted[half, of, :]
        return carry

    lax.fori_loop(0, SEGS, one, 0, unroll=2)
    order = (A_FIRST, B_FIRST)[chunk]
    write_out(place_ref, lambda core, ry, rows: sums.at[core, ry, :, rows, :], keep, send, sems, order)


SMEM = pl.BlockSpec(memory_space=pltpu.SMEM)
VMEM = pl.BlockSpec(memory_space=pltpu.VMEM)
ANY = pl.BlockSpec(memory_space=pl.ANY)
PARAMS = pltpu.CompilerParams(vmem_limit_bytes=40 * 1024 * 1024)


def denom_sums(place, owner, offset, weight, row_frac, bits, col_base, col_frac):
    parts = jax.ShapeDtypeStruct((4, 4, 2, NZ, 16, LANES), F32)
    return pl.pallas_call(
        denom_kernel,
        out_shape=(parts, parts),
        in_specs=[ANY] * 5 + [VMEM] * 3,
        out_specs=(ANY,) * 2,
        scratch_shapes=[
            pltpu.SMEM((4,), jnp.int32), pltpu.SMEM((1, SEGS), jnp.int32), pltpu.SMEM((1, SEGS), jnp.int32),
            pltpu.SMEM((1, SEGS), F32), pltpu.SMEM((1, ROWS), F32),
            pltpu.VMEM((2, 2, NY, NZ, 64, LANES), F32), pltpu.VMEM((2, 2, SEGS, LANES), F32),
            pltpu.SemaphoreType.DMA((32,)),
        ],
        compiler_params=PARAMS,
        cost_estimate=pl.CostEstimate(flops=4 * 10**9, bytes_accessed=4 * 10**6, transcendentals=0),
        name="denom_sums",
    )(place, owner, offset, weight, row_frac, bits, col_base, col_frac)


def row_pass(bank, index, coeff, row_base, row_frac, bits, pixels, after):
    wide = jax.ShapeDtypeStruct((SEGS * ROWS, NBASIS * WIDTH), BF16)
    return pl.pallas_call(
        rows_kernel,
        out_shape=(wide, wide),
        in_specs=[SMEM] * 5 + [VMEM] * 2 + [ANY],
        out_specs=(VMEM, VMEM),
        scratch_shapes=[pltpu.VMEM((NBASIS * BLOCK_ROWS, 3 * BLOCK_ROWS), BF16)],
        compiler_params=PARAMS,
        cost_estimate=pl.CostEstimate(flops=4 * 10**9, bytes_accessed=8 * 10**6, transcendentals=0),
        name="row_pass",
    )(bank, index, coeff, row_base, row_frac, bits, pixels, after)


def band_pass(bank, index, u_high, u_low, after):
    wide = jax.ShapeDtypeStruct((SEGS * ROWS, WIDTH), BF16)
    band = pltpu.VMEM((NBASIS * WIDTH, WIDTH), BF16)
    return pl.pallas_call(
        band_kernel,
        out_shape=(wide, wide),
        in_specs=[SMEM] * 2 + [VMEM] * 2 + [ANY],
        out_specs=(VMEM, VMEM),
        scratch_shapes=[band, band],
        compiler_params=PARAMS,
        cost_estimate=pl.CostEstimate(flops=6 * 10**9, bytes_accessed=8 * 10**6, transcendentals=0),
        name="band_pass",
    )(bank, index, u_high, u_low, after)


def numer_sums(chunk, place, owner, offset, weight, col_base, col_frac, high, low, after):
    parts = jax.ShapeDtypeStruct((4, 4, NZ, 16, LANES), F32)
    return pl.pallas_call(
        functools.partial(place_kernel, chunk),
        out_shape=(parts, parts),
        in_specs=[SMEM] * 4 + [VMEM] * 4 + [ANY],
        out_specs=(ANY,) * 2,
        scratch_shapes=[
            pltpu.VMEM((2, NY, NZ, 64, LANES), F32), pltpu.VMEM((2, SEGS * ROWS, LANES), F32),
            pltpu.SemaphoreType.DMA((32,)),
        ],
        compiler_params=PARAMS,
        cost_estimate=pl.CostEstimate(flops=3 * 10**9, bytes_accessed=4 * 10**6, transcendentals=0),
        name=f"numer_sums_{chunk}",
    )(place, owner, offset, weight, col_base, col_frac, high, low, after)


def permute(value, partner):
    pairs = []
    for z in range(NZ):
        for y in range(NY):
            for x in range(NX):
                for core in range(2):
                    to_core, to_x, to_y, to_z = partner(core, x, y, z)
                    source = (z * NY + y) * 2 * NX + x * 2 + core
                    pairs.append((source, (to_z * NY + to_y) * 2 * NX + to_x * 2 + to_core))
    return lax.ppermute(value, ("sky", "grp"), pairs)


def swap_core(value):
    return permute(value, lambda core, x, y, z: (1 - core, x, y, z))


def swap_u(value, step):
    return permute(value, lambda core, x, y, z: (core, x, y ^ step, z) if core else (core, x ^ step, y, z))


def swap_v(value, step):
    return permute(value, lambda core, x, y, z: (core, x ^ step, y, z) if core else (core, x, y ^ step, z))


def swap_z(value, step):
    return permute(value, lambda core, x, y, z: (core, x, y, z ^ step))


def halve(keep, got):
    middle = keep.shape[0] // 2
    return keep[:middle] + got[:middle], keep[middle:] + got[middle:]


def per_device(
    pixels, mask_bits, owner, row_offset, seg_weight, psf_bank, basis_index, basis_coeff,
    row_base, row_frac, col_base, col_frac,
):
    sky = lax.axis_index("sky").astype(jnp.int32)
    grp = lax.axis_index("grp").astype(jnp.int32)
    place = jnp.stack([grp % 2, grp // 2, sky % NY, sky // NY])
    d_keep, d_send = denom_sums(place, owner, row_offset, seg_weight, row_frac, mask_bits, col_base, col_frac)
    u_high, u_low = row_pass(psf_bank, basis_index, basis_coeff, row_base, row_frac, mask_bits, pixels, d_send)
    d_keep, d_send = halve(d_keep, swap_core(d_send))
    high, low = band_pass(psf_bank, basis_index, u_high, u_low, d_send)
    d_got = swap_u(d_send, 1)
    first = numer_sums(0, place, owner, row_offset, seg_weight, col_base, col_frac, high, low, high)
    second = numer_sums(1, place, owner, row_offset, seg_weight, col_base, col_frac, high, low, first[1])
    n_parts = [halve(keep, swap_core(send)) for keep, send in (first, second)]
    d_keep, d_send = halve(d_keep, d_got)
    d_got = swap_u(d_send, 3)
    n_parts = [halve(keep, swap_u(send, step)) for (keep, send), step in zip(n_parts, (1, 3))]
    n_parts = [keep[0] + swap_u(send, step)[0] for (keep, send), step in zip(n_parts, (3, 1))]
    d_part = (d_keep + d_got)[0]
    both = jnp.concatenate([jnp.stack(n_parts, axis=1), d_part], axis=1)
    keep, send = halve(both[:2], swap_v(both[2:], 1))
    both = jnp.swapaxes((keep + swap_v(send, 3))[0], 0, 1)
    keep, send = halve(both[:4], swap_z(both[4:], 1))
    keep, send = halve(keep, swap_z(send, 2))
    both = (keep + swap_z(send, 6))[0]
    coadd = both[:2] / jnp.maximum(both[2:], 1.0)
    coadd = jnp.swapaxes(coadd.reshape(2, 2, 8, LANES), 0, 1)
    odd = place[0] == 1
    mine = jnp.where(odd, coadd[1], coadd[0])
    other = swap_core(jnp.where(odd, coadd[0], coadd[1]))
    blocks = jnp.where(odd, jnp.concatenate([other, mine]), jnp.concatenate([mine, other]))
    return jnp.swapaxes(blocks, 0, 1).reshape(8, WIDTH)


def solution(mesh):
    placed = (
        P("grp", "sky", None, None),
        P("grp", "sky", None),
        P("grp", "sky"),
        P("grp", "sky"),
        P("grp", "sky"),
        P(),
        P("grp", None),
        P("grp", None),
        P("grp", None),
        P("grp", None),
        P("grp", None),
        P("grp", None),
    )
    return jax.shard_map(
        per_device, mesh=mesh, in_specs=placed, out_specs=P(("sky", "grp"), None), check_vma=False
    )
```

time: 112 us -> 95.5 us (0.85)
  starting transfers between devices: 64.4 us -> 25.8 us
  waiting for transfers between devices: 18.4 us -> 40.1 us
  Pallas kernels: 19 us -> 20.8 us
  local copies, waits for them, and re-layouts: 6.14 us -> 4.97 us
    ppermute x42 -> x15, starting transfers between devices: 64.4 us -> 25.8 us  [permute(): return lax.ppermute(value, ('sky', 'grp'), pairs)]
    ppermute x42 -> x15, waiting for transfers between devices: 18.4 us -> 40.1 us  [permute(): return lax.ppermute(value, ('sky', 'grp'), pairs)]
    pallas_call x2 -> x4, Pallas kernels: 14.7 us -> 16.5 us  [the longest x2 7.1 us: numer_sums(): pl.pallas_call(functools.partial(place_kernel, chunk), out_shape=(parts,...]
  transfers between devices with their start and end apart: 42 -> 15, of which waited for: 8 -> 11; matrix products, arithmetic and copies ran while one was open for 1% -> 1% of each run, Pallas kernels for 3% -> 5%
where the time goes in v2:
time: 95.5 us; the launch traced here: 93.8 us
  waiting for transfers between devices  40.1 us (42%)
  starting transfers between devices  25.8 us (27%)
  Pallas kernels  20.8 us (22%)
  local copies, waits for them, and re-layouts  4.97 us (5%)
  other arithmetic  1.85 us (2%)
    ppermute x15, waiting for transfers between devices, permute(): return lax.ppermute(value, ('sky', 'grp'), pairs)  40.1 us
    ppermute x15, starting transfers between devices, permute(): return lax.ppermute(value, ('sky', 'grp'), pairs)  25.8 us
    pallas_call x2, Pallas kernels, numer_sums(): pl.pallas_call(functools.partial(place_kernel, chunk), out_shape=(parts,...  7.1 us
    pallas_call x1, Pallas kernels, band_pass(): pl.pallas_call(band_kernel, out_shape=(wide, wide), in_specs=[SMEM] * 2 +...  6.51 us
    unnamed x30, local copies, waits for them, and re-layouts  4.93 us
    pallas_call x1, Pallas kernels, row_pass(): pl.pallas_call(rows_kernel, out_shape=(wide, wide), in_specs=[SMEM] * 5 +...  4.26 us
    pallas_call x1, Pallas kernels, denom_sums(): pl.pallas_call(denom_kernel, out_shape=(parts, parts), in_specs=[ANY] * 5...  2.94 us
  transfers between devices with their start and end apart: 15, of which 11 were waited for; matrix products, arithmetic and copies ran while one was open for 1% of the time, Pallas kernels for 5%

profile of v2, /device:TPU:6, one launch (start us, length us, event | category | flops | bytes accessed | tf_op | source)
XLA Modules:
  0.0 93.8 jit_solution(14744690874060341363)
XLA Ops:
  0.1 0.9 copy-done.1
  1.0 0.7 copy-done.3
  1.7 0.7 copy-done.5
  2.4 0.7 copy-done.7
  3.0 0.7 copy-done.11
  3.7 0.7 copy-done.12
  4.3 0.7 copy-done.13
  5.0 2.9 %denom_sums.1 = (f32[4,4,2,8,16,128]{5,4,3,2,1,0:T(8,128)S(1)}, f32[4,4,2,8,16,128]{5,4,3,2,1,0:T(8,128)S(1)}) custom-call(s32[4]{0:T(128)S(1)} %pad_add_fusion.place_hbm.place_ref, s32[1,64]{1,0:T(1,128)S(1)} %copy-done.11, s32[1,64]{1,0:T(1,128)S(1)} %copy-done.12, f32[1,64]{1,0:T(1,128)S(1)} %copy-done.13, f32[1,16]{1,0:T(1,128)S(1)} %copy-done.7, ...), custom_call_target="tpu_custom_call" | custom-call | flops 4000000000 | bytes 4000000 | tf_op jit(solution)/shard_map/denom_sums/pallas_call | solution.py:239
  8.1 4.3 %row_pass.1 = (bf16[1024,1536]{1,0:T(8,128)(2,1)S(1)}, bf16[1024,1536]{1,0:T(8,128)(2,1)S(1)}) custom-call(f32[8,2,21]{2,1,0:T(2,128)S(1)} %copy-done.2, s32[1,3]{1,0:T(1,128)S(1)} %copy-done.10, f32[1,3]{1,0:T(1,128)S(1)} %copy-done.8, s32[1,16]{1,0:T(1,128)S(1)} %copy-done.9, f32[1,16]{1,0:T(1,128)S(1)} %copy-done.7, s32[1,64,512]{2,1,0:T(8,128)S(1)} %copy-done.1, ...), custom_call_target="tpu_custom_call" | custom-call | flops 4000000000 | bytes 8000000 | tf_op jit(solution)/shard_map/row_pass/pallas_call | solution.py:258
  12.7 6.5 %band_pass.1 = (bf16[1024,512]{1,0:T(8,128)(2,1)S(1)}, bf16[1024,512]{1,0:T(8,128)(2,1)S(1)}) custom-call(f32[8,2,21]{2,1,0:T(2,128)S(1)} %copy-done.2, s32[1,3]{1,0:T(1,128)S(1)} %copy-done.10, bf16[1024,1536]{1,0:T(8,128)(2,1)S(1)} %get-tuple-element.16.u_high, bf16[1024,1536]{1,0:T(8,128)(2,1)S(1)} %get-tuple-element.17.u_low, ...), custom_call_target="tpu_custom_call" | custom-call | flops 6000000000 | bytes 8000000 | tf_op jit(solution)/shard_map/band_pass/pallas_call | solution.py:273
  19.2 3.5 %numer_sums_0.1 = (f32[4,4,8,16,128]{4,3,2,1,0:T(8,128)S(1)}, f32[4,4,8,16,128]{4,3,2,1,0:T(8,128)S(1)}) custom-call(s32[4]{0:T(128)S(1)} %pad_add_fusion.place_hbm.place_ref, s32[1,64]{1,0:T(1,128)S(1)} %copy-done.11, s32[1,64]{1,0:T(1,128)S(1)} %copy-done.12, f32[1,64]{1,0:T(1,128)S(1)} %copy-done.14, s32[1,512]{1,0:T(1,128)S(1)} %copy-done.4, ...), custom_call_target="tpu_custom_call" | custom-call | flops 3000000000 | bytes 4000000 | tf_op jit(solution)/shard_map/numer_sums_0/pallas_call | solution.py:287
  22.8 3.5 %numer_sums_1.1 = (f32[4,4,8,16,128]{4,3,2,1,0:T(8,128)S(1)}, f32[4,4,8,16,128]{4,3,2,1,0:T(8,128)S(1)}) custom-call(s32[4]{0:T(128)S(1)} %pad_add_fusion.place_hbm.place_ref, s32[1,64]{1,0:T(1,128)S(1)} %copy-done.11, s32[1,64]{1,0:T(1,128)S(1)} %copy-done.12, f32[1,64]{1,0:T(1,128)S(1)} %copy-done.14, s32[1,512]{1,0:T(1,128)S(1)} %copy-done.4, ...), custom_call_target="tpu_custom_call" | custom-call | flops 3000000000 | bytes 4000000 | tf_op jit(solution)/shard_map/numer_sums_1/pallas_call | solution.py:287
  27.0 0.8 collective-permute-start.7
  27.8 1.4 %collective-permute-done.4 = f32[4,4,8,16,128]{4,3,2,1,0:T(8,128)S(1)} collective-permute-done((f32[4,4,8,16,128]{4,3,2,1,0:T(8,128)S(1)}, f32[4,4,8,16,128]{4,3,2,1,0:T(8,128)S(1)}, u32[]{:S(2)}, u32[]{:S(2)}) %collective-permute-start.4) | collective-permute-done | bytes 1048608 | tf_op jit(solution)/shard_map/ppermute | solution.py:311
  29.4 2.3 %collective-permute-start.5 = (f32[2,4,8,16,128]{4,3,2,1,0:T(8,128)S(1)}, f32[2,4,8,16,128]{4,3,2,1,0:T(8,128)S(1)}, u32[]{:S(2)}, u32[]{:S(2)}) collective-permute-start(f32[2,4,8,16,128]{4,3,2,1,0:T(8,128)S(1)} %get-tuple-element.30), channel_id=1, source_target_pairs={{0,6},{1,25},{2,4},{3,27},{4,2},{5,29},{6,0},{7,31},{8,14},{9,17},... | collective-permute-start | bytes 1572872 | tf_op jit(solution)/shard_map/ppermute | solution.py:311
  31.9 9.9 %collective-permute-done.7 = f32[2,4,2,8,16,128]{5,4,3,2,1,0:T(8,128)S(1)} collective-permute-done((f32[2,4,2,8,16,128]{5,4,3,2,1,0:T(8,128)S(1)}, f32[2,4,2,8,16,128]{5,4,3,2,1,0:T(8,128)S(1)}, u32[]{:S(2)}, u32[]{:S(2)}) %collective-permute-start.7) | collective-permute-done | bytes 1048608 | tf_op jit(solution)/shard_map/ppermute | solution.py:311
  41.9 2.3 %collective-permute-start.8 = (f32[1,4,2,8,16,128]{5,4,3,2,1,0:T(8,128)S(1)}, f32[1,4,2,8,16,128]{5,4,3,2,1,0:T(8,128)S(1)}, u32[]{:S(2)}, u32[]{:S(2)}) collective-permute-start(f32[1,4,2,8,16,128]{5,4,3,2,1,0:T(8,128)S(1)} %slice_add_fusion.2), channel_id=1, source_target_pairs={{0,6},{1,25},{2,4},{3,27},{4,2},{5,29},{6,0},{7,31},{8,14},{9,17},... | collective-permute-start | bytes 1572872 | tf_op jit(solution)/shard_map/ppermute | solution.py:311
  44.3 3.1 %collective-permute-done.2 = f32[2,4,8,16,128]{4,3,2,1,0:T(8,128)S(1)} collective-permute-done((f32[2,4,8,16,128]{4,3,2,1,0:T(8,128)S(1)}, f32[2,4,8,16,128]{4,3,2,1,0:T(8,128)S(1)}, u32[]{:S(2)}, u32[]{:S(2)}) %collective-permute-start.2) | collective-permute-done | bytes 524320 | tf_op jit(solution)/shard_map/ppermute | solution.py:311
  47.5 2.5 %collective-permute-start.3 = (f32[1,4,8,16,128]{4,3,2,1,0:T(8,128)S(1)}, f32[1,4,8,16,128]{4,3,2,1,0:T(8,128)S(1)}, u32[]{:S(2)}, u32[]{:S(2)}) collective-permute-start(f32[1,4,8,16,128]{4,3,2,1,0:T(8,128)S(1)} %slice_add_fusion.12), channel_id=1, source_target_pairs={{0,6},{1,25},{2,4},{3,27},{4,2},{5,29},{6,0},{7,31},{8,14},{9,17},... | collective-permute-start | bytes 786440 | tf_op jit(solution)/shard_map/ppermute | solution.py:311
  49.9 2.4 %collective-permute-done.8 = f32[1,4,2,8,16,128]{5,4,3,2,1,0:T(8,128)S(1)} collective-permute-done((f32[1,4,2,8,16,128]{5,4,3,2,1,0:T(8,128)S(1)}, f32[1,4,2,8,16,128]{5,4,3,2,1,0:T(8,128)S(1)}, u32[]{:S(2)}, u32[]{:S(2)}) %collective-permute-start.8) | collective-permute-done | bytes 524320 | tf_op jit(solution)/shard_map/ppermute | solution.py:311
  52.6 2.8 %collective-permute-done.3 = f32[1,4,8,16,128]{4,3,2,1,0:T(8,128)S(1)} collective-permute-done((f32[1,4,8,16,128]{4,3,2,1,0:T(8,128)S(1)}, f32[1,4,8,16,128]{4,3,2,1,0:T(8,128)S(1)}, u32[]{:S(2)}, u32[]{:S(2)}) %collective-permute-start.3) | collective-permute-done | bytes 262176 | tf_op jit(solution)/shard_map/ppermute | solution.py:311
  55.5 1.7 %collective-permute-start.9 = (f32[2,4,8,16,128]{4,3,2,1,0:T(8,128)S(1)}, f32[2,4,8,16,128]{4,3,2,1,0:T(8,128)S(1)}, u32[]{:S(2)}, u32[]{:S(2)}) collective-permute-start(f32[2,4,8,16,128]{4,3,2,1,0:T(8,128)S(1)} %slice.196), channel_id=1, source_target_pairs={{0,8},{1,3},{2,10},{3,1},{4,12},{5,7},{6,14},{7,5},{8,0},{9,11},{1... | collective-permute-start | bytes 1572872 | tf_op jit(solution)/shard_map/ppermute | solution.py:311
  57.2 7.6 %collective-permute-done.9 = f32[2,4,8,16,128]{4,3,2,1,0:T(8,128)S(1)} collective-permute-done((f32[2,4,8,16,128]{4,3,2,1,0:T(8,128)S(1)}, f32[2,4,8,16,128]{4,3,2,1,0:T(8,128)S(1)}, u32[]{:S(2)}, u32[]{:S(2)}) %collective-permute-start.9) | collective-permute-done | bytes 524320 | tf_op jit(solution)/shard_map/ppermute | solution.py:311
  64.8 3.1 %collective-permute-start.10 = (f32[1,4,8,16,128]{4,3,2,1,0:T(8,128)S(1)}, f32[1,4,8,16,128]{4,3,2,1,0:T(8,128)S(1)}, u32[]{:S(2)}, u32[]{:S(2)}) collective-permute-start(f32[1,4,8,16,128]{4,3,2,1,0:T(8,128)S(1)} %slice_add_fusion.8), channel_id=1, source_target_pairs={{0,24},{1,7},{2,26},{3,5},{4,28},{5,3},{6,30},{7,1},{8,16},{9,15},... | collective-permute-start | bytes 786440 | tf_op jit(solution)/shard_map/ppermute | solution.py:311
  67.9 4.6 %collective-permute-done.10 = f32[1,4,8,16,128]{4,3,2,1,0:T(8,128)S(1)} collective-permute-done((f32[1,4,8,16,128]{4,3,2,1,0:T(8,128)S(1)}, f32[1,4,8,16,128]{4,3,2,1,0:T(8,128)S(1)}, u32[]{:S(2)}, u32[]{:S(2)}) %collective-permute-start.10) | collective-permute-done | bytes 262176 | tf_op jit(solution)/shard_map/ppermute | solution.py:311
  72.6 2.0 %collective-permute-start.11 = (f32[4,4,16,128]{3,2,0,1:T(8,128)S(1)}, f32[4,4,16,128]{3,2,0,1:T(8,128)S(1)}, u32[]{:S(2)}, u32[]{:S(2)}) collective-permute-start(f32[4,4,16,128]{3,2,0,1:T(8,128)S(1)} %slice.200), channel_id=1, source_target_pairs={{0,32},{1,33},{2,34},{3,35},{4,36},{5,37},{6,38},{7,39},{8,40},{9,... | collective-permute-start | bytes 393224 | tf_op jit(solution)/shard_map/ppermute | solution.py:311
  74.6 3.1 %collective-permute-done.11 = f32[4,4,16,128]{3,2,0,1:T(8,128)S(1)} collective-permute-done((f32[4,4,16,128]{3,2,0,1:T(8,128)S(1)}, f32[4,4,16,128]{3,2,0,1:T(8,128)S(1)}, u32[]{:S(2)}, u32[]{:S(2)}) %collective-permute-start.11) | collective-permute-done | bytes 131104 | tf_op jit(solution)/shard_map/ppermute | solution.py:311
  77.7 4.0 %collective-permute-start.12 = (f32[2,4,16,128]{3,2,0,1:T(8,128)S(1)}, f32[2,4,16,128]{3,2,0,1:T(8,128)S(1)}, u32[]{:S(2)}, u32[]{:S(2)}) collective-permute-start(f32[2,4,16,128]{3,2,0,1:T(8,128)S(1)} %get-tuple-element.32), channel_id=1, source_target_pairs={{0,64},{1,65},{2,66},{3,67},{4,68},{5,69},{6,70},{7,71},{8,72},{9,... | collective-permute-start | bytes 196616 | tf_op jit(solution)/shard_map/ppermute | solution.py:311
  81.6 2.2 %collective-permute-done.12 = f32[2,4,16,128]{3,2,0,1:T(8,128)S(1)} collective-permute-done((f32[2,4,16,128]{3,2,0,1:T(8,128)S(1)}, f32[2,4,16,128]{3,2,0,1:T(8,128)S(1)}, u32[]{:S(2)}, u32[]{:S(2)}) %collective-permute-start.12) | collective-permute-done | bytes 65568 | tf_op jit(solution)/shard_map/ppermute | solution.py:311
  83.9 6.2 %collective-permute-start.13 = (f32[1,4,16,128]{3,2,0,1:T(8,128)S(1)}, f32[1,4,16,128]{3,2,0,1:T(8,128)S(1)}, u32[]{:S(2)}, u32[]{:S(2)}) collective-permute-start(f32[1,4,16,128]{3,2,0,1:T(8,128)S(1)} %slice_add_fusion.16), channel_id=1, source_target_pairs={{0,192},{1,193},{2,194},{3,195},{4,196},{5,197},{6,198},{7,199},{8... | collective-permute-start | bytes 98312 | tf_op jit(solution)/shard_map/ppermute | solution.py:311
  90.0 1.9 %collective-permute-done.13 = f32[1,4,16,128]{3,2,0,1:T(8,128)S(1)} collective-permute-done((f32[1,4,16,128]{3,2,0,1:T(8,128)S(1)}, f32[1,4,16,128]{3,2,0,1:T(8,128)S(1)}, u32[]{:S(2)}, u32[]{:S(2)}) %collective-permute-start.13) | collective-permute-done | bytes 32800 | tf_op jit(solution)/shard_map/ppermute | solution.py:311
  92.1 1.1 %collective-permute-done.14 = f32[2,8,128]{2,1,0:T(8,128)S(1)} collective-permute-done((f32[2,8,128]{2,1,0:T(8,128)S(1)}, f32[2,8,128]{2,1,0:T(8,128)S(1)}, u32[]{:S(2)}, u32[]{:S(2)}) %collective-permute-start.14) | collective-permute-done | bytes 8224 | tf_op jit(solution)/shard_map/ppermute | solution.py:311
  (55 shorter events, 3.0 us)
Async XLA Ops:
  0.1 0.9 copy-start.1
  1.0 0.7 copy-start.3
  1.7 0.7 copy-start.5
  2.3 0.7 copy-start.7
  3.0 0.7 copy-start.11
  3.7 0.7 copy-start.12
  4.3 0.7 copy-start.13
  5.0 3.1 %copy-start = (f32[1,64,16,512]{3,2,1,0:T(8,128)S(1)}, f32[1,64,16,512]{3,2,1,0:T(8,128)}, u32[]{:S(2)}) copy-start(f32[1,64,16,512]{3,2,1,0:T(8,128)} %pixels_ref.1) | copy-start | bytes 6291460
  5.0 3.1 %copy-start.2 = (f32[8,2,21]{2,1,0:T(2,128)S(1)}, f32[8,2,21]{2,1,0:T(2,128)}, u32[]{:S(2)}) copy-start(f32[8,2,21]{2,1,0:T(2,128)} %bank_ref.3) | copy-start | bytes 4036
  5.0 3.1 %copy-start.8 = (f32[1,3]{1,0:T(1,128)S(1)}, f32[1,3]{1,0:T(1,128)}, u32[]{:S(2)}) copy-start(f32[1,3]{1,0:T(1,128)} %coeff_ref.1) | copy-start | bytes 40
  5.0 3.1 %copy-start.9 = (s32[1,16]{1,0:T(1,128)S(1)}, s32[1,16]{1,0:T(1,128)}, u32[]{:S(2)}) copy-start(s32[1,16]{1,0:T(1,128)} %base_ref.1) | copy-start | bytes 196
  5.0 3.1 %copy-start.10 = (s32[1,3]{1,0:T(1,128)S(1)}, s32[1,3]{1,0:T(1,128)}, u32[]{:S(2)}) copy-start(s32[1,3]{1,0:T(1,128)} %index_ref.3) | copy-start | bytes 40
  7.9 4.4 %collective-permute-start = (f32[4,4,2,8,16,128]{5,4,3,2,1,0:T(8,128)S(1)}, f32[4,4,2,8,16,128]{5,4,3,2,1,0:T(8,128)S(1)}, u32[]{:S(2)}, u32[]{:S(2)}) collective-permute-start(f32[4,4,2,8,16,128]{5,4,3,2,1,0:T(8,128)S(1)} %get-tuple-element.15.after), channel_id=1, source_target_pairs={{0,1},{1,0},{2,3},{3,2},{4,5},{5,4},{6,7},{7,6},{8,9},{9,8},{10,11... | collective-permute-start | bytes 6291464 | tf_op jit(solution)/shard_map/ppermute | solution.py:311
  12.7 6.6 %copy-start.4 = (s32[1,512]{1,0:T(1,128)S(1)}, s32[1,512]{1,0:T(1,128)}, u32[]{:S(2)}) copy-start(s32[1,512]{1,0:T(1,128)} %col_base_ref.5) | copy-start | bytes 6148
  12.7 6.6 %copy-start.6 = (f32[1,512]{1,0:T(1,128)S(1)}, f32[1,512]{1,0:T(1,128)}, u32[]{:S(2)}) copy-start(f32[1,512]{1,0:T(1,128)} %col_frac_ref.5) | copy-start | bytes 6148
  12.7 6.6 %copy-start.14 = (f32[1,64]{1,0:T(1,128)S(1)}, f32[1,64]{1,0:T(1,128)}, u32[]{:S(2)}) copy-start(f32[1,64]{1,0:T(1,128)} %weight_ref.3) | copy-start | bytes 772
  26.4 2.8 %collective-permute-start.4 = (f32[4,4,8,16,128]{4,3,2,1,0:T(8,128)S(1)}, f32[4,4,8,16,128]{4,3,2,1,0:T(8,128)S(1)}, u32[]{:S(2)}, u32[]{:S(2)}) collective-permute-start(f32[4,4,8,16,128]{4,3,2,1,0:T(8,128)S(1)} %get-tuple-element.24), channel_id=1, source_target_pairs={{0,1},{1,0},{2,3},{3,2},{4,5},{5,4},{6,7},{7,6},{8,9},{9,8},{10,11... | collective-permute-start | bytes 3145736 | tf_op jit(solution)/shard_map/ppermute | solution.py:311
  26.9 4.7 %collective-permute-start.1 = (f32[4,4,8,16,128]{4,3,2,1,0:T(8,128)S(1)}, f32[4,4,8,16,128]{4,3,2,1,0:T(8,128)S(1)}, u32[]{:S(2)}, u32[]{:S(2)}) collective-permute-start(f32[4,4,8,16,128]{4,3,2,1,0:T(8,128)S(1)} %get-tuple-element.22.after), channel_id=1, source_target_pairs={{0,1},{1,0},{2,3},{3,2},{4,5},{5,4},{6,7},{7,6},{8,9},{9,8},{10,11... | collective-permute-start | bytes 3145736 | tf_op jit(solution)/shard_map/ppermute | solution.py:311
  27.0 14.8 %collective-permute-start.7 = (f32[2,4,2,8,16,128]{5,4,3,2,1,0:T(8,128)S(1)}, f32[2,4,2,8,16,128]{5,4,3,2,1,0:T(8,128)S(1)}, u32[]{:S(2)}, u32[]{:S(2)}) collective-permute-start(f32[2,4,2,8,16,128]{5,4,3,2,1,0:T(8,128)S(1)} %get-tuple-element.26.after), channel_id=1, source_target_pairs={{0,2},{1,9},{2,0},{3,11},{4,6},{5,13},{6,4},{7,15},{8,10},{9,1},{1... | collective-permute-start | bytes 3145736 | tf_op jit(solution)/shard_map/ppermute | solution.py:311
  29.4 14.8 %collective-permute-start.5 = (f32[2,4,8,16,128]{4,3,2,1,0:T(8,128)S(1)}, f32[2,4,8,16,128]{4,3,2,1,0:T(8,128)S(1)}, u32[]{:S(2)}, u32[]{:S(2)}) collective-permute-start(f32[2,4,8,16,128]{4,3,2,1,0:T(8,128)S(1)} %get-tuple-element.30), channel_id=1, source_target_pairs={{0,6},{1,25},{2,4},{3,27},{4,2},{5,29},{6,0},{7,31},{8,14},{9,17},... | collective-permute-start | bytes 1572872 | tf_op jit(solution)/shard_map/ppermute | solution.py:311
  31.8 15.6 %collective-permute-start.2 = (f32[2,4,8,16,128]{4,3,2,1,0:T(8,128)S(1)}, f32[2,4,8,16,128]{4,3,2,1,0:T(8,128)S(1)}, u32[]{:S(2)}, u32[]{:S(2)}) collective-permute-start(f32[2,4,8,16,128]{4,3,2,1,0:T(8,128)S(1)} %get-tuple-element.28), channel_id=1, source_target_pairs={{0,2},{1,9},{2,0},{3,11},{4,6},{5,13},{6,4},{7,15},{8,10},{9,1},{1... | collective-permute-start | bytes 1572872 | tf_op jit(solution)/shard_map/ppermute | solution.py:311
  41.9 10.5 %collective-permute-start.8 = (f32[1,4,2,8,16,128]{5,4,3,2,1,0:T(8,128)S(1)}, f32[1,4,2,8,16,128]{5,4,3,2,1,0:T(8,128)S(1)}, u32[]{:S(2)}, u32[]{:S(2)}) collective-permute-start(f32[1,4,2,8,16,128]{5,4,3,2,1,0:T(8,128)S(1)} %slice_add_fusion.2), channel_id=1, source_target_pairs={{0,6},{1,25},{2,4},{3,27},{4,2},{5,29},{6,0},{7,31},{8,14},{9,17},... | collective-permute-start | bytes 1572872 | tf_op jit(solution)/shard_map/ppermute | solution.py:311
  44.2 8.3 %collective-permute-start.6 = (f32[1,4,8,16,128]{4,3,2,1,0:T(8,128)S(1)}, f32[1,4,8,16,128]{4,3,2,1,0:T(8,128)S(1)}, u32[]{:S(2)}, u32[]{:S(2)}) collective-permute-start(f32[1,4,8,16,128]{4,3,2,1,0:T(8,128)S(1)} %slice_add_fusion.10), channel_id=1, source_target_pairs={{0,2},{1,9},{2,0},{3,11},{4,6},{5,13},{6,4},{7,15},{8,10},{9,1},{1... | collective-permute-start | bytes 786440 | tf_op jit(solution)/shard_map/ppermute | solution.py:311
  47.5 7.8 %collective-permute-start.3 = (f32[1,4,8,16,128]{4,3,2,1,0:T(8,128)S(1)}, f32[1,4,8,16,128]{4,3,2,1,0:T(8,128)S(1)}, u32[]{:S(2)}, u32[]{:S(2)}) collective-permute-start(f32[1,4,8,16,128]{4,3,2,1,0:T(8,128)S(1)} %slice_add_fusion.12), channel_id=1, source_target_pairs={{0,6},{1,25},{2,4},{3,27},{4,2},{5,29},{6,0},{7,31},{8,14},{9,17},... | collective-permute-start | bytes 786440 | tf_op jit(solution)/shard_map/ppermute | solution.py:311
  55.5 9.3 %collective-permute-start.9 = (f32[2,4,8,16,128]{4,3,2,1,0:T(8,128)S(1)}, f32[2,4,8,16,128]{4,3,2,1,0:T(8,128)S(1)}, u32[]{:S(2)}, u32[]{:S(2)}) collective-permute-start(f32[2,4,8,16,128]{4,3,2,1,0:T(8,128)S(1)} %slice.196), channel_id=1, source_target_pairs={{0,8},{1,3},{2,10},{3,1},{4,12},{5,7},{6,14},{7,5},{8,0},{9,11},{1... | collective-permute-start | bytes 1572872 | tf_op jit(solution)/shard_map/ppermute | solution.py:311
  64.8 7.7 %collective-permute-start.10 = (f32[1,4,8,16,128]{4,3,2,1,0:T(8,128)S(1)}, f32[1,4,8,16,128]{4,3,2,1,0:T(8,128)S(1)}, u32[]{:S(2)}, u32[]{:S(2)}) collective-permute-start(f32[1,4,8,16,128]{4,3,2,1,0:T(8,128)S(1)} %slice_add_fusion.8), channel_id=1, source_target_pairs={{0,24},{1,7},{2,26},{3,5},{4,28},{5,3},{6,30},{7,1},{8,16},{9,15},... | collective-permute-start | bytes 786440 | tf_op jit(solution)/shard_map/ppermute | solution.py:311
  72.6 5.1 %collective-permute-start.11 = (f32[4,4,16,128]{3,2,0,1:T(8,128)S(1)}, f32[4,4,16,128]{3,2,0,1:T(8,128)S(1)}, u32[]{:S(2)}, u32[]{:S(2)}) collective-permute-start(f32[4,4,16,128]{3,2,0,1:T(8,128)S(1)} %slice.200), channel_id=1, source_target_pairs={{0,32},{1,33},{2,34},{3,35},{4,36},{5,37},{6,38},{7,39},{8,40},{9,... | collective-permute-start | bytes 393224 | tf_op jit(solution)/shard_map/ppermute | solution.py:311
  77.7 6.2 %collective-permute-start.12 = (f32[2,4,16,128]{3,2,0,1:T(8,128)S(1)}, f32[2,4,16,128]{3,2,0,1:T(8,128)S(1)}, u32[]{:S(2)}, u32[]{:S(2)}) collective-permute-start(f32[2,4,16,128]{3,2,0,1:T(8,128)S(1)} %get-tuple-element.32), channel_id=1, source_target_pairs={{0,64},{1,65},{2,66},{3,67},{4,68},{5,69},{6,70},{7,71},{8,72},{9,... | collective-permute-start | bytes 196616 | tf_op jit(solution)/shard_map/ppermute | solution.py:311
  83.9 8.1 %collective-permute-start.13 = (f32[1,4,16,128]{3,2,0,1:T(8,128)S(1)}, f32[1,4,16,128]{3,2,0,1:T(8,128)S(1)}, u32[]{:S(2)}, u32[]{:S(2)}) collective-permute-start(f32[1,4,16,128]{3,2,0,1:T(8,128)S(1)} %slice_add_fusion.16), channel_id=1, source_target_pairs={{0,192},{1,193},{2,194},{3,195},{4,196},{5,197},{6,198},{7,199},{8... | collective-permute-start | bytes 98312 | tf_op jit(solution)/shard_map/ppermute | solution.py:311
  92.0 1.3 %collective-permute-start.14 = (f32[2,8,128]{2,1,0:T(8,128)S(1)}, f32[2,8,128]{2,1,0:T(8,128)S(1)}, u32[]{:S(2)}, u32[]{:S(2)}) collective-permute-start(f32[2,8,128]{2,1,0:T(8,128)S(1)} %fusion.12), channel_id=1, source_target_pairs={{0,1},{1,0},{2,3},{3,2},{4,5},{5,4},{6,7},{7,6},{8,9},{9,8},{10,11... | collective-permute-start | bytes 24584 | tf_op jit(solution)/shard_map/ppermute | solution.py:311

commit v3 on v2

v3 whole, which is shorter than its diff:
```python
import functools

import jax
import jax.numpy as jnp
from jax import lax
from jax.experimental import pallas as pl
from jax.experimental.pallas import tpu as pltpu
from jax.sharding import PartitionSpec as P

F32 = jnp.float32
BF16 = jnp.bfloat16
NX, NY, NZ = 4, 4, 8
SEGS = 64
ROWS = 16
WIDTH = 512
TAPS = 21
REACH = 10
NBASIS = 3
LANES = 128
BLOCKS = WIDTH // LANES
BLOCK_SEGS = 16
BLOCK_ROWS = BLOCK_SEGS * ROWS
OWNER = 4
OFFSET = OWNER + SEGS
INDEX = OFFSET + SEGS
ROW_BASE = INDEX + NBASIS
FRAC = SEGS
COEFF = FRAC + ROWS
BANK = COEFF + NBASIS


def split(value):
    high = value.astype(BF16)
    return high, (value - high.astype(F32)).astype(BF16)


def column_factor(bits):
    bad = (bits & 1).astype(F32)
    full = ((bits >> 1) & 1).astype(F32)
    cosmic = ((bits >> 2) & 1).astype(F32)
    return (1.0 - bad) * (1.0 - 0.75 * full) * (1.0 - 0.5 * cosmic)


def column_warp(base, frac):
    source = lax.broadcasted_iota(jnp.int32, (WIDTH, base.shape[1]), 0).astype(F32)
    return jnp.where(source == base, 1.0 - frac, 0.0) + jnp.where(source == base + 1, frac, 0.0)


def column_of(ref, start, shape):
    row = lax.broadcasted_iota(jnp.int32, shape, 0)
    result = jnp.full(shape, ref[start])
    for i in range(1, ROWS):
        result = jnp.where(row == i, ref[start + i], result)
    return result


A_FIRST = (0, 3, 1, 2)
B_FIRST = (0, 1, 3, 2)


def relative_patch(ints, owner):
    ry = (owner % NY) ^ ints[2]
    rz = (owner // NY) ^ ints[3]
    return ry, (rz & 1) * 4 + ((rz >> 1) ^ (rz >> 2)) % 2 * 2 + (rz >> 2)


def write_out(ints, sums, keep, send, sems, u_order, v_order):
    copies = []
    for to, core in ((keep, ints[0]), (send, 1 - ints[0])):
        for pu, ru in enumerate(u_order):
            for pv, rv in enumerate(v_order):
                rx = ru + core * (rv - ru)
                ry = rv + core * (ru - rv)
                rows = pl.ds(pl.multiple_of(((ints[1] ^ rx) * 2 + core) * 8, 8), 8)
                copies.append((sums.at[:, ry, :, rows, :], to.at[pu, pv]))
    started = [pltpu.make_async_copy(src, dst, sems.at[i]) for i, (src, dst) in enumerate(copies)]
    for copy in started:
        copy.start()
    for copy in started:
        copy.wait()


def denom_kernel(ints, floats, bits_ref, columns_ref, keep, send, sums, cover, sems):
    factor = column_factor(bits_ref[0]).astype(BF16)
    warp_high, warp_low = split(column_warp(columns_ref[0:1, :], columns_ref[1:2, :]))
    coverage = jnp.dot(factor, warp_high, preferred_element_type=F32) + jnp.dot(
        factor, warp_low, preferred_element_type=F32
    )
    for block in range(BLOCKS):
        cover[block] = coverage[:, block * LANES : (block + 1) * LANES]
    sums[...] = jnp.zeros(sums.shape, F32)
    frac = column_of(floats, FRAC, (ROWS, LANES))
    spread = (1.0 - frac) + frac

    def one(s, carry):
        ry, rz = relative_patch(ints, ints[OWNER + s])
        rows = pl.ds(ints[OFFSET + s], ROWS)
        share = spread * floats[s]
        for block in range(BLOCKS):
            sums[block, ry, rz, rows, :] += share * cover[block, pl.ds(s, 1), :]
        return carry

    lax.fori_loop(0, SEGS, one, 0, unroll=2)
    write_out(ints, sums, keep, send, sems, A_FIRST, A_FIRST)


def row_tables(ints, floats, k):
    shape = (ROWS, BLOCK_ROWS)
    delta = lax.broadcasted_iota(jnp.int32, shape, 1) % ROWS - column_of(ints, ROW_BASE, shape) + REACH
    frac = column_of(floats, FRAC, shape)
    term = ints[INDEX + k]
    lower = jnp.zeros(shape, F32)
    higher = jnp.zeros(shape, F32)
    for tap in range(TAPS):
        value = floats[BANK + (2 * term) * TAPS + tap]
        lower = jnp.where(delta == tap, value, lower)
        higher = jnp.where(delta == tap + 1, value, higher)
    return ((1.0 - frac) * lower + frac * higher) * floats[COEFF + k]


def band_tables(ints, floats, k):
    lane = lax.broadcasted_iota(jnp.int32, (LANES, WIDTH), 1)
    term = ints[INDEX + k]
    base = jnp.zeros((LANES, WIDTH), F32)
    for tap in range(TAPS):
        base = jnp.where(lane == LANES + REACH - tap, floats[BANK + (2 * term + 1) * TAPS + tap], base)
    return pltpu.roll(base, 0, 1, stride=1, stride_axis=0)[:, : 3 * LANES]


def rows_kernel(ints, floats, bits_ref, pixels_ref, after, u_high, u_low, blockdiag):
    same = (
        lax.broadcasted_iota(jnp.int32, (BLOCK_ROWS, BLOCK_ROWS), 0) // ROWS
        == lax.broadcasted_iota(jnp.int32, (BLOCK_ROWS, BLOCK_ROWS), 1) // ROWS
    )
    for k in range(NBASIS):
        table = row_tables(ints, floats, k)
        whole = jnp.where(same, jnp.concatenate([table] * BLOCK_SEGS, axis=0), 0.0)
        high, low = split(whole)
        rows = slice(k * BLOCK_ROWS, (k + 1) * BLOCK_ROWS)
        blockdiag[rows, 0:BLOCK_ROWS] = high
        blockdiag[rows, BLOCK_ROWS : 2 * BLOCK_ROWS] = high
        blockdiag[rows, 2 * BLOCK_ROWS :] = low

    def one(b, carry):
        segs = pl.ds(b * BLOCK_SEGS, BLOCK_SEGS)
        factor = column_factor(bits_ref[0, segs, :])
        masked = (pixels_ref[0, segs] * factor[:, None, :]).reshape(BLOCK_ROWS, WIDTH)
        high, low = split(masked)
        product = jnp.dot(
            blockdiag[...], jnp.concatenate([high, low, high], axis=0), preferred_element_type=F32
        )
        rows = pl.ds(pl.multiple_of(b * BLOCK_ROWS, BLOCK_ROWS), BLOCK_ROWS)
        for k in range(NBASIS):
            part_high, part_low = split(product[k * BLOCK_ROWS : (k + 1) * BLOCK_ROWS])
            u_high[rows, k * WIDTH : (k + 1) * WIDTH] = part_high
            u_low[rows, k * WIDTH : (k + 1) * WIDTH] = part_low
        return carry

    lax.fori_loop(0, SEGS // BLOCK_SEGS, one, 0)


def band_kernel(ints, floats, u_high, u_low, after, high_ref, low_ref, band_high, band_low):
    band_high[...] = jnp.zeros(band_high.shape, BF16)
    band_low[...] = jnp.zeros(band_low.shape, BF16)
    for k in range(NBASIS):
        high, low = split(band_tables(ints, floats, k))
        for block in range(BLOCKS):
            first = max(block - 1, 0)
            last = min(block + 1, BLOCKS - 1)
            rows = slice(k * WIDTH + block * LANES, k * WIDTH + (block + 1) * LANES)
            to = slice(first * LANES, (last + 1) * LANES)
            of = slice((first - block + 1) * LANES, (last - block + 2) * LANES)
            band_high[rows, to] = high[:, of]
            band_low[rows, to] = low[:, of]
    dot = functools.partial(jnp.dot, preferred_element_type=F32)

    def one(b, carry):
        rows = pl.ds(pl.multiple_of(b * BLOCK_ROWS, BLOCK_ROWS), BLOCK_ROWS)
        part_high = u_high[rows, :]
        part_low = u_low[rows, :]
        wide = dot(part_high, band_high[...]) + dot(part_high, band_low[...]) + dot(part_low, band_high[...])
        high, low = split(wide)
        high_ref[rows, :] = high
        low_ref[rows, :] = low
        return carry

    lax.fori_loop(0, SEGS * ROWS // BLOCK_ROWS, one, 0)


def place_kernel(
    chunk, ints, floats, columns_ref, high_ref, low_ref, after, keep, send, sums, lifted, sems
):
    cols = slice(2 * chunk * LANES, 2 * (chunk + 1) * LANES)
    warp_high, warp_low = split(column_warp(columns_ref[0:1, cols], columns_ref[1:2, cols]))
    dot = functools.partial(jnp.dot, preferred_element_type=F32)
    high = high_ref[...]
    warped = dot(high, warp_high) + dot(high, warp_low) + dot(low_ref[...], warp_high)
    for half in range(2):
        lifted[half] = warped[:, half * LANES : (half + 1) * LANES]
    sums[...] = jnp.zeros(sums.shape, F32)

    def one(s, carry):
        ry, rz = relative_patch(ints, ints[OWNER + s])
        rows = pl.ds(ints[OFFSET + s], ROWS)
        weight = floats[s]
        of = pl.ds(pl.multiple_of(s * ROWS, ROWS), ROWS)
        for half in range(2):
            sums[half, ry, rz, rows, :] += weight * lifted[half, of, :]
        return carry

    lax.fori_loop(0, SEGS, one, 0, unroll=2)
    order = (A_FIRST, B_FIRST)[chunk]
    write_out(ints, sums, keep, send, sems, order, B_FIRST)


SMEM = pl.BlockSpec(memory_space=pltpu.SMEM)
VMEM = pl.BlockSpec(memory_space=pltpu.VMEM)
ANY = pl.BlockSpec(memory_space=pl.ANY)
PARAMS = pltpu.CompilerParams(vmem_limit_bytes=40 * 1024 * 1024)


def denom_sums(ints, floats, bits, columns):
    parts = jax.ShapeDtypeStruct((4, 4, BLOCKS, NZ, 8, LANES), F32)
    return pl.pallas_call(
        denom_kernel,
        out_shape=(parts, parts),
        in_specs=[SMEM] * 2 + [VMEM] * 2,
        out_specs=(ANY,) * 2,
        scratch_shapes=[
            pltpu.VMEM((BLOCKS, NY, NZ, 64, LANES), F32), pltpu.VMEM((BLOCKS, SEGS, LANES), F32),
            pltpu.SemaphoreType.DMA((32,)),
        ],
        compiler_params=PARAMS,
        cost_estimate=pl.CostEstimate(flops=10**3, bytes_accessed=10**3, transcendentals=0),
        name="denom_sums",
    )(ints, floats, bits, columns)


def row_pass(ints, floats, bits, pixels, after):
    wide = jax.ShapeDtypeStruct((SEGS * ROWS, NBASIS * WIDTH), BF16)
    return pl.pallas_call(
        rows_kernel,
        out_shape=(wide, wide),
        in_specs=[SMEM] * 2 + [VMEM] * 2 + [ANY],
        out_specs=(VMEM, VMEM),
        scratch_shapes=[
            pltpu.VMEM((NBASIS * BLOCK_ROWS, 3 * BLOCK_ROWS), BF16),
        ],
        compiler_params=PARAMS,
        cost_estimate=pl.CostEstimate(flops=10**3, bytes_accessed=10**3, transcendentals=0),
        name="row_pass",
    )(ints, floats, bits, pixels, after)


def band_pass(ints, floats, u_high, u_low, after):
    wide = jax.ShapeDtypeStruct((SEGS * ROWS, WIDTH), BF16)
    band = pltpu.VMEM((NBASIS * WIDTH, WIDTH), BF16)
    return pl.pallas_call(
        band_kernel,
        out_shape=(wide, wide),
        in_specs=[SMEM] * 2 + [VMEM] * 2 + [ANY],
        out_specs=(VMEM, VMEM),
        scratch_shapes=[band, band],
        compiler_params=PARAMS,
        cost_estimate=pl.CostEstimate(flops=10**3, bytes_accessed=10**3, transcendentals=0),
        name="band_pass",
    )(ints, floats, u_high, u_low, after)


def numer_sums(chunk, ints, floats, columns, high, low, after):
    parts = jax.ShapeDtypeStruct((4, 4, 2, NZ, 8, LANES), F32)
    return pl.pallas_call(
        functools.partial(place_kernel, chunk),
        out_shape=(parts, parts),
        in_specs=[SMEM] * 2 + [VMEM] * 3 + [ANY],
        out_specs=(ANY,) * 2,
        scratch_shapes=[
            pltpu.VMEM((2, NY, NZ, 64, LANES), F32), pltpu.VMEM((2, SEGS * ROWS, LANES), F32),
            pltpu.SemaphoreType.DMA((32,)),
        ],
        compiler_params=PARAMS,
        cost_estimate=pl.CostEstimate(flops=10**3, bytes_accessed=10**3, transcendentals=0),
        name=f"numer_sums_{chunk}",
    )(ints, floats, columns, high, low, after)


def permute(value, partner):
    pairs = []
    for z in range(NZ):
        for y in range(NY):
            for x in range(NX):
                for core in range(2):
                    to_core, to_x, to_y, to_z = partner(core, x, y, z)
                    source = (z * NY + y) * 2 * NX + x * 2 + core
                    pairs.append((source, (to_z * NY + to_y) * 2 * NX + to_x * 2 + to_core))
    return lax.ppermute(value, ("sky", "grp"), pairs)


def swap_core(value):
    return permute(value, lambda core, x, y, z: (1 - core, x, y, z))


def swap_u(value, step):
    return permute(value, lambda core, x, y, z: (core, x, y ^ step, z) if core else (core, x ^ step, y, z))


def swap_v(value, step):
    return permute(value, lambda core, x, y, z: (core, x ^ step, y, z) if core else (core, x, y ^ step, z))


def swap_z(value, step):
    return permute(value, lambda core, x, y, z: (core, x, y, z ^ step))


def halve(keep, got):
    middle = keep.shape[0] // 2
    return keep[:middle] + got[:middle], keep[middle:] + got[middle:]


def hold(values, after):
    def kernel(*refs):
        pass

    return pl.pallas_call(
        kernel,
        out_shape=tuple(jax.ShapeDtypeStruct(value.shape, value.dtype) for value in values),
        in_specs=[ANY] * (len(values) + 1),
        out_specs=(ANY,) * len(values),
        input_output_aliases={i: i for i in range(len(values))},
        name="hold",
    )(*values, after)


def per_device(
    pixels, mask_bits, owner, row_offset, seg_weight, psf_bank, basis_index, basis_coeff,
    row_base, row_frac, col_base, col_frac,
):
    sky = lax.axis_index("sky").astype(jnp.int32)
    grp = lax.axis_index("grp").astype(jnp.int32)
    place = jnp.stack([grp % 2, grp // 2, sky % NY, sky // NY])
    ints = jnp.concatenate([place, owner[0], row_offset[0], basis_index[0], row_base[0]])
    floats = jnp.concatenate([seg_weight[0], row_frac[0], basis_coeff[0], psf_bank.reshape(-1)])
    columns = jnp.concatenate([col_base.astype(F32), col_frac])
    d_keep, d_send = denom_sums(ints, floats, mask_bits, columns)
    u_high, u_low = row_pass(ints, floats, mask_bits, pixels, d_send)
    (d_got,) = hold((swap_core(d_send),), u_high)
    d_keep, d_send = halve(d_keep, d_got)
    high, low = band_pass(ints, floats, u_high, u_low, d_send)
    d_got = swap_u(d_send, 1)
    first = numer_sums(0, ints, floats, columns, high, low, high)
    second = numer_sums(1, ints, floats, columns, high, low, first[1])
    d_keep, d_send = halve(d_keep, d_got)
    n_sends = hold((first[1], second[1]), d_send)
    n_got = [swap_core(send) for send in n_sends]
    d_got = swap_u(d_send, 3)
    n_parts = [halve(keep, got) for (keep, _), got in zip((first, second), n_got)]
    n_parts = [halve(keep, swap_u(send, step)) for (keep, send), step in zip(n_parts, (1, 3))]
    d_part = (d_keep + d_got)[0]
    d_keep, d_send = halve(d_part[:2], swap_v(d_part[2:], 1))
    n_parts = [keep[0] + swap_u(send, step)[0] for (keep, send), step in zip(n_parts, (3, 1))]
    n_part = jnp.concatenate(n_parts, axis=1)
    n_keep, n_send = halve(n_part[:2], swap_v(n_part[2:], 3))
    d_part = (d_keep + swap_v(d_send, 3))[0]
    n_part = (n_keep + swap_v(n_send, 1))[0]
    both = jnp.swapaxes(jnp.concatenate([n_part, d_part]), 0, 1)
    keep, send = halve(both[:4], swap_z(both[4:], 1))
    keep, send = halve(keep, swap_z(send, 2))
    both = (keep + swap_z(send, 6))[0]
    coadd = both[:BLOCKS] / jnp.maximum(both[BLOCKS:], 1.0)
    return jnp.swapaxes(coadd, 0, 1).reshape(8, WIDTH)


def solution(mesh):
    placed = (
        P("grp", "sky", None, None),
        P("grp", "sky", None),
        P("grp", "sky"),
        P("grp", "sky"),
        P("grp", "sky"),
        P(),
        P("grp", None),
        P("grp", None),
        P("grp", None),
        P("grp", None),
        P("grp", None),
        P("grp", None),
    )
    return jax.shard_map(
        per_device, mesh=mesh, in_specs=placed, out_specs=P(("sky", "grp"), None), check_vma=False
    )
```

time: 95.5 us -> 95.4 us (level); the launches traced: 93.8 us -> 95.1 us
  waiting for transfers between devices: 40.1 us -> 32.5 us
  other arithmetic: 1.85 us -> 7.33 us
  local copies, waits for them, and re-layouts: 4.97 us -> 8.32 us
    ppermute x15 -> x16, waiting for transfers between devices: 40.1 us -> 32.5 us  [permute(): return lax.ppermute(value, ('sky', 'grp'), pairs)]
    add x9 -> x10, other arithmetic: 0.77 us -> 4.28 us  [halve(): return (keep[:middle] + got[:middle], keep[middle:] + got[middle:])]
    unnamed x30 -> x24, local copies, waits for them, and re-layouts: 4.93 us -> 6.73 us
    concatenate x1 -> x3, other arithmetic: 0.09 us -> 1.47 us  [the longest x1 0.76 us: per_device(): jnp.concatenate([seg_weight[0], row_frac[0], basis_coeff[0], psf_bank.res...]
    pallas_call x2 -> x4, Pallas kernels: 7.2 us -> 7.55 us  [the longest x1 4.14 us: row_pass(): pl.pallas_call(rows_kernel, out_shape=(wide, wide), in_specs=[SMEM] * 2 +...]
    ppermute x15 -> x16, starting transfers between devices: 25.8 us -> 25.6 us  [permute(): return lax.ppermute(value, ('sky', 'grp'), pairs)]
  transfers between devices with their start and end apart: 15 -> 16, of which waited for: 11 -> 13; matrix products, arithmetic and copies ran while one was open for 1% -> 1% of each run, Pallas kernels for 5% -> 19%
where the time goes in v3:
time: 95.4 us; the launch traced here: 95.1 us
  waiting for transfers between devices  32.5 us (34%)
  starting transfers between devices  25.6 us (27%)
  Pallas kernels  21.1 us (22%)
  local copies, waits for them, and re-layouts  8.32 us (9%)
  other arithmetic  7.33 us (8%)
    ppermute x16, waiting for transfers between devices, permute(): return lax.ppermute(value, ('sky', 'grp'), pairs)  32.5 us
    ppermute x16, starting transfers between devices, permute(): return lax.ppermute(value, ('sky', 'grp'), pairs)  25.6 us
    pallas_call x2, Pallas kernels, numer_sums(): pl.pallas_call(functools.partial(place_kernel, chunk), out_shape=(parts,...  7.09 us
    unnamed x24, local copies, waits for them, and re-layouts  6.73 us
    pallas_call x1, Pallas kernels, band_pass(): pl.pallas_call(band_kernel, out_shape=(wide, wide), in_specs=[SMEM] * 2 +...  6.41 us
    add x10, other arithmetic, halve(): return (keep[:middle] + got[:middle], keep[middle:] + got[middle:])  4.28 us
    pallas_call x1, Pallas kernels, row_pass(): pl.pallas_call(rows_kernel, out_shape=(wide, wide), in_specs=[SMEM] * 2 +...  4.14 us
    pallas_call x1, Pallas kernels, denom_sums(): pl.pallas_call(denom_kernel, out_shape=(parts, parts), in_specs=[SMEM] *...  3.41 us
  transfers between devices with their start and end apart: 16, of which 13 were waited for; matrix products, arithmetic and copies ran while one was open for 1% of the time, Pallas kernels for 19%

profile of v3, /device:TPU:6, one launch (start us, length us, event | category | flops | bytes accessed | tf_op | source)
XLA Modules:
  0.0 95.1 jit_solution(5769797740494554245)
XLA Ops:
  4.6 3.4 %denom_sums.1 = (f32[4,4,4,8,8,128]{5,4,3,2,1,0:T(8,128)S(1)}, f32[4,4,4,8,8,128]{5,4,3,2,1,0:T(8,128)S(1)}) custom-call(s32[151]{0:T(256)S(1)} %concatenate.15.ints, f32[419]{0:T(512)S(1)} %pad_maximum_fusion.2.floats, s32[1,64,512]{2,1,0:T(8,128)S(1)} %copy-done.6, f32[2,512]{1,0:T(2,128)S(1)} %pad_maximum_fusion.1.columns_ref), custom_call_target="tpu_custom_call" | custom-call | flops 1000 | bytes 1000 | tf_op jit(solution)/shard_map/denom_sums/pallas_call | solution.py:224
  8.0 1.3 %copy-done.3 = f32[4,4,4,8,8,128]{5,4,3,2,1,0:T(8,128)} copy-done((f32[4,4,4,8,8,128]{5,4,3,2,1,0:T(8,128)}, f32[4,4,4,8,8,128]{5,4,3,2,1,0:T(8,128)S(1)}, u32[]{:S(2)}) %copy-start.3) | copy-done | bytes 2097176
  9.4 1.6 %copy-done.4 = f32[1,64,16,512]{3,2,1,0:T(8,128)S(1)} copy-done((f32[1,64,16,512]{3,2,1,0:T(8,128)S(1)}, f32[1,64,16,512]{3,2,1,0:T(8,128)}, u32[]{:S(2)}) %copy-start.4) | copy-done | bytes 2097176
  11.0 4.1 %row_pass.1 = (bf16[1024,1536]{1,0:T(8,128)(2,1)S(1)}, bf16[1024,1536]{1,0:T(8,128)(2,1)S(1)}) custom-call(s32[151]{0:T(256)S(1)} %concatenate.15.ints, f32[419]{0:T(512)S(1)} %pad_maximum_fusion.2.floats, s32[1,64,512]{2,1,0:T(8,128)S(1)} %copy-done.6, f32[1,64,16,512]{3,2,1,0:T(8,128)S(1)} %copy-done.4, f32[4,4,4,8,8,128]{5,4,3,2,1,0:T(8,128)S(1)} %get-tuple-element.17.after), custom_call_target="tpu_custom_call" | custom-call | flops 1000 | bytes 1000 | tf_op jit(solution)/shard_map/row_pass/pallas_call | solution.py:241
  15.1 1.6 %copy-done = bf16[1024,1536]{1,0:T(8,128)(2,1)} copy-done((bf16[1024,1536]{1,0:T(8,128)(2,1)}, bf16[1024,1536]{1,0:T(8,128)(2,1)S(1)}, u32[]{:S(2)}) %copy-start) | copy-done | bytes 3145752
  16.8 2.9 %slice_add_fusion = (f32[2,4,4,8,8,128]{5,4,3,2,1,0:T(8,128)S(1)}, f32[2,4,4,8,8,128]{5,4,3,2,1,0:T(8,128)S(1)}) fusion(f32[4,4,4,8,8,128]{5,4,3,2,1,0:T(8,128)} %hold.2, f32[4,4,4,8,8,128]{5,4,3,2,1,0:T(8,128)} %copy-done.3), kind=kLoop, calls=%fused_computation | loop fusion | flops 524288 | bytes 6291456 | tf_op jit(solution)/shard_map/add | solution.py:317
  19.7 0.9 collective-permute-start.1
  20.6 6.4 %band_pass.1 = (bf16[1024,512]{1,0:T(8,128)(2,1)S(1)}, bf16[1024,512]{1,0:T(8,128)(2,1)S(1)}) custom-call(s32[151]{0:T(256)S(1)} %concatenate.15.ints, f32[419]{0:T(512)S(1)} %pad_maximum_fusion.2.floats, bf16[1024,1536]{1,0:T(8,128)(2,1)S(1)} %copy-done.1, bf16[1024,1536]{1,0:T(8,128)(2,1)S(1)} %get-tuple-element.19.u_low, ...), custom_call_target="tpu_custom_call" | custom-call | flops 1000 | bytes 1000 | tf_op jit(solution)/shard_map/band_pass/pallas_call | solution.py:258
  27.0 3.5 %numer_sums_0.1 = (f32[4,4,2,8,8,128]{5,4,3,2,1,0:T(8,128)S(1)}, f32[4,4,2,8,8,128]{5,4,3,2,1,0:T(8,128)S(1)}) custom-call(s32[151]{0:T(256)S(1)} %concatenate.15.ints, f32[419]{0:T(512)S(1)} %pad_maximum_fusion.2.floats, f32[2,512]{1,0:T(2,128)S(1)} %pad_maximum_fusion.1.columns_ref, bf16[1024,512]{1,0:T(8,128)(2,1)S(1)} %get-tuple-element.21.high_ref.after, ...), custom_call_target="tpu_custom_call" | custom-call | flops 1000 | bytes 1000 | tf_op jit(solution)/shard_map/numer_sums_0/pallas_call | solution.py:272
  30.6 3.5 %numer_sums_1.1 = (f32[4,4,2,8,8,128]{5,4,3,2,1,0:T(8,128)S(1)}, f32[4,4,2,8,8,128]{5,4,3,2,1,0:T(8,128)S(1)}) custom-call(s32[151]{0:T(256)S(1)} %concatenate.15.ints, f32[419]{0:T(512)S(1)} %pad_maximum_fusion.2.floats, f32[2,512]{1,0:T(2,128)S(1)} %pad_maximum_fusion.1.columns_ref, bf16[1024,512]{1,0:T(8,128)(2,1)S(1)} %get-tuple-element.21.high_ref.after, ...), custom_call_target="tpu_custom_call" | custom-call | flops 1000 | bytes 1000 | tf_op jit(solution)/shard_map/numer_sums_1/pallas_call | solution.py:272
  34.1 1.0 %copy-done.5 = f32[4,4,2,8,8,128]{5,4,3,2,1,0:T(8,128)} copy-done((f32[4,4,2,8,8,128]{5,4,3,2,1,0:T(8,128)}, f32[4,4,2,8,8,128]{5,4,3,2,1,0:T(8,128)S(1)}, u32[]{:S(2)}) %copy-start.5) | copy-done | bytes 1048600
  35.1 0.9 slice_add_fusion.7.refs_2_
  36.3 1.0 %collective-permute-start.2 = (f32[4,4,2,8,8,128]{5,4,3,2,1,0:T(8,128)}, f32[4,4,2,8,8,128]{5,4,3,2,1,0:T(8,128)S(1)}, u32[]{:S(2)}, u32[]{:S(2)}) collective-permute-start(f32[4,4,2,8,8,128]{5,4,3,2,1,0:T(8,128)} %get-tuple-element.26), channel_id=1, source_target_pairs={{0,1},{1,0},{2,3},{3,2},{4,5},{5,4},{6,7},{7,6},{8,9},{9,8},{10,11... | collective-permute-start | bytes 3145736 | tf_op jit(solution)/shard_map/ppermute | solution.py:296
  37.3 1.6 %collective-permute-start.10 = (f32[1,4,4,8,8,128]{5,4,3,2,1,0:T(8,128)S(1)}, f32[1,4,4,8,8,128]{5,4,3,2,1,0:T(8,128)S(1)}, u32[]{:S(2)}, u32[]{:S(2)}) collective-permute-start(f32[1,4,4,8,8,128]{5,4,3,2,1,0:T(8,128)S(1)} %copy-done.9), channel_id=1, source_target_pairs={{0,6},{1,25},{2,4},{3,27},{4,2},{5,29},{6,0},{7,31},{8,14},{9,17},... | collective-permute-start | bytes 1572872 | tf_op jit(solution)/shard_map/ppermute | solution.py:296
  41.4 1.7 %collective-permute-start.6 = (f32[2,4,2,8,8,128]{5,4,3,2,1,0:T(8,128)S(1)}, f32[2,4,2,8,8,128]{5,4,3,2,1,0:T(8,128)S(1)}, u32[]{:S(2)}, u32[]{:S(2)}) collective-permute-start(f32[2,4,2,8,8,128]{5,4,3,2,1,0:T(8,128)S(1)} %get-tuple-element.32), channel_id=1, source_target_pairs={{0,6},{1,25},{2,4},{3,27},{4,2},{5,29},{6,0},{7,31},{8,14},{9,17},... | collective-permute-start | bytes 1572872 | tf_op jit(solution)/shard_map/ppermute | solution.py:296
  43.1 4.6 %collective-permute-done.10 = f32[1,4,4,8,8,128]{5,4,3,2,1,0:T(8,128)S(1)} collective-permute-done((f32[1,4,4,8,8,128]{5,4,3,2,1,0:T(8,128)S(1)}, f32[1,4,4,8,8,128]{5,4,3,2,1,0:T(8,128)S(1)}, u32[]{:S(2)}, u32[]{:S(2)}) %collective-permute-start.10) | collective-permute-done | bytes 524320 | tf_op jit(solution)/shard_map/ppermute | solution.py:296
  47.8 1.4 %collective-permute-done.3 = f32[2,4,2,8,8,128]{5,4,3,2,1,0:T(8,128)S(1)} collective-permute-done((f32[2,4,2,8,8,128]{5,4,3,2,1,0:T(8,128)S(1)}, f32[2,4,2,8,8,128]{5,4,3,2,1,0:T(8,128)S(1)}, u32[]{:S(2)}, u32[]{:S(2)}) %collective-permute-start.3) | collective-permute-done | bytes 524320 | tf_op jit(solution)/shard_map/ppermute | solution.py:296
  49.2 1.4 %collective-permute-start.4 = (f32[1,4,2,8,8,128]{5,4,3,2,1,0:T(8,128)S(1)}, f32[1,4,2,8,8,128]{5,4,3,2,1,0:T(8,128)S(1)}, u32[]{:S(2)}, u32[]{:S(2)}) collective-permute-start(f32[1,4,2,8,8,128]{5,4,3,2,1,0:T(8,128)S(1)} %slice_add_fusion.10), channel_id=1, source_target_pairs={{0,6},{1,25},{2,4},{3,27},{4,2},{5,29},{6,0},{7,31},{8,14},{9,17},... | collective-permute-start | bytes 786440 | tf_op jit(solution)/shard_map/ppermute | solution.py:296
  50.6 2.7 %collective-permute-done.6 = f32[2,4,2,8,8,128]{5,4,3,2,1,0:T(8,128)S(1)} collective-permute-done((f32[2,4,2,8,8,128]{5,4,3,2,1,0:T(8,128)S(1)}, f32[2,4,2,8,8,128]{5,4,3,2,1,0:T(8,128)S(1)}, u32[]{:S(2)}, u32[]{:S(2)}) %collective-permute-start.6) | collective-permute-done | bytes 524320 | tf_op jit(solution)/shard_map/ppermute | solution.py:296
  53.5 1.7 %collective-permute-start.11 = (f32[2,4,8,8,128]{4,3,2,1,0:T(8,128)S(1)}, f32[2,4,8,8,128]{4,3,2,1,0:T(8,128)S(1)}, u32[]{:S(2)}, u32[]{:S(2)}) collective-permute-start(f32[2,4,8,8,128]{4,3,2,1,0:T(8,128)S(1)} %slice_bitcast_fusion), channel_id=1, source_target_pairs={{0,8},{1,3},{2,10},{3,1},{4,12},{5,7},{6,14},{7,5},{8,0},{9,11},{1... | collective-permute-start | bytes 786440 | tf_op jit(solution)/shard_map/ppermute | solution.py:296
  55.1 2.0 %collective-permute-done.4 = f32[1,4,2,8,8,128]{5,4,3,2,1,0:T(8,128)S(1)} collective-permute-done((f32[1,4,2,8,8,128]{5,4,3,2,1,0:T(8,128)S(1)}, f32[1,4,2,8,8,128]{5,4,3,2,1,0:T(8,128)S(1)}, u32[]{:S(2)}, u32[]{:S(2)}) %collective-permute-start.4) | collective-permute-done | bytes 262176 | tf_op jit(solution)/shard_map/ppermute | solution.py:296
  57.1 4.7 %collective-permute-done.7 = f32[1,4,2,8,8,128]{5,4,3,2,1,0:T(8,128)S(1)} collective-permute-done((f32[1,4,2,8,8,128]{5,4,3,2,1,0:T(8,128)S(1)}, f32[1,4,2,8,8,128]{5,4,3,2,1,0:T(8,128)S(1)}, u32[]{:S(2)}, u32[]{:S(2)}) %collective-permute-start.7) | collective-permute-done | bytes 262176 | tf_op jit(solution)/shard_map/ppermute | solution.py:296
  62.0 2.3 %collective-permute-start.8 = (f32[2,4,8,8,128]{4,3,2,1,0:T(8,128)S(1)}, f32[2,4,8,8,128]{4,3,2,1,0:T(8,128)S(1)}, u32[]{:S(2)}, u32[]{:S(2)}) collective-permute-start(f32[2,4,8,8,128]{4,3,2,1,0:T(8,128)S(1)} %fusion.1), channel_id=1, source_target_pairs={{0,24},{1,7},{2,26},{3,5},{4,28},{5,3},{6,30},{7,1},{8,16},{9,15},... | collective-permute-start | bytes 786440 | tf_op jit(solution)/shard_map/ppermute | solution.py:296
  64.3 1.1 %collective-permute-start.12 = (f32[1,4,8,8,128]{4,3,2,1,0:T(8,128)S(1)}, f32[1,4,8,8,128]{4,3,2,1,0:T(8,128)S(1)}, u32[]{:S(2)}, u32[]{:S(2)}) collective-permute-start(f32[1,4,8,8,128]{4,3,2,1,0:T(8,128)S(1)} %slice_add_fusion.12), channel_id=1, source_target_pairs={{0,24},{1,7},{2,26},{3,5},{4,28},{5,3},{6,30},{7,1},{8,16},{9,15},... | collective-permute-start | bytes 393224 | tf_op jit(solution)/shard_map/ppermute | solution.py:296
  65.4 4.2 %collective-permute-done.8 = f32[2,4,8,8,128]{4,3,2,1,0:T(8,128)S(1)} collective-permute-done((f32[2,4,8,8,128]{4,3,2,1,0:T(8,128)S(1)}, f32[2,4,8,8,128]{4,3,2,1,0:T(8,128)S(1)}, u32[]{:S(2)}, u32[]{:S(2)}) %collective-permute-start.8) | collective-permute-done | bytes 262176 | tf_op jit(solution)/shard_map/ppermute | solution.py:296
  71.1 3.6 %collective-permute-done.9 = f32[1,4,8,8,128]{4,3,2,1,0:T(8,128)S(1)} collective-permute-done((f32[1,4,8,8,128]{4,3,2,1,0:T(8,128)S(1)}, f32[1,4,8,8,128]{4,3,2,1,0:T(8,128)S(1)}, u32[]{:S(2)}, u32[]{:S(2)}) %collective-permute-start.9) | collective-permute-done | bytes 131104 | tf_op jit(solution)/shard_map/ppermute | solution.py:296
  74.8 2.0 %collective-permute-start.13 = (f32[4,8,8,128]{3,2,0,1:T(8,128)S(1)}, f32[4,8,8,128]{3,2,0,1:T(8,128)S(1)}, u32[]{:S(2)}, u32[]{:S(2)}) collective-permute-start(f32[4,8,8,128]{3,2,0,1:T(8,128)S(1)} %slice.232), channel_id=1, source_target_pairs={{0,32},{1,33},{2,34},{3,35},{4,36},{5,37},{6,38},{7,39},{8,40},{9,... | collective-permute-start | bytes 393224 | tf_op jit(solution)/shard_map/ppermute | solution.py:296
  76.8 3.1 %collective-permute-done.13 = f32[4,8,8,128]{3,2,0,1:T(8,128)S(1)} collective-permute-done((f32[4,8,8,128]{3,2,0,1:T(8,128)S(1)}, f32[4,8,8,128]{3,2,0,1:T(8,128)S(1)}, u32[]{:S(2)}, u32[]{:S(2)}) %collective-permute-start.13) | collective-permute-done | bytes 131104 | tf_op jit(solution)/shard_map/ppermute | solution.py:296
  79.9 4.1 %collective-permute-start.14 = (f32[2,8,8,128]{3,2,0,1:T(8,128)S(1)}, f32[2,8,8,128]{3,2,0,1:T(8,128)S(1)}, u32[]{:S(2)}, u32[]{:S(2)}) collective-permute-start(f32[2,8,8,128]{3,2,0,1:T(8,128)S(1)} %get-tuple-element.36), channel_id=1, source_target_pairs={{0,64},{1,65},{2,66},{3,67},{4,68},{5,69},{6,70},{7,71},{8,72},{9,... | collective-permute-start | bytes 196616 | tf_op jit(solution)/shard_map/ppermute | solution.py:296
  83.9 2.2 %collective-permute-done.14 = f32[2,8,8,128]{3,2,0,1:T(8,128)S(1)} collective-permute-done((f32[2,8,8,128]{3,2,0,1:T(8,128)S(1)}, f32[2,8,8,128]{3,2,0,1:T(8,128)S(1)}, u32[]{:S(2)}, u32[]{:S(2)}) %collective-permute-start.14) | collective-permute-done | bytes 65568 | tf_op jit(solution)/shard_map/ppermute | solution.py:296
  86.2 6.3 %collective-permute-start.15 = (f32[1,8,8,128]{3,2,0,1:T(8,128)S(1)}, f32[1,8,8,128]{3,2,0,1:T(8,128)S(1)}, u32[]{:S(2)}, u32[]{:S(2)}) collective-permute-start(f32[1,8,8,128]{3,2,0,1:T(8,128)S(1)} %slice_add_fusion.18), channel_id=1, source_target_pairs={{0,192},{1,193},{2,194},{3,195},{4,196},{5,197},{6,198},{7,199},{8... | collective-permute-start | bytes 98312 | tf_op jit(solution)/shard_map/ppermute | solution.py:296
  92.5 2.0 %collective-permute-done.15 = f32[1,8,8,128]{3,2,0,1:T(8,128)S(1)} collective-permute-done((f32[1,8,8,128]{3,2,0,1:T(8,128)S(1)}, f32[1,8,8,128]{3,2,0,1:T(8,128)S(1)}, u32[]{:S(2)}, u32[]{:S(2)}) %collective-permute-start.15) | collective-permute-done | bytes 32800 | tf_op jit(solution)/shard_map/ppermute | solution.py:296
  (57 shorter events, 9.9 us)
Async XLA Ops:
  3.7 0.9 copy-start.6
  8.0 1.3 %copy-start.3 = (f32[4,4,4,8,8,128]{5,4,3,2,1,0:T(8,128)}, f32[4,4,4,8,8,128]{5,4,3,2,1,0:T(8,128)S(1)}, u32[]{:S(2)}) copy-start(f32[4,4,4,8,8,128]{5,4,3,2,1,0:T(8,128)S(1)} %get-tuple-element.20) | copy-start | bytes 6291460
  9.4 7.4 %collective-permute-start = (f32[4,4,4,8,8,128]{5,4,3,2,1,0:T(8,128)S(1)}, f32[4,4,4,8,8,128]{5,4,3,2,1,0:T(8,128)}, u32[]{:S(2)}, u32[]{:S(2)}) collective-permute-start(f32[4,4,4,8,8,128]{5,4,3,2,1,0:T(8,128)S(1)} %get-tuple-element.17.after), channel_id=1, source_target_pairs={{0,1},{1,0},{2,3},{3,2},{4,5},{5,4},{6,7},{7,6},{8,9},{9,8},{10,11... | collective-permute-start | bytes 6291464 | tf_op jit(solution)/shard_map/ppermute | solution.py:296
  9.4 1.6 %copy-start.4 = (f32[1,64,16,512]{3,2,1,0:T(8,128)S(1)}, f32[1,64,16,512]{3,2,1,0:T(8,128)}, u32[]{:S(2)}) copy-start(f32[1,64,16,512]{3,2,1,0:T(8,128)} %pixels_ref.1) | copy-start | bytes 6291460
  15.1 1.6 %copy-start = (bf16[1024,1536]{1,0:T(8,128)(2,1)}, bf16[1024,1536]{1,0:T(8,128)(2,1)S(1)}, u32[]{:S(2)}) copy-start(bf16[1024,1536]{1,0:T(8,128)(2,1)S(1)} %get-tuple-element.18.refs_1_.u_high) | copy-start | bytes 9437188
  16.8 3.8 %copy-start.1 = (bf16[1024,1536]{1,0:T(8,128)(2,1)S(1)}, bf16[1024,1536]{1,0:T(8,128)(2,1)}, u32[]{:S(2)}) copy-start(bf16[1024,1536]{1,0:T(8,128)(2,1)} %copy-done) | copy-start | bytes 9437188
  19.7 15.5 %copy-start.7 = (f32[2,4,4,8,8,128]{5,4,3,2,1,0:T(8,128)}, f32[2,4,4,8,8,128]{5,4,3,2,1,0:T(8,128)S(1)}, u32[]{:S(2)}) copy-start(f32[2,4,4,8,8,128]{5,4,3,2,1,0:T(8,128)S(1)} %get-tuple-element.29) | copy-start | bytes 3145732
  19.7 15.5 %collective-permute-start.1 = (f32[2,4,4,8,8,128]{5,4,3,2,1,0:T(8,128)S(1)}, f32[2,4,4,8,8,128]{5,4,3,2,1,0:T(8,128)S(1)}, u32[]{:S(2)}, u32[]{:S(2)}) collective-permute-start(f32[2,4,4,8,8,128]{5,4,3,2,1,0:T(8,128)S(1)} %get-tuple-element.30.after), channel_id=1, source_target_pairs={{0,2},{1,9},{2,0},{3,11},{4,6},{5,13},{6,4},{7,15},{8,10},{9,1},{1... | collective-permute-start | bytes 3145736 | tf_op jit(solution)/shard_map/ppermute | solution.py:296
  30.6 5.5 %copy-start.2 = (f32[4,4,2,8,8,128]{5,4,3,2,1,0:T(8,128)}, f32[4,4,2,8,8,128]{5,4,3,2,1,0:T(8,128)S(1)}, u32[]{:S(2)}) copy-start(f32[4,4,2,8,8,128]{5,4,3,2,1,0:T(8,128)S(1)} %get-tuple-element.24.after.refs_0_) | copy-start | bytes 3145732
  34.1 1.0 %copy-start.5 = (f32[4,4,2,8,8,128]{5,4,3,2,1,0:T(8,128)}, f32[4,4,2,8,8,128]{5,4,3,2,1,0:T(8,128)S(1)}, u32[]{:S(2)}) copy-start(f32[4,4,2,8,8,128]{5,4,3,2,1,0:T(8,128)S(1)} %get-tuple-element.25.refs_1_) | copy-start | bytes 3145732
  35.1 1.1 %copy-start.10 = (f32[2,4,4,8,8,128]{5,4,3,2,1,0:T(8,128)}, f32[2,4,4,8,8,128]{5,4,3,2,1,0:T(8,128)S(1)}, u32[]{:S(2)}) copy-start(f32[2,4,4,8,8,128]{5,4,3,2,1,0:T(8,128)S(1)} %collective-permute-done.1) | copy-start | bytes 3145732
  36.3 1.0 %copy-start.9 = (f32[1,4,4,8,8,128]{5,4,3,2,1,0:T(8,128)S(1)}, f32[1,4,4,8,8,128]{5,4,3,2,1,0:T(8,128)}, u32[]{:S(2)}) copy-start(f32[1,4,4,8,8,128]{5,4,3,2,1,0:T(8,128)} %slice_add_fusion.7.refs_2_) | copy-start | bytes 1572868
  36.3 3.5 %collective-permute-start.2 = (f32[4,4,2,8,8,128]{5,4,3,2,1,0:T(8,128)}, f32[4,4,2,8,8,128]{5,4,3,2,1,0:T(8,128)S(1)}, u32[]{:S(2)}, u32[]{:S(2)}) collective-permute-start(f32[4,4,2,8,8,128]{5,4,3,2,1,0:T(8,128)} %get-tuple-element.26), channel_id=1, source_target_pairs={{0,1},{1,0},{2,3},{3,2},{4,5},{5,4},{6,7},{7,6},{8,9},{9,8},{10,11... | collective-permute-start | bytes 3145736 | tf_op jit(solution)/shard_map/ppermute | solution.py:296
  37.2 4.0 %collective-permute-start.5 = (f32[4,4,2,8,8,128]{5,4,3,2,1,0:T(8,128)}, f32[4,4,2,8,8,128]{5,4,3,2,1,0:T(8,128)S(1)}, u32[]{:S(2)}, u32[]{:S(2)}) collective-permute-start(f32[4,4,2,8,8,128]{5,4,3,2,1,0:T(8,128)} %get-tuple-element.28), channel_id=1, source_target_pairs={{0,1},{1,0},{2,3},{3,2},{4,5},{5,4},{6,7},{7,6},{8,9},{9,8},{10,11... | collective-permute-start | bytes 3145736 | tf_op jit(solution)/shard_map/ppermute | solution.py:296
  37.3 10.4 %collective-permute-start.10 = (f32[1,4,4,8,8,128]{5,4,3,2,1,0:T(8,128)S(1)}, f32[1,4,4,8,8,128]{5,4,3,2,1,0:T(8,128)S(1)}, u32[]{:S(2)}, u32[]{:S(2)}) collective-permute-start(f32[1,4,4,8,8,128]{5,4,3,2,1,0:T(8,128)S(1)} %copy-done.9), channel_id=1, source_target_pairs={{0,6},{1,25},{2,4},{3,27},{4,2},{5,29},{6,0},{7,31},{8,14},{9,17},... | collective-permute-start | bytes 1572872 | tf_op jit(solution)/shard_map/ppermute | solution.py:296
  39.9 7.8 %copy-start.8 = (f32[2,4,4,8,8,128]{5,4,3,2,1,0:T(8,128)S(1)}, f32[2,4,4,8,8,128]{5,4,3,2,1,0:T(8,128)}, u32[]{:S(2)}) copy-start(f32[2,4,4,8,8,128]{5,4,3,2,1,0:T(8,128)} %copy-done.7) | copy-start | bytes 3145732
  39.9 7.8 %copy-start.11 = (f32[2,4,4,8,8,128]{5,4,3,2,1,0:T(8,128)S(1)}, f32[2,4,4,8,8,128]{5,4,3,2,1,0:T(8,128)}, u32[]{:S(2)}) copy-start(f32[2,4,4,8,8,128]{5,4,3,2,1,0:T(8,128)} %copy-done.10) | copy-start | bytes 3145732
  39.9 9.3 %collective-permute-start.3 = (f32[2,4,2,8,8,128]{5,4,3,2,1,0:T(8,128)S(1)}, f32[2,4,2,8,8,128]{5,4,3,2,1,0:T(8,128)S(1)}, u32[]{:S(2)}, u32[]{:S(2)}) collective-permute-start(f32[2,4,2,8,8,128]{5,4,3,2,1,0:T(8,128)S(1)} %get-tuple-element.34), channel_id=1, source_target_pairs={{0,2},{1,9},{2,0},{3,11},{4,6},{5,13},{6,4},{7,15},{8,10},{9,1},{1... | collective-permute-start | bytes 1572872 | tf_op jit(solution)/shard_map/ppermute | solution.py:296
  41.4 11.9 %collective-permute-start.6 = (f32[2,4,2,8,8,128]{5,4,3,2,1,0:T(8,128)S(1)}, f32[2,4,2,8,8,128]{5,4,3,2,1,0:T(8,128)S(1)}, u32[]{:S(2)}, u32[]{:S(2)}) collective-permute-start(f32[2,4,2,8,8,128]{5,4,3,2,1,0:T(8,128)S(1)} %get-tuple-element.32), channel_id=1, source_target_pairs={{0,6},{1,25},{2,4},{3,27},{4,2},{5,29},{6,0},{7,31},{8,14},{9,17},... | collective-permute-start | bytes 1572872 | tf_op jit(solution)/shard_map/ppermute | solution.py:296
  49.2 7.8 %collective-permute-start.4 = (f32[1,4,2,8,8,128]{5,4,3,2,1,0:T(8,128)S(1)}, f32[1,4,2,8,8,128]{5,4,3,2,1,0:T(8,128)S(1)}, u32[]{:S(2)}, u32[]{:S(2)}) collective-permute-start(f32[1,4,2,8,8,128]{5,4,3,2,1,0:T(8,128)S(1)} %slice_add_fusion.10), channel_id=1, source_target_pairs={{0,6},{1,25},{2,4},{3,27},{4,2},{5,29},{6,0},{7,31},{8,14},{9,17},... | collective-permute-start | bytes 786440 | tf_op jit(solution)/shard_map/ppermute | solution.py:296
  53.4 8.5 %collective-permute-start.7 = (f32[1,4,2,8,8,128]{5,4,3,2,1,0:T(8,128)S(1)}, f32[1,4,2,8,8,128]{5,4,3,2,1,0:T(8,128)S(1)}, u32[]{:S(2)}, u32[]{:S(2)}) collective-permute-start(f32[1,4,2,8,8,128]{5,4,3,2,1,0:T(8,128)S(1)} %slice_add_fusion.8), channel_id=1, source_target_pairs={{0,2},{1,9},{2,0},{3,11},{4,6},{5,13},{6,4},{7,15},{8,10},{9,1},{1... | collective-permute-start | bytes 786440 | tf_op jit(solution)/shard_map/ppermute | solution.py:296
  53.5 10.8 %collective-permute-start.11 = (f32[2,4,8,8,128]{4,3,2,1,0:T(8,128)S(1)}, f32[2,4,8,8,128]{4,3,2,1,0:T(8,128)S(1)}, u32[]{:S(2)}, u32[]{:S(2)}) collective-permute-start(f32[2,4,8,8,128]{4,3,2,1,0:T(8,128)S(1)} %slice_bitcast_fusion), channel_id=1, source_target_pairs={{0,8},{1,3},{2,10},{3,1},{4,12},{5,7},{6,14},{7,5},{8,0},{9,11},{1... | collective-permute-start | bytes 786440 | tf_op jit(solution)/shard_map/ppermute | solution.py:296
  62.0 7.7 %collective-permute-start.8 = (f32[2,4,8,8,128]{4,3,2,1,0:T(8,128)S(1)}, f32[2,4,8,8,128]{4,3,2,1,0:T(8,128)S(1)}, u32[]{:S(2)}, u32[]{:S(2)}) collective-permute-start(f32[2,4,8,8,128]{4,3,2,1,0:T(8,128)S(1)} %fusion.1), channel_id=1, source_target_pairs={{0,24},{1,7},{2,26},{3,5},{4,28},{5,3},{6,30},{7,1},{8,16},{9,15},... | collective-permute-start | bytes 786440 | tf_op jit(solution)/shard_map/ppermute | solution.py:296
  64.3 6.8 %collective-permute-start.12 = (f32[1,4,8,8,128]{4,3,2,1,0:T(8,128)S(1)}, f32[1,4,8,8,128]{4,3,2,1,0:T(8,128)S(1)}, u32[]{:S(2)}, u32[]{:S(2)}) collective-permute-start(f32[1,4,8,8,128]{4,3,2,1,0:T(8,128)S(1)} %slice_add_fusion.12), channel_id=1, source_target_pairs={{0,24},{1,7},{2,26},{3,5},{4,28},{5,3},{6,30},{7,1},{8,16},{9,15},... | collective-permute-start | bytes 393224 | tf_op jit(solution)/shard_map/ppermute | solution.py:296
  69.7 5.1 %collective-permute-start.9 = (f32[1,4,8,8,128]{4,3,2,1,0:T(8,128)S(1)}, f32[1,4,8,8,128]{4,3,2,1,0:T(8,128)S(1)}, u32[]{:S(2)}, u32[]{:S(2)}) collective-permute-start(f32[1,4,8,8,128]{4,3,2,1,0:T(8,128)S(1)} %slice_add_fusion.14), channel_id=1, source_target_pairs={{0,8},{1,3},{2,10},{3,1},{4,12},{5,7},{6,14},{7,5},{8,0},{9,11},{1... | collective-permute-start | bytes 393224 | tf_op jit(solution)/shard_map/ppermute | solution.py:296
  74.8 5.1 %collective-permute-start.13 = (f32[4,8,8,128]{3,2,0,1:T(8,128)S(1)}, f32[4,8,8,128]{3,2,0,1:T(8,128)S(1)}, u32[]{:S(2)}, u32[]{:S(2)}) collective-permute-start(f32[4,8,8,128]{3,2,0,1:T(8,128)S(1)} %slice.232), channel_id=1, source_target_pairs={{0,32},{1,33},{2,34},{3,35},{4,36},{5,37},{6,38},{7,39},{8,40},{9,... | collective-permute-start | bytes 393224 | tf_op jit(solution)/shard_map/ppermute | solution.py:296
  79.9 6.3 %collective-permute-start.14 = (f32[2,8,8,128]{3,2,0,1:T(8,128)S(1)}, f32[2,8,8,128]{3,2,0,1:T(8,128)S(1)}, u32[]{:S(2)}, u32[]{:S(2)}) collective-permute-start(f32[2,8,8,128]{3,2,0,1:T(8,128)S(1)} %get-tuple-element.36), channel_id=1, source_target_pairs={{0,64},{1,65},{2,66},{3,67},{4,68},{5,69},{6,70},{7,71},{8,72},{9,... | collective-permute-start | bytes 196616 | tf_op jit(solution)/shard_map/ppermute | solution.py:296
  86.2 8.3 %collective-permute-start.15 = (f32[1,8,8,128]{3,2,0,1:T(8,128)S(1)}, f32[1,8,8,128]{3,2,0,1:T(8,128)S(1)}, u32[]{:S(2)}, u32[]{:S(2)}) collective-permute-start(f32[1,8,8,128]{3,2,0,1:T(8,128)S(1)} %slice_add_fusion.18), channel_id=1, source_target_pairs={{0,192},{1,193},{2,194},{3,195},{4,196},{5,197},{6,198},{7,199},{8... | collective-permute-start | bytes 98312 | tf_op jit(solution)/shard_map/ppermute | solution.py:296

commit v4 on v2

--- a/solution.py
+++ b/solution.py
@@ -57,15 +57,15 @@
     return ry, (rz & 1) * 4 + ((rz >> 1) ^ (rz >> 2)) % 2 * 2 + (rz >> 2)
 
 
-def write_out(place_ref, source, keep, send, sems, order):
+def write_out(place_ref, sums, keep, send, sems, u_order, v_order):
     copies = []
     for to, core in ((keep, place_ref[0]), (send, 1 - place_ref[0])):
-        for pu, ru in enumerate(order):
-            for pv, rv in enumerate(A_FIRST):
+        for pu, ru in enumerate(u_order):
+            for pv, rv in enumerate(v_order):
                 rx = ru + core * (rv - ru)
                 ry = rv + core * (ru - rv)
-                rows = pl.ds(pl.multiple_of((place_ref[1] ^ rx) * 16, 16), 16)
-                copies.append((source(core, ry, rows), to.at[pu, pv]))
+                rows = pl.ds(pl.multiple_of(((place_ref[1] ^ rx) * 2 + core) * 8, 8), 8)
+                copies.append((sums.at[:, ry, :, rows, :], to.at[pu, pv]))
     started = [pltpu.make_async_copy(src, dst, sems.at[i]) for i, (src, dst) in enumerate(copies)]
     for copy in started:
         copy.start()
@@ -73,31 +73,36 @@
         copy.wait()
 
 
+def fetch(pairs, sems):
+    copies = [pltpu.make_async_copy(src, dst, sems.at[i]) for i, (src, dst) in enumerate(pairs)]
+    for copy in copies:
+        copy.start()
+    return copies
+
+
 def denom_kernel(
-    place_hbm, owner_hbm, offset_hbm, weight_hbm, frac_hbm, bits_ref, col_base_ref, col_frac_ref,
-    keep, send, place_ref, owner_ref, offset_ref, weight_ref, frac_ref, sums, cover, sems,
+    place_hbm, owner_hbm, offset_hbm, weight_hbm, frac_hbm, bits_hbm, col_base_hbm, col_frac_hbm,
+    keep, send, done, place_ref, owner_ref, offset_ref, weight_ref, frac_ref, bits_ref, col_base_ref, col_frac_ref,
+    sums, cover, sems,
 ):
-    small = [
-        pltpu.make_async_copy(src, dst, sems.at[i])
-        for i, (src, dst) in enumerate(
-            (
-                (place_hbm, place_ref), (owner_hbm, owner_ref), (offset_hbm, offset_ref),
-                (weight_hbm, weight_ref), (frac_hbm, frac_ref),
-            )
-        )
-    ]
+    small = fetch(
+        (
+            (place_hbm, place_ref), (owner_hbm, owner_ref), (offset_hbm, offset_ref),
+            (weight_hbm, weight_ref), (frac_hbm, frac_ref), (bits_hbm, bits_ref),
+            (col_base_hbm, col_base_ref), (col_frac_hbm, col_frac_ref),
+        ),
+        sems,
+    )
+    sums[...] = jnp.zeros(sums.shape, F32)
     for copy in small:
-        copy.start()
+        copy.wait()
     factor = column_factor(bits_ref[0]).astype(BF16)
     warp_high, warp_low = split(column_warp(col_base_ref[...], col_frac_ref[...]))
     coverage = jnp.dot(factor, warp_high, preferred_element_type=F32) + jnp.dot(
         factor, warp_low, preferred_element_type=F32
     )
     for block in range(BLOCKS):
-        cover[block // 2, block % 2] = coverage[:, block * LANES : (block + 1) * LANES]
-    sums[...] = jnp.zeros(sums.shape, F32)
-    for copy in small:
-        copy.wait()
+        cover[block] = coverage[:, block * LANES : (block + 1) * LANES]
     frac = column_of(frac_ref, (ROWS, LANES))
     spread = (1.0 - frac) + frac
 
@@ -105,13 +110,13 @@
         ry, rz = relative_patch(place_ref, owner_ref[0, s])
         rows = pl.ds(offset_ref[0, s], ROWS)
         share = spread * weight_ref[0, s]
-        for half in range(2):
-            for j in range(2):
-                sums[half, j, ry, rz, rows, :] += share * cover[half, j, pl.ds(s, 1), :]
+        for block in range(BLOCKS):
+            sums[block, ry, rz, rows, :] += share * cover[block, pl.ds(s, 1), :]
         return carry
 
     lax.fori_loop(0, SEGS, one, 0, unroll=2)
-    write_out(place_ref, lambda core, ry, rows: sums.at[core, :, ry, :, rows, :], keep, send, sems, A_FIRST)
+    write_out(place_ref, sums, keep, send, sems, A_FIRST, A_FIRST)
+    done[...] = jnp.zeros(done.shape, F32)
 
 
 def row_tables(bank_ref, index_ref, coeff_ref, base_ref, frac_ref, k):
@@ -138,8 +143,26 @@
 
 
 def rows_kernel(
-    bank_ref, index_ref, coeff_ref, base_ref, frac_ref, bits_ref, pixels_ref, after, u_high, u_low, blockdiag
+    bank_hbm, index_hbm, coeff_hbm, base_hbm, frac_hbm, bits_hbm, pixels_hbm, after,
+    u_high, u_low, done, bank_ref, index_ref, coeff_ref, base_ref, frac_ref, bits_ref, pixels_ref, blockdiag, sems,
 ):
+    small = fetch(
+        (
+            (bank_hbm, bank_ref), (index_hbm, index_ref), (coeff_hbm, coeff_ref),
+            (base_hbm, base_ref), (frac_hbm, frac_ref), (bits_hbm, bits_ref),
+        ),
+        sems,
+    )
+    blocks = SEGS // BLOCK_SEGS
+
+    def fetch_block(b):
+        segs = pl.ds(b * BLOCK_SEGS, BLOCK_SEGS)
+        return pltpu.make_async_copy(pixels_hbm.at[:, segs], pixels_ref.at[:, segs], sems.at[len(small) + b])
+
+    for b in range(blocks):
+        fetch_block(b).start()
+    for copy in small:
+        copy.wait()
     same = (
         lax.broadcasted_iota(jnp.int32, (BLOCK_ROWS, BLOCK_ROWS), 0) // ROWS
         == lax.broadcasted_iota(jnp.int32, (BLOCK_ROWS, BLOCK_ROWS), 1) // ROWS
@@ -154,6 +177,7 @@
         blockdiag[rows, 2 * BLOCK_ROWS :] = low
 
     def one(b, carry):
+        fetch_block(b).wait()
         segs = pl.ds(b * BLOCK_SEGS, BLOCK_SEGS)
         factor = column_factor(bits_ref[0, segs, :])
         masked = (pixels_ref[0, segs] * factor[:, None, :]).reshape(BLOCK_ROWS, WIDTH)
@@ -169,11 +193,17 @@
         return carry
 
     lax.fori_loop(0, SEGS // BLOCK_SEGS, one, 0)
-
-
-def band_kernel(bank_ref, index_ref, u_high, u_low, after, high_ref, low_ref, band_high, band_low):
+    done[...] = jnp.zeros(done.shape, F32)
+
+
+def band_kernel(
+    bank_hbm, index_hbm, u_high, u_low, after, high_ref, low_ref, bank_ref, index_ref, band_high, band_low, sems
+):
+    small = fetch(((bank_hbm, bank_ref), (index_hbm, index_ref)), sems)
     band_high[...] = jnp.zeros(band_high.shape, BF16)
     band_low[...] = jnp.zeros(band_low.shape, BF16)
+    for copy in small:
+        copy.wait()
     for k in range(NBASIS):
         high, low = split(band_tables(bank_ref, index_ref, k))
         for block in range(BLOCKS):
@@ -201,12 +231,10 @@
 
 def place_kernel(
     chunk, place_ref, owner_ref, offset_ref, weight_ref, col_base_ref, col_frac_ref, high_ref, low_ref, after,
-    keep, send, sums, lifted, sems,
+    keep, send, done, sums, lifted, sems,
 ):
-    picked = [slice((2 * half + chunk) * LANES, (2 * half + chunk + 1) * LANES) for half in range(2)]
-    base = jnp.concatenate([col_base_ref[:, cols] for cols in picked], axis=1)
-    frac = jnp.concatenate([col_frac_ref[:, cols] for cols in picked], axis=1)
-    warp_high, warp_low = split(column_warp(base, frac))
+    cols = slice(2 * chunk * LANES, 2 * (chunk + 1) * LANES)
+    warp_high, warp_low = split(column_warp(col_base_ref[:, cols], col_frac_ref[:, cols]))
     dot = functools.partial(jnp.dot, preferred_element_type=F32)
     high = high_ref[...]
     warped = dot(high, warp_high) + dot(high, warp_low) + dot(low_ref[...], warp_high)
@@ -225,46 +253,59 @@
 
     lax.fori_loop(0, SEGS, one, 0, unroll=2)
     order = (A_FIRST, B_FIRST)[chunk]
-    write_out(place_ref, lambda core, ry, rows: sums.at[core, ry, :, rows, :], keep, send, sems, order)
+    write_out(place_ref, sums, keep, send, sems, order, B_FIRST)
+    done[...] = jnp.zeros(done.shape, F32)
 
 
 SMEM = pl.BlockSpec(memory_space=pltpu.SMEM)
 VMEM = pl.BlockSpec(memory_space=pltpu.VMEM)
 ANY = pl.BlockSpec(memory_space=pl.ANY)
+HBM = pl.BlockSpec(memory_space=pltpu.HBM)
+TOKEN = jax.ShapeDtypeStruct((8, LANES), F32)
 PARAMS = pltpu.CompilerParams(vmem_limit_bytes=40 * 1024 * 1024)
 
 
+def pinned(*values):
+    return [pltpu.with_memory_space_constraint(value, pltpu.HBM) for value in values]
+
+
 def denom_sums(place, owner, offset, weight, row_frac, bits, col_base, col_frac):
-    parts = jax.ShapeDtypeStruct((4, 4, 2, NZ, 16, LANES), F32)
+    parts = jax.ShapeDtypeStruct((4, 4, BLOCKS, NZ, 8, LANES), F32)
     return pl.pallas_call(
         denom_kernel,
-        out_shape=(parts, parts),
-        in_specs=[ANY] * 5 + [VMEM] * 3,
-        out_specs=(ANY,) * 2,
+        out_shape=(parts, parts, TOKEN),
+        in_specs=[HBM] * 8,
+        out_specs=(ANY, ANY, VMEM),
         scratch_shapes=[
             pltpu.SMEM((4,), jnp.int32), pltpu.SMEM((1, SEGS), jnp.int32), pltpu.SMEM((1, SEGS), jnp.int32),
-            pltpu.SMEM((1, SEGS), F32), pltpu.SMEM((1, ROWS), F32),
-            pltpu.VMEM((2, 2, NY, NZ, 64, LANES), F32), pltpu.VMEM((2, 2, SEGS, LANES), F32),
+            pltpu.SMEM((1, SEGS), F32), pltpu.SMEM((1, ROWS), F32), pltpu.VMEM((1, SEGS, WIDTH), jnp.int32),
+            pltpu.VMEM((1, WIDTH), jnp.int32), pltpu.VMEM((1, WIDTH), F32),
+            pltpu.VMEM((BLOCKS, NY, NZ, 64, LANES), F32), pltpu.VMEM((BLOCKS, SEGS, LANES), F32),
             pltpu.SemaphoreType.DMA((32,)),
         ],
         compiler_params=PARAMS,
-        cost_estimate=pl.CostEstimate(flops=4 * 10**9, bytes_accessed=4 * 10**6, transcendentals=0),
+        cost_estimate=pl.CostEstimate(flops=10**3, bytes_accessed=10**3, transcendentals=0),
         name="denom_sums",
-    )(place, owner, offset, weight, row_frac, bits, col_base, col_frac)
+    )(*pinned(place, owner, offset, weight, row_frac, bits, col_base, col_frac))
 
 
 def row_pass(bank, index, coeff, row_base, row_frac, bits, pixels, after):
     wide = jax.ShapeDtypeStruct((SEGS * ROWS, NBASIS * WIDTH), BF16)
     return pl.pallas_call(
         rows_kernel,
-        out_shape=(wide, wide),
-        in_specs=[SMEM] * 5 + [VMEM] * 2 + [ANY],
-        out_specs=(VMEM, VMEM),
-        scratch_shapes=[pltpu.VMEM((NBASIS * BLOCK_ROWS, 3 * BLOCK_ROWS), BF16)],
+        out_shape=(wide, wide, TOKEN),
+        in_specs=[HBM] * 7 + [VMEM],
+        out_specs=(VMEM, VMEM, VMEM),
+        scratch_shapes=[
+            pltpu.SMEM(bank.shape, F32), pltpu.SMEM((1, NBASIS), jnp.int32), pltpu.SMEM((1, NBASIS), F32),
+            pltpu.SMEM((1, ROWS), jnp.int32), pltpu.SMEM((1, ROWS), F32),
+            pltpu.VMEM(bits.shape, jnp.int32), pltpu.VMEM(pixels.shape, F32),
+            pltpu.VMEM((NBASIS * BLOCK_ROWS, 3 * BLOCK_ROWS), BF16), pltpu.SemaphoreType.DMA((10,)),
+        ],
         compiler_params=PARAMS,
-        cost_estimate=pl.CostEstimate(flops=4 * 10**9, bytes_accessed=8 * 10**6, transcendentals=0),
+        cost_estimate=pl.CostEstimate(flops=10**3, bytes_accessed=10**3, transcendentals=0),
         name="row_pass",
-    )(bank, index, coeff, row_base, row_frac, bits, pixels, after)
+    )(*pinned(bank, index, coeff, row_base, row_frac, bits, pixels), after)
 
 
 def band_pass(bank, index, u_high, u_low, after):
@@ -273,28 +314,30 @@
     return pl.pallas_call(
         band_kernel,
         out_shape=(wide, wide),
-        in_specs=[SMEM] * 2 + [VMEM] * 2 + [ANY],
+        in_specs=[HBM] * 2 + [VMEM] * 3,
         out_specs=(VMEM, VMEM),
-        scratch_shapes=[band, band],
+        scratch_shapes=[
+            pltpu.SMEM(bank.shape, F32), pltpu.SMEM(index.shape, jnp.int32), band, band, pltpu.SemaphoreType.DMA((2,))
+        ],
         compiler_params=PARAMS,
-        cost_estimate=pl.CostEstimate(flops=6 * 10**9, bytes_accessed=8 * 10**6, transcendentals=0),
+        cost_estimate=pl.CostEstimate(flops=10**3, bytes_accessed=10**3, transcendentals=0),
         name="band_pass",
-    )(bank, index, u_high, u_low, after)
+    )(*pinned(bank, index), u_high, u_low, after)
 
 
 def numer_sums(chunk, place, owner, offset, weight, col_base, col_frac, high, low, after):
-    parts = jax.ShapeDtypeStruct((4, 4, NZ, 16, LANES), F32)
+    parts = jax.ShapeDtypeStruct((4, 4, 2, NZ, 8, LANES), F32)
     return pl.pallas_call(
         functools.partial(place_kernel, chunk),
-        out_shape=(parts, parts),
-        in_specs=[SMEM] * 4 + [VMEM] * 4 + [ANY],
-        out_specs=(ANY,) * 2,
+        out_shape=(parts, parts, TOKEN),
+        in_specs=[SMEM] * 4 + [VMEM] * 5,
+        out_specs=(ANY, ANY, VMEM),
         scratch_shapes=[
             pltpu.VMEM((2, NY, NZ, 64, LANES), F32), pltpu.VMEM((2, SEGS * ROWS, LANES), F32),
             pltpu.SemaphoreType.DMA((32,)),
         ],
         compiler_params=PARAMS,
-        cost_estimate=pl.CostEstimate(flops=3 * 10**9, bytes_accessed=4 * 10**6, transcendentals=0),
+        cost_estimate=pl.CostEstimate(flops=10**3, bytes_accessed=10**3, transcendentals=0),
         name=f"numer_sums_{chunk}",
     )(place, owner, offset, weight, col_base, col_frac, high, low, after)
 
@@ -332,6 +375,21 @@
     return keep[:middle] + got[:middle], keep[middle:] + got[middle:]
 
 
+def hold(values, after):
+    def kernel(*refs):
+        pass
+
+    return pl.pallas_call(
+        kernel,
+        out_shape=tuple(jax.ShapeDtypeStruct(value.shape, value.dtype) for value in values),
+        in_specs=[VMEM] * (len(values) + 1),
+        out_specs=(VMEM,) * len(values),
+        input_output_aliases={i: i for i in range(len(values))},
+        compiler_params=PARAMS,
+        name="hold",
+    )(*values, after)
+
+
 def per_device(
     pixels, mask_bits, owner, row_offset, seg_weight, psf_bank, basis_index, basis_coeff,
     row_base, row_frac, col_base, col_frac,
@@ -339,32 +397,37 @@
     sky = lax.axis_index("sky").astype(jnp.int32)
     grp = lax.axis_index("grp").astype(jnp.int32)
     place = jnp.stack([grp % 2, grp // 2, sky % NY, sky // NY])
-    d_keep, d_send = denom_sums(place, owner, row_offset, seg_weight, row_frac, mask_bits, col_base, col_frac)
-    u_high, u_low = row_pass(psf_bank, basis_index, basis_coeff, row_base, row_frac, mask_bits, pixels, d_send)
-    d_keep, d_send = halve(d_keep, swap_core(d_send))
+    d_keep, d_send, done = denom_sums(
+        place, owner, row_offset, seg_weight, row_frac, mask_bits, col_base, col_frac
+    )
+    u_high, u_low, done = row_pass(
+        psf_bank, basis_index, basis_coeff, row_base, row_frac, mask_bits, pixels, done
+    )
+    (d_got,) = hold((swap_core(d_send),), done)
+    d_keep, d_send = halve(d_keep, d_got)
     high, low = band_pass(psf_bank, basis_index, u_high, u_low, d_send)
     d_got = swap_u(d_send, 1)
-    first = numer_sums(0, place, owner, row_offset, seg_weight, col_base, col_frac, high, low, high)
-    second = numer_sums(1, place, owner, row_offset, seg_weight, col_base, col_frac, high, low, first[1])
-    n_parts = [halve(keep, swap_core(send)) for keep, send in (first, second)]
+    first = numer_sums(0, place, owner, row_offset, seg_weight, col_base, col_frac, high, low, done)
+    second = numer_sums(1, place, owner, row_offset, seg_weight, col_base, col_frac, high, low, first[2])
     d_keep, d_send = halve(d_keep, d_got)
+    n_sends = hold((first[1], second[1]), d_send)
+    n_got = [swap_core(send) for send in n_sends]
     d_got = swap_u(d_send, 3)
+    n_parts = [halve(keep, got) for (keep, _, _), got in zip((first, second), n_got)]
     n_parts = [halve(keep, swap_u(send, step)) for (keep, send), step in zip(n_parts, (1, 3))]
+    d_part = (d_keep + d_got)[0]
+    d_keep, d_send = halve(d_part[:2], swap_v(d_part[2:], 1))
     n_parts = [keep[0] + swap_u(send, step)[0] for (keep, send), step in zip(n_parts, (3, 1))]
-    d_part = (d_keep + d_got)[0]
-    both = jnp.concatenate([jnp.stack(n_parts, axis=1), d_part], axis=1)
-    keep, send = halve(both[:2], swap_v(both[2:], 1))
-    both = jnp.swapaxes((keep + swap_v(send, 3))[0], 0, 1)
+    n_part = jnp.concatenate(n_parts, axis=1)
+    n_keep, n_send = halve(n_part[:2], swap_v(n_part[2:], 3))
+    d_part = (d_keep + swap_v(d_send, 3))[0]
+    n_part = (n_keep + swap_v(n_send, 1))[0]
+    both = jnp.swapaxes(jnp.concatenate([n_part, d_part]), 0, 1)
     keep, send = halve(both[:4], swap_z(both[4:], 1))
     keep, send = halve(keep, swap_z(send, 2))
     both = (keep + swap_z(send, 6))[0]
-    coadd = both[:2] / jnp.maximum(both[2:], 1.0)
-    coadd = jnp.swapaxes(coadd.reshape(2, 2, 8, LANES), 0, 1)
-    odd = place[0] == 1
-    mine = jnp.where(odd, coadd[1], coadd[0])
-    other = swap_core(jnp.where(odd, coadd[0], coadd[1]))
-    blocks = jnp.where(odd, jnp.concatenate([other, mine]), jnp.concatenate([mine, other]))
-    return jnp.swapaxes(blocks, 0, 1).reshape(8, WIDTH)
+    coadd = both[:BLOCKS] / jnp.maximum(both[BLOCKS:], 1.0)
+    return jnp.swapaxes(coadd, 0, 1).reshape(8, WIDTH)
 
 
 def solution(mesh):

time: 95.5 us -> 83.1 us (0.87); the launches traced: 93.8 us -> 82.9 us
  waiting for transfers between devices: 40.1 us -> 33.6 us
  local copies, waits for them, and re-layouts: 4.97 us -> 0.06 us
  starting transfers between devices: 25.8 us -> 24 us
  Pallas kernels: 20.8 us -> 22.5 us
    ppermute x15 -> x16, waiting for transfers between devices: 40.1 us -> 33.6 us  [permute(): return lax.ppermute(value, ('sky', 'grp'), pairs)]
    unnamed x30 -> x12, local copies, waits for them, and re-layouts: 4.93 us -> 0.03 us
    ppermute x15 -> x16, starting transfers between devices: 25.8 us -> 24 us  [permute(): return lax.ppermute(value, ('sky', 'grp'), pairs)]
    pallas_call x3 -> x5, Pallas kernels: 13.7 us -> 14.9 us  [the longest x1 6.73 us: band_pass(): pl.pallas_call(band_kernel, out_shape=(wide, wide), in_specs=[HBM] * 2 +...]
  transfers between devices with their start and end apart: 15 -> 16, of which waited for: 11 -> 13; matrix products, arithmetic and copies ran while one was open for 1% -> 1% of each run, Pallas kernels for 5% -> 23%
where the time goes in v4:
time: 83.1 us; the launch traced here: 82.9 us
  waiting for transfers between devices  33.6 us (40%)
  starting transfers between devices  24 us (29%)
  Pallas kernels  22.5 us (27%)
  other arithmetic  2.46 us (3%)
    ppermute x16, waiting for transfers between devices, permute(): return lax.ppermute(value, ('sky', 'grp'), pairs)  33.6 us
    ppermute x16, starting transfers between devices, permute(): return lax.ppermute(value, ('sky', 'grp'), pairs)  24 us
    pallas_call x2, Pallas kernels, numer_sums(): pl.pallas_call(functools.partial(place_kernel, chunk), out_shape=(parts,...  7.59 us
    pallas_call x1, Pallas kernels, band_pass(): pl.pallas_call(band_kernel, out_shape=(wide, wide), in_specs=[HBM] * 2 +...  6.73 us
    pallas_call x1, Pallas kernels, row_pass(): pl.pallas_call(rows_kernel, out_shape=(wide, wide, TOKEN), in_specs=[HBM]...  4.58 us
    pallas_call x1, Pallas kernels, denom_sums(): pl.pallas_call(denom_kernel, out_shape=(parts, parts, TOKEN), in_specs=[H...  3.55 us
  transfers between devices with their start and end apart: 16, of which 13 were waited for; matrix products, arithmetic and copies ran while one was open for 1% of the time, Pallas kernels for 23%

profile of v4, /device:TPU:6, one launch (start us, length us, event | category | flops | bytes accessed | tf_op | source)
XLA Modules:
  0.0 82.9 jit_solution(5341308519383928109)
XLA Ops:
  0.0 0.6 pad_add_fusion.place_hbm.place_ref
  0.6 3.6 %denom_sums.1 = (f32[4,4,4,8,8,128]{5,4,3,2,1,0:T(8,128)S(1)}, f32[4,4,4,8,8,128]{5,4,3,2,1,0:T(8,128)S(1)}, f32[8,128]{1,0:T(8,128)S(1)}) custom-call(s32[4]{0:T(128)} %pad_add_fusion.place_hbm.place_ref, s32[1,64]{1,0:T(1,128)} %owner_ref.3, s32[1,64]{1,0:T(1,128)} %offset_ref.3, f32[1,64]{1,0:T(1,128)} %weight_ref.3, f32[1,16]{1,0:T(1,128)} %frac_hbm.3, ...), custom_call_target="tpu_custom_call" | custom-call | flops 1000 | bytes 1000 | tf_op jit(solution)/shard_map/denom_sums/pallas_call | solution.py:274
  4.3 4.6 %row_pass.1 = (bf16[1024,1536]{1,0:T(8,128)(2,1)S(1)}, bf16[1024,1536]{1,0:T(8,128)(2,1)S(1)}, f32[8,128]{1,0:T(8,128)S(1)}) custom-call(f32[8,2,21]{2,1,0:T(2,128)} %bank_hbm.3, s32[1,3]{1,0:T(1,128)} %index_hbm.3, f32[1,3]{1,0:T(1,128)} %coeff_hbm.1, s32[1,16]{1,0:T(1,128)} %base_hbm.1, f32[1,16]{1,0:T(1,128)} %frac_hbm.3, s32[1,64,512]{2,1,0:T(8,128)} %bits_hbm.3, ...), custom_call_target="tpu_custom_call" | custom-call | flops 1000 | bytes 1000 | tf_op jit(solution)/shard_map/row_pass/pallas_call | solution.py:294
  9.3 0.9 %collective-permute-start.1 = (f32[2,4,4,8,8,128]{5,4,3,2,1,0:T(8,128)S(1)}, f32[2,4,4,8,8,128]{5,4,3,2,1,0:T(8,128)S(1)}, u32[]{:S(2)}, u32[]{:S(2)}) collective-permute-start(f32[2,4,4,8,8,128]{5,4,3,2,1,0:T(8,128)S(1)} %get-tuple-element.36.after), channel_id=1, source_target_pairs={{0,2},{1,9},{2,0},{3,11},{4,6},{5,13},{6,4},{7,15},{8,10},{9,1},{1... | collective-permute-start | bytes 3145736 | tf_op jit(solution)/shard_map/ppermute | solution.py:354
  10.2 6.7 %band_pass.1 = (bf16[1024,512]{1,0:T(8,128)(2,1)S(1)}, bf16[1024,512]{1,0:T(8,128)(2,1)S(1)}) custom-call(f32[8,2,21]{2,1,0:T(2,128)} %bank_hbm.3, s32[1,3]{1,0:T(1,128)} %index_hbm.3, bf16[1024,1536]{1,0:T(8,128)(2,1)S(1)} %get-tuple-element.21.u_high, bf16[1024,1536]{1,0:T(8,128)(2,1)S(1)} %get-tuple-element.22.u_low, ...), custom_call_target="tpu_custom_call" | custom-call | flops 1000 | bytes 1000 | tf_op jit(solution)/shard_map/band_pass/pallas_call | solution.py:314
  17.0 3.5 %numer_sums_0.1 = (f32[4,4,2,8,8,128]{5,4,3,2,1,0:T(8,128)S(1)}, f32[4,4,2,8,8,128]{5,4,3,2,1,0:T(8,128)S(1)}, f32[8,128]{1,0:T(8,128)S(1)}) custom-call(s32[4]{0:T(128)S(1)} %copy-done.2, s32[1,64]{1,0:T(1,128)S(1)} %copy-done.3, s32[1,64]{1,0:T(1,128)S(1)} %copy-done.4, f32[1,64]{1,0:T(1,128)S(1)} %copy-done.5, s32[1,512]{1,0:T(1,128)S(1)} %copy-done, ...), custom_call_target="tpu_custom_call" | custom-call | flops 1000 | bytes 1000 | tf_op jit(solution)/shard_map/numer_sums_0/pallas_call | solution.py:330
  20.6 4.1 %numer_sums_1.1 = (f32[4,4,2,8,8,128]{5,4,3,2,1,0:T(8,128)S(1)}, f32[4,4,2,8,8,128]{5,4,3,2,1,0:T(8,128)S(1)}, f32[8,128]{1,0:T(8,128)}) custom-call(s32[4]{0:T(128)S(1)} %copy-done.2, s32[1,64]{1,0:T(1,128)S(1)} %copy-done.3, s32[1,64]{1,0:T(1,128)S(1)} %copy-done.4, f32[1,64]{1,0:T(1,128)S(1)} %copy-done.5, s32[1,512]{1,0:T(1,128)S(1)} %copy-done, ...), custom_call_target="tpu_custom_call" | custom-call | flops 1000 | bytes 1000 | tf_op jit(solution)/shard_map/numer_sums_1/pallas_call | solution.py:330
  24.7 1.0 %collective-permute-start.2 = (f32[4,4,2,8,8,128]{5,4,3,2,1,0:T(8,128)S(1)}, f32[4,4,2,8,8,128]{5,4,3,2,1,0:T(8,128)S(1)}, u32[]{:S(2)}, u32[]{:S(2)}) collective-permute-start(f32[4,4,2,8,8,128]{5,4,3,2,1,0:T(8,128)S(1)} %get-tuple-element.32), channel_id=1, source_target_pairs={{0,1},{1,0},{2,3},{3,2},{4,5},{5,4},{6,7},{7,6},{8,9},{9,8},{10,11... | collective-permute-start | bytes 3145736 | tf_op jit(solution)/shard_map/ppermute | solution.py:354
  25.9 1.2 %collective-permute-start.10 = (f32[1,4,4,8,8,128]{5,4,3,2,1,0:T(8,128)S(1)}, f32[1,4,4,8,8,128]{5,4,3,2,1,0:T(8,128)S(1)}, u32[]{:S(2)}, u32[]{:S(2)}) collective-permute-start(f32[1,4,4,8,8,128]{5,4,3,2,1,0:T(8,128)S(1)} %slice_add_fusion.7.refs_2_), channel_id=1, source_target_pairs={{0,6},{1,25},{2,4},{3,27},{4,2},{5,29},{6,0},{7,31},{8,14},{9,17},... | collective-permute-start | bytes 1572872 | tf_op jit(solution)/shard_map/ppermute | solution.py:354
  27.1 1.0 %collective-permute-done.2 = f32[4,4,2,8,8,128]{5,4,3,2,1,0:T(8,128)S(1)} collective-permute-done((f32[4,4,2,8,8,128]{5,4,3,2,1,0:T(8,128)S(1)}, f32[4,4,2,8,8,128]{5,4,3,2,1,0:T(8,128)S(1)}, u32[]{:S(2)}, u32[]{:S(2)}) %collective-permute-start.2) | collective-permute-done | bytes 1048608 | tf_op jit(solution)/shard_map/ppermute | solution.py:354
  28.2 0.9 %collective-permute-start.3 = (f32[2,4,2,8,8,128]{5,4,3,2,1,0:T(8,128)S(1)}, f32[2,4,2,8,8,128]{5,4,3,2,1,0:T(8,128)S(1)}, u32[]{:S(2)}, u32[]{:S(2)}) collective-permute-start(f32[2,4,2,8,8,128]{5,4,3,2,1,0:T(8,128)S(1)} %get-tuple-element.40), channel_id=1, source_target_pairs={{0,2},{1,9},{2,0},{3,11},{4,6},{5,13},{6,4},{7,15},{8,10},{9,1},{1... | collective-permute-start | bytes 1572872 | tf_op jit(solution)/shard_map/ppermute | solution.py:354
  29.7 1.7 %collective-permute-start.6 = (f32[2,4,2,8,8,128]{5,4,3,2,1,0:T(8,128)S(1)}, f32[2,4,2,8,8,128]{5,4,3,2,1,0:T(8,128)S(1)}, u32[]{:S(2)}, u32[]{:S(2)}) collective-permute-start(f32[2,4,2,8,8,128]{5,4,3,2,1,0:T(8,128)S(1)} %get-tuple-element.38), channel_id=1, source_target_pairs={{0,6},{1,25},{2,4},{3,27},{4,2},{5,29},{6,0},{7,31},{8,14},{9,17},... | collective-permute-start | bytes 1572872 | tf_op jit(solution)/shard_map/ppermute | solution.py:354
  31.4 4.8 %collective-permute-done.10 = f32[1,4,4,8,8,128]{5,4,3,2,1,0:T(8,128)S(1)} collective-permute-done((f32[1,4,4,8,8,128]{5,4,3,2,1,0:T(8,128)S(1)}, f32[1,4,4,8,8,128]{5,4,3,2,1,0:T(8,128)S(1)}, u32[]{:S(2)}, u32[]{:S(2)}) %collective-permute-start.10) | collective-permute-done | bytes 524320 | tf_op jit(solution)/shard_map/ppermute | solution.py:354
  36.4 1.1 %collective-permute-done.3 = f32[2,4,2,8,8,128]{5,4,3,2,1,0:T(8,128)S(1)} collective-permute-done((f32[2,4,2,8,8,128]{5,4,3,2,1,0:T(8,128)S(1)}, f32[2,4,2,8,8,128]{5,4,3,2,1,0:T(8,128)S(1)}, u32[]{:S(2)}, u32[]{:S(2)}) %collective-permute-start.3) | collective-permute-done | bytes 524320 | tf_op jit(solution)/shard_map/ppermute | solution.py:354
  37.5 1.4 %collective-permute-start.4 = (f32[1,4,2,8,8,128]{5,4,3,2,1,0:T(8,128)S(1)}, f32[1,4,2,8,8,128]{5,4,3,2,1,0:T(8,128)S(1)}, u32[]{:S(2)}, u32[]{:S(2)}) collective-permute-start(f32[1,4,2,8,8,128]{5,4,3,2,1,0:T(8,128)S(1)} %slice_add_fusion.10), channel_id=1, source_target_pairs={{0,6},{1,25},{2,4},{3,27},{4,2},{5,29},{6,0},{7,31},{8,14},{9,17},... | collective-permute-start | bytes 786440 | tf_op jit(solution)/shard_map/ppermute | solution.py:354
  39.0 2.9 %collective-permute-done.6 = f32[2,4,2,8,8,128]{5,4,3,2,1,0:T(8,128)S(1)} collective-permute-done((f32[2,4,2,8,8,128]{5,4,3,2,1,0:T(8,128)S(1)}, f32[2,4,2,8,8,128]{5,4,3,2,1,0:T(8,128)S(1)}, u32[]{:S(2)}, u32[]{:S(2)}) %collective-permute-start.6) | collective-permute-done | bytes 524320 | tf_op jit(solution)/shard_map/ppermute | solution.py:354
  42.0 1.1 %collective-permute-start.11 = (f32[2,4,8,8,128]{4,3,2,1,0:T(8,128)S(1)}, f32[2,4,8,8,128]{4,3,2,1,0:T(8,128)S(1)}, u32[]{:S(2)}, u32[]{:S(2)}) collective-permute-start(f32[2,4,8,8,128]{4,3,2,1,0:T(8,128)S(1)} %slice_bitcast_fusion), channel_id=1, source_target_pairs={{0,8},{1,3},{2,10},{3,1},{4,12},{5,7},{6,14},{7,5},{8,0},{9,11},{1... | collective-permute-start | bytes 786440 | tf_op jit(solution)/shard_map/ppermute | solution.py:354
  43.2 2.2 %collective-permute-done.4 = f32[1,4,2,8,8,128]{5,4,3,2,1,0:T(8,128)S(1)} collective-permute-done((f32[1,4,2,8,8,128]{5,4,3,2,1,0:T(8,128)S(1)}, f32[1,4,2,8,8,128]{5,4,3,2,1,0:T(8,128)S(1)}, u32[]{:S(2)}, u32[]{:S(2)}) %collective-permute-start.4) | collective-permute-done | bytes 262176 | tf_op jit(solution)/shard_map/ppermute | solution.py:354
  45.5 4.4 %collective-permute-done.7 = f32[1,4,2,8,8,128]{5,4,3,2,1,0:T(8,128)S(1)} collective-permute-done((f32[1,4,2,8,8,128]{5,4,3,2,1,0:T(8,128)S(1)}, f32[1,4,2,8,8,128]{5,4,3,2,1,0:T(8,128)S(1)}, u32[]{:S(2)}, u32[]{:S(2)}) %collective-permute-start.7) | collective-permute-done | bytes 262176 | tf_op jit(solution)/shard_map/ppermute | solution.py:354
  50.0 2.3 %collective-permute-start.8 = (f32[2,4,8,8,128]{4,3,2,1,0:T(8,128)S(1)}, f32[2,4,8,8,128]{4,3,2,1,0:T(8,128)S(1)}, u32[]{:S(2)}, u32[]{:S(2)}) collective-permute-start(f32[2,4,8,8,128]{4,3,2,1,0:T(8,128)S(1)} %fusion.1), channel_id=1, source_target_pairs={{0,24},{1,7},{2,26},{3,5},{4,28},{5,3},{6,30},{7,1},{8,16},{9,15},... | collective-permute-start | bytes 786440 | tf_op jit(solution)/shard_map/ppermute | solution.py:354
  52.3 1.1 %collective-permute-start.12 = (f32[1,4,8,8,128]{4,3,2,1,0:T(8,128)S(1)}, f32[1,4,8,8,128]{4,3,2,1,0:T(8,128)S(1)}, u32[]{:S(2)}, u32[]{:S(2)}) collective-permute-start(f32[1,4,8,8,128]{4,3,2,1,0:T(8,128)S(1)} %slice_add_fusion.12), channel_id=1, source_target_pairs={{0,24},{1,7},{2,26},{3,5},{4,28},{5,3},{6,30},{7,1},{8,16},{9,15},... | collective-permute-start | bytes 393224 | tf_op jit(solution)/shard_map/ppermute | solution.py:354
  53.4 4.2 %collective-permute-done.8 = f32[2,4,8,8,128]{4,3,2,1,0:T(8,128)S(1)} collective-permute-done((f32[2,4,8,8,128]{4,3,2,1,0:T(8,128)S(1)}, f32[2,4,8,8,128]{4,3,2,1,0:T(8,128)S(1)}, u32[]{:S(2)}, u32[]{:S(2)}) %collective-permute-start.8) | collective-permute-done | bytes 262176 | tf_op jit(solution)/shard_map/ppermute | solution.py:354
  57.7 0.6 collective-permute-start.9
  58.3 0.8 collective-permute-done.12
  59.1 3.6 %collective-permute-done.9 = f32[1,4,8,8,128]{4,3,2,1,0:T(8,128)S(1)} collective-permute-done((f32[1,4,8,8,128]{4,3,2,1,0:T(8,128)S(1)}, f32[1,4,8,8,128]{4,3,2,1,0:T(8,128)S(1)}, u32[]{:S(2)}, u32[]{:S(2)}) %collective-permute-start.9) | collective-permute-done | bytes 131104 | tf_op jit(solution)/shard_map/ppermute | solution.py:354
  62.8 2.0 %collective-permute-start.13 = (f32[4,8,8,128]{3,2,0,1:T(8,128)S(1)}, f32[4,8,8,128]{3,2,0,1:T(8,128)S(1)}, u32[]{:S(2)}, u32[]{:S(2)}) collective-permute-start(f32[4,8,8,128]{3,2,0,1:T(8,128)S(1)} %slice.232), channel_id=1, source_target_pairs={{0,32},{1,33},{2,34},{3,35},{4,36},{5,37},{6,38},{7,39},{8,40},{9,... | collective-permute-start | bytes 393224 | tf_op jit(solution)/shard_map/ppermute | solution.py:354
  64.8 3.8 %collective-permute-done.13 = f32[4,8,8,128]{3,2,0,1:T(8,128)S(1)} collective-permute-done((f32[4,8,8,128]{3,2,0,1:T(8,128)S(1)}, f32[4,8,8,128]{3,2,0,1:T(8,128)S(1)}, u32[]{:S(2)}, u32[]{:S(2)}) %collective-permute-start.13) | collective-permute-done | bytes 131104 | tf_op jit(solution)/shard_map/ppermute | solution.py:354
  68.6 2.9 %collective-permute-start.14 = (f32[2,8,8,128]{3,2,0,1:T(8,128)S(1)}, f32[2,8,8,128]{3,2,0,1:T(8,128)S(1)}, u32[]{:S(2)}, u32[]{:S(2)}) collective-permute-start(f32[2,8,8,128]{3,2,0,1:T(8,128)S(1)} %get-tuple-element.42), channel_id=1, source_target_pairs={{0,64},{1,65},{2,66},{3,67},{4,68},{5,69},{6,70},{7,71},{8,72},{9,... | collective-permute-start | bytes 196616 | tf_op jit(solution)/shard_map/ppermute | solution.py:354
  71.5 2.3 %collective-permute-done.14 = f32[2,8,8,128]{3,2,0,1:T(8,128)S(1)} collective-permute-done((f32[2,8,8,128]{3,2,0,1:T(8,128)S(1)}, f32[2,8,8,128]{3,2,0,1:T(8,128)S(1)}, u32[]{:S(2)}, u32[]{:S(2)}) %collective-permute-start.14) | collective-permute-done | bytes 65568 | tf_op jit(solution)/shard_map/ppermute | solution.py:354
  73.8 6.5 %collective-permute-start.15 = (f32[1,8,8,128]{3,2,0,1:T(8,128)S(1)}, f32[1,8,8,128]{3,2,0,1:T(8,128)S(1)}, u32[]{:S(2)}, u32[]{:S(2)}) collective-permute-start(f32[1,8,8,128]{3,2,0,1:T(8,128)S(1)} %slice_add_fusion.18), channel_id=1, source_target_pairs={{0,192},{1,193},{2,194},{3,195},{4,196},{5,197},{6,198},{7,199},{8... | collective-permute-start | bytes 98312 | tf_op jit(solution)/shard_map/ppermute | solution.py:354
  80.3 1.9 %collective-permute-done.15 = f32[1,8,8,128]{3,2,0,1:T(8,128)S(1)} collective-permute-done((f32[1,8,8,128]{3,2,0,1:T(8,128)S(1)}, f32[1,8,8,128]{3,2,0,1:T(8,128)S(1)}, u32[]{:S(2)}, u32[]{:S(2)}) %collective-permute-start.15) | collective-permute-done | bytes 32800 | tf_op jit(solution)/shard_map/ppermute | solution.py:354
  82.3 0.6 fusion.12
  (41 shorter events, 2.0 us)
Async XLA Ops:
  4.2 4.7 %collective-permute-start = (f32[4,4,4,8,8,128]{5,4,3,2,1,0:T(8,128)S(1)}, f32[4,4,4,8,8,128]{5,4,3,2,1,0:T(8,128)S(1)}, u32[]{:S(2)}, u32[]{:S(2)}) collective-permute-start(f32[4,4,4,8,8,128]{5,4,3,2,1,0:T(8,128)S(1)} %get-tuple-element.24), channel_id=1, source_target_pairs={{0,1},{1,0},{2,3},{3,2},{4,5},{5,4},{6,7},{7,6},{8,9},{9,8},{10,11... | collective-permute-start | bytes 6291464 | tf_op jit(solution)/shard_map/ppermute | solution.py:354
  9.3 15.4 %collective-permute-start.1 = (f32[2,4,4,8,8,128]{5,4,3,2,1,0:T(8,128)S(1)}, f32[2,4,4,8,8,128]{5,4,3,2,1,0:T(8,128)S(1)}, u32[]{:S(2)}, u32[]{:S(2)}) collective-permute-start(f32[2,4,4,8,8,128]{5,4,3,2,1,0:T(8,128)S(1)} %get-tuple-element.36.after), channel_id=1, source_target_pairs={{0,2},{1,9},{2,0},{3,11},{4,6},{5,13},{6,4},{7,15},{8,10},{9,1},{1... | collective-permute-start | bytes 3145736 | tf_op jit(solution)/shard_map/ppermute | solution.py:354
  10.2 6.8 %copy-start = (s32[1,512]{1,0:T(1,128)S(1)}, s32[1,512]{1,0:T(1,128)}, u32[]{:S(2)}) copy-start(s32[1,512]{1,0:T(1,128)} %col_base_ref.3) | copy-start | bytes 6148
  10.2 6.8 %copy-start.1 = (f32[1,512]{1,0:T(1,128)S(1)}, f32[1,512]{1,0:T(1,128)}, u32[]{:S(2)}) copy-start(f32[1,512]{1,0:T(1,128)} %col_frac_ref.3) | copy-start | bytes 6148
  10.2 6.8 %copy-start.2 = (s32[4]{0:T(128)S(1)}, s32[4]{0:T(128)}, u32[]{:S(2)}) copy-start(s32[4]{0:T(128)} %pad_add_fusion.place_hbm.place_ref) | copy-start | bytes 52
  10.2 6.8 %copy-start.3 = (s32[1,64]{1,0:T(1,128)S(1)}, s32[1,64]{1,0:T(1,128)}, u32[]{:S(2)}) copy-start(s32[1,64]{1,0:T(1,128)} %owner_ref.3) | copy-start | bytes 772
  10.2 6.8 %copy-start.4 = (s32[1,64]{1,0:T(1,128)S(1)}, s32[1,64]{1,0:T(1,128)}, u32[]{:S(2)}) copy-start(s32[1,64]{1,0:T(1,128)} %offset_ref.3) | copy-start | bytes 772
  10.2 6.8 %copy-start.5 = (f32[1,64]{1,0:T(1,128)S(1)}, f32[1,64]{1,0:T(1,128)}, u32[]{:S(2)}) copy-start(f32[1,64]{1,0:T(1,128)} %weight_ref.3) | copy-start | bytes 772
  24.7 3.3 %collective-permute-start.2 = (f32[4,4,2,8,8,128]{5,4,3,2,1,0:T(8,128)S(1)}, f32[4,4,2,8,8,128]{5,4,3,2,1,0:T(8,128)S(1)}, u32[]{:S(2)}, u32[]{:S(2)}) collective-permute-start(f32[4,4,2,8,8,128]{5,4,3,2,1,0:T(8,128)S(1)} %get-tuple-element.32), channel_id=1, source_target_pairs={{0,1},{1,0},{2,3},{3,2},{4,5},{5,4},{6,7},{7,6},{8,9},{9,8},{10,11... | collective-permute-start | bytes 3145736 | tf_op jit(solution)/shard_map/ppermute | solution.py:354
  25.8 3.8 %collective-permute-start.5 = (f32[4,4,2,8,8,128]{5,4,3,2,1,0:T(8,128)S(1)}, f32[4,4,2,8,8,128]{5,4,3,2,1,0:T(8,128)S(1)}, u32[]{:S(2)}, u32[]{:S(2)}) collective-permute-start(f32[4,4,2,8,8,128]{5,4,3,2,1,0:T(8,128)S(1)} %get-tuple-element.34), channel_id=1, source_target_pairs={{0,1},{1,0},{2,3},{3,2},{4,5},{5,4},{6,7},{7,6},{8,9},{9,8},{10,11... | collective-permute-start | bytes 3145736 | tf_op jit(solution)/shard_map/ppermute | solution.py:354
  25.9 10.4 %collective-permute-start.10 = (f32[1,4,4,8,8,128]{5,4,3,2,1,0:T(8,128)S(1)}, f32[1,4,4,8,8,128]{5,4,3,2,1,0:T(8,128)S(1)}, u32[]{:S(2)}, u32[]{:S(2)}) collective-permute-start(f32[1,4,4,8,8,128]{5,4,3,2,1,0:T(8,128)S(1)} %slice_add_fusion.7.refs_2_), channel_id=1, source_target_pairs={{0,6},{1,25},{2,4},{3,27},{4,2},{5,29},{6,0},{7,31},{8,14},{9,17},... | collective-permute-start | bytes 1572872 | tf_op jit(solution)/shard_map/ppermute | solution.py:354
  28.2 9.3 %collective-permute-start.3 = (f32[2,4,2,8,8,128]{5,4,3,2,1,0:T(8,128)S(1)}, f32[2,4,2,8,8,128]{5,4,3,2,1,0:T(8,128)S(1)}, u32[]{:S(2)}, u32[]{:S(2)}) collective-permute-start(f32[2,4,2,8,8,128]{5,4,3,2,1,0:T(8,128)S(1)} %get-tuple-element.40), channel_id=1, source_target_pairs={{0,2},{1,9},{2,0},{3,11},{4,6},{5,13},{6,4},{7,15},{8,10},{9,1},{1... | collective-permute-start | bytes 1572872 | tf_op jit(solution)/shard_map/ppermute | solution.py:354
  29.7 12.1 %collective-permute-start.6 = (f32[2,4,2,8,8,128]{5,4,3,2,1,0:T(8,128)S(1)}, f32[2,4,2,8,8,128]{5,4,3,2,1,0:T(8,128)S(1)}, u32[]{:S(2)}, u32[]{:S(2)}) collective-permute-start(f32[2,4,2,8,8,128]{5,4,3,2,1,0:T(8,128)S(1)} %get-tuple-element.38), channel_id=1, source_target_pairs={{0,6},{1,25},{2,4},{3,27},{4,2},{5,29},{6,0},{7,31},{8,14},{9,17},... | collective-permute-start | bytes 1572872 | tf_op jit(solution)/shard_map/ppermute | solution.py:354
  37.5 7.8 %collective-permute-start.4 = (f32[1,4,2,8,8,128]{5,4,3,2,1,0:T(8,128)S(1)}, f32[1,4,2,8,8,128]{5,4,3,2,1,0:T(8,128)S(1)}, u32[]{:S(2)}, u32[]{:S(2)}) collective-permute-start(f32[1,4,2,8,8,128]{5,4,3,2,1,0:T(8,128)S(1)} %slice_add_fusion.10), channel_id=1, source_target_pairs={{0,6},{1,25},{2,4},{3,27},{4,2},{5,29},{6,0},{7,31},{8,14},{9,17},... | collective-permute-start | bytes 786440 | tf_op jit(solution)/shard_map/ppermute | solution.py:354
  41.9 8.0 %collective-permute-start.7 = (f32[1,4,2,8,8,128]{5,4,3,2,1,0:T(8,128)S(1)}, f32[1,4,2,8,8,128]{5,4,3,2,1,0:T(8,128)S(1)}, u32[]{:S(2)}, u32[]{:S(2)}) collective-permute-start(f32[1,4,2,8,8,128]{5,4,3,2,1,0:T(8,128)S(1)} %slice_add_fusion.8), channel_id=1, source_target_pairs={{0,2},{1,9},{2,0},{3,11},{4,6},{5,13},{6,4},{7,15},{8,10},{9,1},{1... | collective-permute-start | bytes 786440 | tf_op jit(solution)/shard_map/ppermute | solution.py:354
  42.0 10.2 %collective-permute-start.11 = (f32[2,4,8,8,128]{4,3,2,1,0:T(8,128)S(1)}, f32[2,4,8,8,128]{4,3,2,1,0:T(8,128)S(1)}, u32[]{:S(2)}, u32[]{:S(2)}) collective-permute-start(f32[2,4,8,8,128]{4,3,2,1,0:T(8,128)S(1)} %slice_bitcast_fusion), channel_id=1, source_target_pairs={{0,8},{1,3},{2,10},{3,1},{4,12},{5,7},{6,14},{7,5},{8,0},{9,11},{1... | collective-permute-start | bytes 786440 | tf_op jit(solution)/shard_map/ppermute | solution.py:354
  50.0 7.7 %collective-permute-start.8 = (f32[2,4,8,8,128]{4,3,2,1,0:T(8,128)S(1)}, f32[2,4,8,8,128]{4,3,2,1,0:T(8,128)S(1)}, u32[]{:S(2)}, u32[]{:S(2)}) collective-permute-start(f32[2,4,8,8,128]{4,3,2,1,0:T(8,128)S(1)} %fusion.1), channel_id=1, source_target_pairs={{0,24},{1,7},{2,26},{3,5},{4,28},{5,3},{6,30},{7,1},{8,16},{9,15},... | collective-permute-start | bytes 786440 | tf_op jit(solution)/shard_map/ppermute | solution.py:354
  52.3 6.8 %collective-permute-start.12 = (f32[1,4,8,8,128]{4,3,2,1,0:T(8,128)S(1)}, f32[1,4,8,8,128]{4,3,2,1,0:T(8,128)S(1)}, u32[]{:S(2)}, u32[]{:S(2)}) collective-permute-start(f32[1,4,8,8,128]{4,3,2,1,0:T(8,128)S(1)} %slice_add_fusion.12), channel_id=1, source_target_pairs={{0,24},{1,7},{2,26},{3,5},{4,28},{5,3},{6,30},{7,1},{8,16},{9,15},... | collective-permute-start | bytes 393224 | tf_op jit(solution)/shard_map/ppermute | solution.py:354
  57.7 5.1 %collective-permute-start.9 = (f32[1,4,8,8,128]{4,3,2,1,0:T(8,128)S(1)}, f32[1,4,8,8,128]{4,3,2,1,0:T(8,128)S(1)}, u32[]{:S(2)}, u32[]{:S(2)}) collective-permute-start(f32[1,4,8,8,128]{4,3,2,1,0:T(8,128)S(1)} %slice_add_fusion.14), channel_id=1, source_target_pairs={{0,8},{1,3},{2,10},{3,1},{4,12},{5,7},{6,14},{7,5},{8,0},{9,11},{1... | collective-permute-start | bytes 393224 | tf_op jit(solution)/shard_map/ppermute | solution.py:354
  62.8 5.8 %collective-permute-start.13 = (f32[4,8,8,128]{3,2,0,1:T(8,128)S(1)}, f32[4,8,8,128]{3,2,0,1:T(8,128)S(1)}, u32[]{:S(2)}, u32[]{:S(2)}) collective-permute-start(f32[4,8,8,128]{3,2,0,1:T(8,128)S(1)} %slice.232), channel_id=1, source_target_pairs={{0,32},{1,33},{2,34},{3,35},{4,36},{5,37},{6,38},{7,39},{8,40},{9,... | collective-permute-start | bytes 393224 | tf_op jit(solution)/shard_map/ppermute | solution.py:354
  68.6 5.3 %collective-permute-start.14 = (f32[2,8,8,128]{3,2,0,1:T(8,128)S(1)}, f32[2,8,8,128]{3,2,0,1:T(8,128)S(1)}, u32[]{:S(2)}, u32[]{:S(2)}) collective-permute-start(f32[2,8,8,128]{3,2,0,1:T(8,128)S(1)} %get-tuple-element.42), channel_id=1, source_target_pairs={{0,64},{1,65},{2,66},{3,67},{4,68},{5,69},{6,70},{7,71},{8,72},{9,... | collective-permute-start | bytes 196616 | tf_op jit(solution)/shard_map/ppermute | solution.py:354
  73.8 8.4 %collective-permute-start.15 = (f32[1,8,8,128]{3,2,0,1:T(8,128)S(1)}, f32[1,8,8,128]{3,2,0,1:T(8,128)S(1)}, u32[]{:S(2)}, u32[]{:S(2)}) collective-permute-start(f32[1,8,8,128]{3,2,0,1:T(8,128)S(1)} %slice_add_fusion.18), channel_id=1, source_target_pairs={{0,192},{1,193},{2,194},{3,195},{4,196},{5,197},{6,198},{7,199},{8... | collective-permute-start | bytes 98312 | tf_op jit(solution)/shard_map/ppermute | solution.py:354

commit v5 on v4

v5 whole, which is shorter than its diff:
```python
import functools

import jax
import jax.numpy as jnp
from jax import lax
from jax.experimental import pallas as pl
from jax.experimental.pallas import tpu as pltpu
from jax.sharding import PartitionSpec as P

F32 = jnp.float32
BF16 = jnp.bfloat16
NX, NY, NZ = 4, 4, 8
SEGS = 64
ROWS = 16
WIDTH = 512
TAPS = 21
REACH = 10
NBASIS = 3
LANES = 128
BLOCKS = WIDTH // LANES
HALF = WIDTH // 2
BLOCK_SEGS = 16
BLOCK_ROWS = BLOCK_SEGS * ROWS


def split(value):
    high = value.astype(BF16)
    return high, (value - high.astype(F32)).astype(BF16)


def column_factor(bits):
    bad = (bits & 1).astype(F32)
    full = ((bits >> 1) & 1).astype(F32)
    cosmic = ((bits >> 2) & 1).astype(F32)
    return (1.0 - bad) * (1.0 - 0.75 * full) * (1.0 - 0.5 * cosmic)


def column_warp(base, frac):
    source = lax.broadcasted_iota(jnp.int32, (WIDTH, base.shape[1]), 0)
    return jnp.where(source == base, 1.0 - frac, 0.0) + jnp.where(source == base + 1, frac, 0.0)


def column_of(ref, shape):
    row = lax.broadcasted_iota(jnp.int32, shape, 0)
    result = jnp.full(shape, ref[0, 0])
    for i in range(1, ROWS):
        result = jnp.where(row == i, ref[0, i], result)
    return result


A_FIRST = (0, 3, 1, 2)
B_FIRST = (0, 1, 3, 2)
U_ORDER = (A_FIRST, B_FIRST)
Z_ORDER = (0, 4, 2, 6, 1, 5, 3, 7)


def own_place():
    sky = lax.axis_index("sky")
    grp = lax.axis_index("grp")
    return grp % 2, grp // 2, sky % NY, sky // NY


def relative_patch(place, owner):
    ry = (owner % NY) ^ place[2]
    rz = (owner // NY) ^ place[3]
    return ry, (rz & 1) * 4 + ((rz >> 1) & 1) * 2 + (rz >> 2)


def write_out(place, sums, keep, send, sems, u_order):
    copies = []
    for to, core in ((keep, place[0]), (send, 1 - place[0])):
        for pu, ru in enumerate(u_order):
            for rv in range(4):
                rx = ru + core * (rv - ru)
                ry = rv + core * (ru - rv)
                rows = pl.ds(pl.multiple_of(((place[1] ^ rx) * 2 + core) * 8, 8), 8)
                copies.append(pltpu.make_async_copy(sums.at[:, ry, :, rows, :], to.at[pu, rv], sems.at[len(copies)]))
    for copy in copies:
        copy.start()
    return copies


def fetch(pairs, sems):
    copies = [pltpu.make_async_copy(src, dst, sems.at[i]) for i, (src, dst) in enumerate(pairs)]
    for copy in copies:
        copy.start()
    return copies


def denom_kernel(
    owner_hbm, offset_hbm, weight_hbm, bank_hbm, index_hbm, coeff_hbm, base_hbm, frac_hbm, bits_hbm,
    col_base_hbm, col_frac_hbm, pixels_hbm,
    keep, send, pixels_ref, factor_ref, blockdiag, profiles, warp_high, warp_low,
    owner_ref, offset_ref, weight_ref, bank_ref, index_ref, coeff_ref, base_ref, frac_ref, bits_ref,
    col_base_ref, col_frac_ref, sums, cover, sems, out_sems,
):
    place = own_place()
    inputs = fetch(
        (
            (owner_hbm, owner_ref), (offset_hbm, offset_ref), (weight_hbm, weight_ref),
            (frac_hbm, frac_ref), (bits_hbm, bits_ref), (col_base_hbm, col_base_ref), (col_frac_hbm, col_frac_ref),
            (bank_hbm, bank_ref), (index_hbm, index_ref), (coeff_hbm, coeff_ref), (base_hbm, base_ref),
            (pixels_hbm, pixels_ref),
        ),
        sems,
    )
    sums[...] = jnp.zeros(sums.shape, F32)
    for copy in inputs[:7]:
        copy.wait()
    factor = column_factor(bits_ref[0])
    factor_ref[...] = factor
    high, low = split(column_warp(col_base_ref[...], col_frac_ref[...]))
    warp_high[...] = high
    warp_low[...] = low
    factor = factor.astype(BF16)
    coverage = jnp.dot(factor, high, preferred_element_type=F32) + jnp.dot(factor, low, preferred_element_type=F32)
    for block in range(BLOCKS):
        cover[block] = coverage[:, block * LANES : (block + 1) * LANES]
    frac = column_of(frac_ref, (ROWS, LANES))
    spread = (1.0 - frac) + frac

    def one(s, carry):
        ry, rz = relative_patch(place, owner_ref[0, s])
        rows = pl.ds(offset_ref[0, s], ROWS)
        share = spread * weight_ref[0, s]
        for block in range(BLOCKS):
            sums[block, ry, rz, rows, :] += share * cover[block, pl.ds(s, 1), :]
        return carry

    lax.fori_loop(0, SEGS, one, 0, unroll=4)
    outputs = []
    for half in range(2):
        part = sums.at[2 * half : 2 * half + 2]
        outputs += write_out(place, part, keep.at[half], send.at[half], out_sems.at[half], U_ORDER[half])
    for copy in inputs[7:]:
        copy.wait()
    same = (
        lax.broadcasted_iota(jnp.int32, (BLOCK_ROWS, BLOCK_ROWS), 0) // ROWS
        == lax.broadcasted_iota(jnp.int32, (BLOCK_ROWS, BLOCK_ROWS), 1) // ROWS
    )
    for k in range(NBASIS):
        table = row_tables(bank_ref, index_ref, coeff_ref, base_ref, frac_ref, k)
        whole = jnp.where(same, jnp.concatenate([table] * BLOCK_SEGS, axis=0), 0.0)
        high, low = split(whole)
        rows = slice(k * BLOCK_ROWS, (k + 1) * BLOCK_ROWS)
        blockdiag[rows, 0:BLOCK_ROWS] = high
        blockdiag[rows, BLOCK_ROWS : 2 * BLOCK_ROWS] = high
        blockdiag[rows, 2 * BLOCK_ROWS :] = low
        profiles[k] = profile_row(bank_ref, index_ref, k)
    for copy in outputs:
        copy.wait()


def row_tables(bank_ref, index_ref, coeff_ref, base_ref, frac_ref, k):
    shape = (ROWS, BLOCK_ROWS)
    delta = lax.broadcasted_iota(jnp.int32, shape, 1) % ROWS - column_of(base_ref, shape) + REACH
    frac = column_of(frac_ref, shape)
    term = index_ref[0, k]
    lower = jnp.zeros(shape, F32)
    higher = jnp.zeros(shape, F32)
    for tap in range(TAPS):
        value = bank_ref[term, 0, tap]
        lower = jnp.where(delta == tap, value, lower)
        higher = jnp.where(delta == tap + 1, value, higher)
    return ((1.0 - frac) * lower + frac * higher) * coeff_ref[0, k]


def profile_row(bank_ref, index_ref, k):
    lane = lax.broadcasted_iota(jnp.int32, (8, WIDTH), 1)
    term = index_ref[0, k]
    row = jnp.zeros((8, WIDTH), F32)
    for tap in range(TAPS):
        row = jnp.where(lane == LANES + REACH - tap, bank_ref[term, 1, tap], row)
    return row


def band_tables(profile):
    return pltpu.roll(jnp.concatenate([profile] * (LANES // 8), axis=0), 0, 1, stride=1, stride_axis=0)[:, : 3 * LANES]


def rows_kernel(
    pixels_ref, factor_ref, blockdiag, profiles, u_high, u_low, near_high, near_low, cross_high, cross_low, done
):
    cross_high[...] = jnp.zeros(cross_high.shape, BF16)
    cross_low[...] = jnp.zeros(cross_low.shape, BF16)
    for k in range(NBASIS):
        for near, cross, band in zip(
            (near_high, near_low), (cross_high, cross_low), split(band_tables(profiles[k]))
        ):
            top = slice(k * HALF, k * HALF + LANES)
            bottom = slice(k * HALF + LANES, (k + 1) * HALF)
            left, middle, right = (band[:, i * LANES : (i + 1) * LANES] for i in range(3))
            near[top, :LANES] = middle
            near[top, LANES:] = right
            near[bottom, :LANES] = left
            near[bottom, LANES:] = middle
            cross[top, LANES:] = right
            cross[bottom, :LANES] = left
    def one(b, carry):
        segs = pl.ds(b * BLOCK_SEGS, BLOCK_SEGS)
        masked = (pixels_ref[0, segs] * factor_ref[segs, :][:, None, :]).reshape(BLOCK_ROWS, WIDTH)
        high, low = split(masked)
        product = jnp.dot(
            blockdiag[...], jnp.concatenate([high, low, high], axis=0), preferred_element_type=F32
        )
        rows = pl.ds(pl.multiple_of(b * BLOCK_ROWS, BLOCK_ROWS), BLOCK_ROWS)
        for k in range(NBASIS):
            part_high, part_low = split(product[k * BLOCK_ROWS : (k + 1) * BLOCK_ROWS])
            for half in range(2):
                of = slice(half * HALF, (half + 1) * HALF)
                u_high[half, rows, k * HALF : (k + 1) * HALF] = part_high[:, of]
                u_low[half, rows, k * HALF : (k + 1) * HALF] = part_low[:, of]
        return carry

    lax.fori_loop(0, SEGS // BLOCK_SEGS, one, 0, unroll=True)
    done[...] = jnp.zeros(done.shape, F32)


def put(place, owner_ref, offset_ref, weight_ref, lifted, first, sums):
    def one(s, carry):
        ry, rz = relative_patch(place, owner_ref[0, s])
        rows = pl.ds(offset_ref[0, s], ROWS)
        weight = weight_ref[0, s]
        of = pl.ds(pl.multiple_of(s * ROWS, ROWS), ROWS)
        for block in range(2):
            sums[block, ry, rz, rows, :] += weight * lifted[first + block, of, :]
        return carry

    lax.fori_loop(0, SEGS, one, 0, unroll=4)


def numer_kernel(
    owner_ref, offset_ref, weight_ref, warp_high, warp_low, u_high, u_low, near_high, near_low, cross_high, cross_low,
    after_0, after_1, keep, send, lifted, sums, y_high, y_low, sems,
):
    place = own_place()
    sums[...] = jnp.zeros(sums.shape, F32)
    dot = functools.partial(jnp.dot, preferred_element_type=F32)

    def one(b, carry):
        rows = pl.ds(pl.multiple_of(b * BLOCK_ROWS, BLOCK_ROWS), BLOCK_ROWS)
        part_high = u_high[:, rows, :].reshape(2 * BLOCK_ROWS, NBASIS * HALF)
        part_low = u_low[:, rows, :].reshape(2 * BLOCK_ROWS, NBASIS * HALF)
        near = dot(part_high, near_high[...]) + dot(part_high, near_low[...]) + dot(part_low, near_high[...])
        border_high, border_low = (
            jnp.concatenate(
                [
                    u[half, rows, k * HALF + (1 - half) * LANES : k * HALF + (2 - half) * LANES]
                    for k in range(NBASIS)
                    for half in range(2)
                ],
                axis=1,
            )
            for u in (u_high, u_low)
        )
        cross = (
            dot(border_high, cross_high[...]) + dot(border_high, cross_low[...]) + dot(border_low, cross_high[...])
        )
        left, right = near[:BLOCK_ROWS], near[BLOCK_ROWS:]
        wide = jnp.concatenate(
            [left[:, :LANES], left[:, LANES:] + cross[:, :LANES], right[:, :LANES] + cross[:, LANES:], right[:, LANES:]],
            axis=1,
        )
        high, low = split(wide)
        y_high[rows, :] = high
        y_low[rows, :] = low
        return carry

    lax.fori_loop(0, SEGS * ROWS // BLOCK_ROWS, one, 0, unroll=True)
    for half in range(2):
        cols = slice(half * HALF, (half + 1) * HALF)
        warped = (
            dot(y_high[...], warp_high[:, cols]) + dot(y_high[...], warp_low[:, cols])
            + dot(y_low[...], warp_high[:, cols])
        )
        lifted[2 * half] = warped[:, :LANES]
        lifted[2 * half + 1] = warped[:, LANES:]

    put(place, owner_ref, offset_ref, weight_ref, lifted, 0, sums)
    for copy in write_out(place, sums, keep, send, sems, U_ORDER[0]):
        copy.wait()


def second_kernel(owner_ref, offset_ref, weight_ref, lifted, keep, send, sums, sems):
    place = own_place()
    sums[...] = jnp.zeros(sums.shape, F32)
    put(place, owner_ref, offset_ref, weight_ref, lifted, 2, sums)
    for copy in write_out(place, sums, keep, send, sems, U_ORDER[1]):
        copy.wait()


SMEM = pl.BlockSpec(memory_space=pltpu.SMEM)
VMEM = pl.BlockSpec(memory_space=pltpu.VMEM)
ANY = pl.BlockSpec(memory_space=pl.ANY)
HBM = pl.BlockSpec(memory_space=pltpu.HBM)
TOKEN = jax.ShapeDtypeStruct((8, LANES), F32)
PARAMS = pltpu.CompilerParams(vmem_limit_bytes=40 * 1024 * 1024)


def pinned(*values):
    return [pltpu.with_memory_space_constraint(value, pltpu.HBM) for value in values]


def denom_sums(owner, offset, weight, bank, index, coeff, row_base, row_frac, bits, col_base, col_frac, pixels):
    parts = jax.ShapeDtypeStruct((2, 4, 4, 2, NZ, 8, LANES), F32)
    warp = jax.ShapeDtypeStruct((WIDTH, WIDTH), BF16)
    small = (owner, offset, weight, bank, index, coeff, row_base, row_frac)
    return pl.pallas_call(
        denom_kernel,
        out_shape=(
            parts, parts, jax.ShapeDtypeStruct(pixels.shape, F32), jax.ShapeDtypeStruct((SEGS, WIDTH), F32),
            jax.ShapeDtypeStruct((NBASIS * BLOCK_ROWS, 3 * BLOCK_ROWS), BF16),
            jax.ShapeDtypeStruct((NBASIS, 8, WIDTH), F32), warp, warp,
        ),
        in_specs=[HBM] * 12,
        out_specs=(ANY,) * 2 + (VMEM,) * 6,
        scratch_shapes=[pltpu.SMEM(value.shape, value.dtype) for value in small]
        + [pltpu.VMEM(value.shape, value.dtype) for value in (bits, col_base, col_frac)]
        + [
            pltpu.VMEM((BLOCKS, NY, NZ, 64, LANES), F32), pltpu.VMEM((BLOCKS, SEGS, LANES), F32),
            pltpu.SemaphoreType.DMA((12,)), pltpu.SemaphoreType.DMA((2, 32)),
        ],
        compiler_params=PARAMS,
        cost_estimate=pl.CostEstimate(flops=10**3, bytes_accessed=10**3, transcendentals=0),
        name="denom_sums",
    )(*(pltpu.with_memory_space_constraint(v, pltpu.HBM) for v in (*small, bits, col_base, col_frac, pixels)))


def row_pass(pixels, factor, blockdiag, profiles):
    band = jax.ShapeDtypeStruct((NBASIS * HALF, HALF), BF16)
    wide = jax.ShapeDtypeStruct((2, SEGS * ROWS, NBASIS * HALF), BF16)
    return pl.pallas_call(
        rows_kernel,
        out_shape=(wide, wide, band, band, band, band, TOKEN),
        in_specs=[VMEM] * 4,
        out_specs=(VMEM,) * 7,
        compiler_params=PARAMS,
        cost_estimate=pl.CostEstimate(flops=10**3, bytes_accessed=10**3, transcendentals=0),
        name="row_pass",
    )(pixels, factor, blockdiag, profiles)


PARTS = jax.ShapeDtypeStruct((4, 4, 2, NZ, 8, LANES), F32)
SUMS = pltpu.VMEM((2, NY, NZ, 64, LANES), F32)


def numer_sums(owner, offset, weight, warp, tables, after):
    wide = pltpu.VMEM((SEGS * ROWS, WIDTH), BF16)
    return pl.pallas_call(
        numer_kernel,
        out_shape=(PARTS, PARTS, jax.ShapeDtypeStruct((BLOCKS, SEGS * ROWS, LANES), F32)),
        in_specs=[SMEM] * 3 + [VMEM] * 10,
        out_specs=(ANY, ANY, VMEM),
        scratch_shapes=[SUMS, wide, wide, pltpu.SemaphoreType.DMA((32,))],
        compiler_params=PARAMS,
        cost_estimate=pl.CostEstimate(flops=10**3, bytes_accessed=10**3, transcendentals=0),
        name="numer_sums",
    )(owner, offset, weight, *warp, *tables, *after)


def second_sums(owner, offset, weight, lifted):
    return pl.pallas_call(
        second_kernel,
        out_shape=(PARTS, PARTS),
        in_specs=[SMEM] * 3 + [VMEM],
        out_specs=(ANY, ANY),
        scratch_shapes=[SUMS, pltpu.SemaphoreType.DMA((32,))],
        compiler_params=PARAMS,
        cost_estimate=pl.CostEstimate(flops=10**3, bytes_accessed=10**3, transcendentals=0),
        name="second_sums",
    )(owner, offset, weight, lifted)


def permute(value, partner):
    pairs = []
    for z in range(NZ):
        for y in range(NY):
            for x in range(NX):
                for core in range(2):
                    to_core, to_x, to_y, to_z = partner(core, x, y, z)
                    source = (z * NY + y) * 2 * NX + x * 2 + core
                    pairs.append((source, (to_z * NY + to_y) * 2 * NX + to_x * 2 + to_core))
    return lax.ppermute(value, ("sky", "grp"), pairs)


def swap_core(value):
    return permute(value, lambda core, x, y, z: (1 - core, x, y, z))


def swap_u(value, step):
    return permute(value, lambda core, x, y, z: (core, x, y ^ step, z) if core else (core, x ^ step, y, z))


def swap_v(value, step):
    return permute(value, lambda core, x, y, z: (core, x ^ step, y, z) if core else (core, x, y ^ step, z))


def swap_z(value, step):
    return permute(value, lambda core, x, y, z: (core, x, y, z ^ step))


def halve(keep, got):
    middle = keep.shape[0] // 2
    return keep[:middle] + got[:middle], keep[middle:] + got[middle:]


def hold(values, after):
    def kernel(*refs):
        pass

    return pl.pallas_call(
        kernel,
        out_shape=tuple(jax.ShapeDtypeStruct(value.shape, value.dtype) for value in values),
        in_specs=[VMEM] * (len(values) + len(after)),
        out_specs=(VMEM,) * len(values),
        input_output_aliases={i: i for i in range(len(values))},
        compiler_params=PARAMS,
        name="hold",
    )(*values, *after)


def per_device(
    pixels, mask_bits, owner, row_offset, seg_weight, psf_bank, basis_index, basis_coeff,
    row_base, row_frac, col_base, col_frac,
):
    d_keep, d_send, pixels, factor, blockdiag, profiles, *warp = denom_sums(
        owner, row_offset, seg_weight, psf_bank, basis_index, basis_coeff, row_base, row_frac,
        mask_bits, col_base, col_frac, pixels,
    )
    *tables, done = row_pass(pixels, factor, blockdiag, profiles)
    (d_got,) = hold((swap_core(d_send),), (done,))
    d_parts = [halve(d_keep[half], d_got[half]) for half in range(2)]
    keep_0, send_0, lifted = numer_sums(
        owner, row_offset, seg_weight, warp, tables, [send for _, send in d_parts]
    )
    keep_1, send_1 = second_sums(owner, row_offset, seg_weight, lifted)
    d_parts = [halve(keep, swap_u(send, step)) for (keep, send), step in zip(d_parts, (1, 3))]
    (send_1,) = hold((send_1,), [send for _, send in d_parts])
    n_parts = [halve(keep, swap_core(send)) for keep, send in ((keep_0, send_0), (keep_1, send_1))]
    d_parts = [keep[0] + swap_u(send, step)[0] for (keep, send), step in zip(d_parts, (3, 1))]
    n_parts = [halve(keep, swap_u(send, step)) for (keep, send), step in zip(n_parts, (1, 3))]
    n_parts = [keep[0] + swap_u(send, step)[0] for (keep, send), step in zip(n_parts, (3, 1))]
    both = jnp.concatenate(n_parts + d_parts, axis=1)
    both = both[0] + swap_v(both[1], 1) + swap_v(both[3], 3) + swap_v(both[2], 2)
    both = jnp.swapaxes(both, 0, 1)
    keep, send = halve(both[:4], swap_z(both[4:], 1))
    keep, send = halve(keep, swap_z(send, 2))
    both = (keep + swap_z(send, 4))[0]
    coadd = both[:BLOCKS] / jnp.maximum(both[BLOCKS:], 1.0)
    return jnp.swapaxes(coadd, 0, 1).reshape(8, WIDTH)


def solution(mesh):
    placed = (
        P("grp", "sky", None, None),
        P("grp", "sky", None),
        P("grp", "sky"),
        P("grp", "sky"),
        P("grp", "sky"),
        P(),
        P("grp", None),
        P("grp", None),
        P("grp", None),
        P("grp", None),
        P("grp", None),
        P("grp", None),
    )
    return jax.shard_map(
        per_device, mesh=mesh, in_specs=placed, out_specs=P(("sky", "grp"), None), check_vma=False
    )
```

time: 83.1 us -> 78.8 us (0.948)
  Pallas kernels: 22.5 us -> 16.9 us
  starting transfers between devices: 24 us -> 29.6 us
  waiting for transfers between devices: 33.6 us -> 29.6 us
    ppermute x16 -> x17, starting transfers between devices: 24 us -> 29.6 us  [permute(): return lax.ppermute(value, ('sky', 'grp'), pairs)]
    pallas_call x5 -> x4, Pallas kernels: 22.5 us -> 16.9 us  [the longest x1 7.66 us: numer_sums(): pl.pallas_call(numer_kernel, out_shape=(PARTS, PARTS, jax.ShapeDtypeStruc...]
    ppermute x16 -> x17, waiting for transfers between devices: 33.6 us -> 29.6 us  [permute(): return lax.ppermute(value, ('sky', 'grp'), pairs)]
  transfers between devices with their start and end apart: 16 -> 17, of which waited for: 13 -> 13; matrix products, arithmetic and copies ran while one was open for 1% -> 1% of each run, Pallas kernels for 23% -> 16%
where the time goes in v5:
time: 78.8 us; the launch traced here: 78.2 us
  starting transfers between devices  29.6 us (38%)
  waiting for transfers between devices  29.6 us (38%)
  Pallas kernels  16.9 us (21%)
  other arithmetic  1.86 us (2%)
    ppermute x17, waiting for transfers between devices, permute(): return lax.ppermute(value, ('sky', 'grp'), pairs)  29.6 us
    ppermute x17, starting transfers between devices, permute(): return lax.ppermute(value, ('sky', 'grp'), pairs)  29.6 us
    pallas_call x1, Pallas kernels, numer_sums(): pl.pallas_call(numer_kernel, out_shape=(PARTS, PARTS, jax.ShapeDtypeStruc...  7.66 us
    pallas_call x1, Pallas kernels, denom_sums(): pl.pallas_call(denom_kernel, out_shape=(parts, parts, jax.ShapeDtypeStruc...  4.27 us
    pallas_call x1, Pallas kernels, row_pass(): pl.pallas_call(rows_kernel, out_shape=(wide, wide, band, band, band, band...  2.75 us
    pallas_call x1, Pallas kernels, second_sums(): pl.pallas_call(second_kernel, out_shape=(PARTS, PARTS), in_specs=[SMEM] *...  2.21 us
  transfers between devices with their start and end apart: 17, of which 13 were waited for; matrix products, arithmetic and copies ran while one was open for 1% of the time, Pallas kernels for 16%

profile of v5, /device:TPU:6, one launch (start us, length us, event | category | flops | bytes accessed | tf_op | source)
XLA Modules:
  0.0 78.2 jit_solution(4777893174620365285)
XLA Ops:
  0.0 4.3 %denom_sums.1 = (f32[2,4,4,2,8,8,128]{6,5,4,3,2,1,0:T(8,128)S(1)}, f32[2,4,4,2,8,8,128]{6,5,4,3,2,1,0:T(8,128)S(1)}, f32[1,64,16,512]{3,2,1,0:T(8,128)S(1)}, f32...) custom-call(s32[1,64]{1,0:T(1,128)} %owner_ref.3, ...), custom_call_target="tpu_custom_call" | custom-call | flops 1000 | bytes 1000 | tf_op jit(solution)/shard_map/denom_sums/pallas_call | solution.py:308
  4.4 2.8 %row_pass.1 = (bf16[2,1024,768]{2,1,0:T(8,128)(2,1)S(1)}, bf16[2,1024,768]{2,1,0:T(8,128)(2,1)S(1)}, bf16[768,256]{1,0:T(8,128)(2,1)S(1)}, bf16[768,256]{1,0:T(8...) custom-call(f32[1,64,16,512]{3,2,1,0:T(8,128)S(1)} %get-tuple-element.27.pixels_ref, ...), custom_call_target="tpu_custom_call" | custom-call | flops 1000 | bytes 1000 | tf_op jit(solution)/shard_map/row_pass/pallas_call | solution.py:332
  7.1 1.4 %collective-permute-done.refs_0_ = f32[2,4,4,2,8,8,128]{6,5,4,3,2,1,0:T(8,128)S(1)} collective-permute-done((f32[2,4,4,2,8,8,128]{6,5,4,3,2,1,0:T(8,128)S(1)}, f32[2,4,4,2,8,8,128]{6,5,4,3,2,1,0:T(8,128)S(1)}, u32[]{:S(2)}, u32[]{:S(2)}) %collective-permute-start) | collective-permute-done | bytes 2097184 | tf_op jit(solution)/shard_map/ppermute | solution.py:383
  8.5 0.4 slice_add_fusion.3
  8.9 2.3 %collective-permute-start.5 = (f32[2,4,2,8,8,128]{5,4,3,2,1,0:T(8,128)S(1)}, f32[2,4,2,8,8,128]{5,4,3,2,1,0:T(8,128)S(1)}, u32[]{:S(2)}, u32[]{:S(2)}) collective-permute-start(f32[2,4,2,8,8,128]{5,4,3,2,1,0:T(8,128)S(1)} %get-tuple-element.47.after_1), channel_id=1, source_target_pairs={{0,6},{1,25},{2,4},{3,27},{4,2},{5,29},{6,0},{7,31},{8,14},{9,17},... | collective-permute-start | bytes 1572872 | tf_op jit(solution)/shard_map/ppermute | solution.py:383
  11.2 7.7 %numer_sums.1 = (f32[4,4,2,8,8,128]{5,4,3,2,1,0:T(8,128)S(1)}, f32[4,4,2,8,8,128]{5,4,3,2,1,0:T(8,128)S(1)}, f32[4,1024,128]{2,1,0:T(8,128)S(1)}) custom-call(s32[1,64]{1,0:T(1,128)S(1)} %copy-done, s32[1,64]{1,0:T(1,128)S(1)} %copy-done.1, f32[1,64]{1,0:T(1,128)S(1)} %copy-done.2, bf16[512,512]{1,0:T(8,128)(2,1)S(1)} %get-tuple-element.25.warp_high, ...), custom_call_target="tpu_custom_call" | custom-call | flops 1000 | bytes 1000 | tf_op jit(solution)/shard_map/numer_sums/pallas_call | solution.py:349
  18.9 0.9 %collective-permute-start.1 = (f32[4,4,2,8,8,128]{5,4,3,2,1,0:T(8,128)S(1)}, f32[4,4,2,8,8,128]{5,4,3,2,1,0:T(8,128)S(1)}, u32[]{:S(2)}, u32[]{:S(2)}) collective-permute-start(f32[4,4,2,8,8,128]{5,4,3,2,1,0:T(8,128)S(1)} %get-tuple-element.41), channel_id=1, source_target_pairs={{0,1},{1,0},{2,3},{3,2},{4,5},{5,4},{6,7},{7,6},{8,9},{9,8},{10,11... | collective-permute-start | bytes 3145736 | tf_op jit(solution)/shard_map/ppermute | solution.py:383
  19.8 2.2 %second_sums.1 = (f32[4,4,2,8,8,128]{5,4,3,2,1,0:T(8,128)S(1)}, f32[4,4,2,8,8,128]{5,4,3,2,1,0:T(8,128)S(1)}) custom-call(s32[1,64]{1,0:T(1,128)S(1)} %copy-done, s32[1,64]{1,0:T(1,128)S(1)} %copy-done.1, f32[1,64]{1,0:T(1,128)S(1)} %copy-done.2, f32[4,1024,128]{2,1,0:T(8,128)S(1)} %get-tuple-element.42.lifted), custom_call_target="tpu_custom_call" | custom-call | flops 1000 | bytes 1000 | tf_op jit(solution)/shard_map/second_sums/pallas_call | solution.py:362
  22.3 1.8 %collective-permute-start.10 = (f32[1,4,2,8,8,128]{5,4,3,2,1,0:T(8,128)S(1)}, f32[1,4,2,8,8,128]{5,4,3,2,1,0:T(8,128)S(1)}, u32[]{:S(2)}, u32[]{:S(2)}) collective-permute-start(f32[1,4,2,8,8,128]{5,4,3,2,1,0:T(8,128)S(1)} %slice_add_fusion.12.refs_2_), channel_id=1, source_target_pairs={{0,2},{1,9},{2,0},{3,11},{4,6},{5,13},{6,4},{7,15},{8,10},{9,1},{1... | collective-permute-start | bytes 786440 | tf_op jit(solution)/shard_map/ppermute | solution.py:383
  24.3 0.4 collective-permute-start.2
  24.7 0.3 collective-permute-done.6
  25.1 0.8 %collective-permute-start.7 = (f32[2,4,2,8,8,128]{5,4,3,2,1,0:T(8,128)S(1)}, f32[2,4,2,8,8,128]{5,4,3,2,1,0:T(8,128)S(1)}, u32[]{:S(2)}, u32[]{:S(2)}) collective-permute-start(f32[2,4,2,8,8,128]{5,4,3,2,1,0:T(8,128)S(1)} %get-tuple-element.52), channel_id=1, source_target_pairs={{0,6},{1,25},{2,4},{3,27},{4,2},{5,29},{6,0},{7,31},{8,14},{9,17},... | collective-permute-start | bytes 1572872 | tf_op jit(solution)/shard_map/ppermute | solution.py:383
  25.9 2.5 %collective-permute-start.9 = (f32[1,4,2,8,8,128]{5,4,3,2,1,0:T(8,128)S(1)}, f32[1,4,2,8,8,128]{5,4,3,2,1,0:T(8,128)S(1)}, u32[]{:S(2)}, u32[]{:S(2)}) collective-permute-start(f32[1,4,2,8,8,128]{5,4,3,2,1,0:T(8,128)S(1)} %slice_add_fusion.13.refs_1_), channel_id=1, source_target_pairs={{0,6},{1,25},{2,4},{3,27},{4,2},{5,29},{6,0},{7,31},{8,14},{9,17},... | collective-permute-start | bytes 786440 | tf_op jit(solution)/shard_map/ppermute | solution.py:383
  28.4 0.3 collective-permute-done.10
  28.8 5.6 %collective-permute-done.2 = f32[2,4,2,8,8,128]{5,4,3,2,1,0:T(8,128)S(1)} collective-permute-done((f32[2,4,2,8,8,128]{5,4,3,2,1,0:T(8,128)S(1)}, f32[2,4,2,8,8,128]{5,4,3,2,1,0:T(8,128)S(1)}, u32[]{:S(2)}, u32[]{:S(2)}) %collective-permute-start.2) | collective-permute-done | bytes 524320 | tf_op jit(solution)/shard_map/ppermute | solution.py:383
  34.4 1.1 %collective-permute-start.3 = (f32[1,4,2,8,8,128]{5,4,3,2,1,0:T(8,128)S(1)}, f32[1,4,2,8,8,128]{5,4,3,2,1,0:T(8,128)S(1)}, u32[]{:S(2)}, u32[]{:S(2)}) collective-permute-start(f32[1,4,2,8,8,128]{5,4,3,2,1,0:T(8,128)S(1)} %slice_add_fusion.14), channel_id=1, source_target_pairs={{0,6},{1,25},{2,4},{3,27},{4,2},{5,29},{6,0},{7,31},{8,14},{9,17},... | collective-permute-start | bytes 786440 | tf_op jit(solution)/shard_map/ppermute | solution.py:383
  35.6 1.2 %collective-permute-start.8 = (f32[1,4,2,8,8,128]{5,4,3,2,1,0:T(8,128)S(1)}, f32[1,4,2,8,8,128]{5,4,3,2,1,0:T(8,128)S(1)}, u32[]{:S(2)}, u32[]{:S(2)}) collective-permute-start(f32[1,4,2,8,8,128]{5,4,3,2,1,0:T(8,128)S(1)} %slice_add_fusion.10), channel_id=1, source_target_pairs={{0,2},{1,9},{2,0},{3,11},{4,6},{5,13},{6,4},{7,15},{8,10},{9,1},{1... | collective-permute-start | bytes 786440 | tf_op jit(solution)/shard_map/ppermute | solution.py:383
  36.8 1.6 %collective-permute-done.9 = f32[1,4,2,8,8,128]{5,4,3,2,1,0:T(8,128)S(1)} collective-permute-done((f32[1,4,2,8,8,128]{5,4,3,2,1,0:T(8,128)S(1)}, f32[1,4,2,8,8,128]{5,4,3,2,1,0:T(8,128)S(1)}, u32[]{:S(2)}, u32[]{:S(2)}) %collective-permute-start.9) | collective-permute-done | bytes 262176 | tf_op jit(solution)/shard_map/ppermute | solution.py:383
  38.5 3.6 %collective-permute-done.3 = f32[1,4,2,8,8,128]{5,4,3,2,1,0:T(8,128)S(1)} collective-permute-done((f32[1,4,2,8,8,128]{5,4,3,2,1,0:T(8,128)S(1)}, f32[1,4,2,8,8,128]{5,4,3,2,1,0:T(8,128)S(1)}, u32[]{:S(2)}, u32[]{:S(2)}) %collective-permute-start.3) | collective-permute-done | bytes 262176 | tf_op jit(solution)/shard_map/ppermute | solution.py:383
  42.3 1.8 %collective-permute-start.11 = (f32[8,8,8,128]{3,2,1,0:T(8,128)S(1)}, f32[8,8,8,128]{3,2,1,0:T(8,128)S(1)}, u32[]{:S(2)}, u32[]{:S(2)}) collective-permute-start(f32[8,8,8,128]{3,2,1,0:T(8,128)S(1)} %get-tuple-element.53), channel_id=1, source_target_pairs={{0,8},{1,3},{2,10},{3,1},{4,12},{5,7},{6,14},{7,5},{8,0},{9,11},{1... | collective-permute-start | bytes 786440 | tf_op jit(solution)/shard_map/ppermute | solution.py:383
  44.1 2.6 %collective-permute-start.13 = (f32[8,8,8,128]{3,2,1,0:T(8,128)S(1)}, f32[8,8,8,128]{3,2,1,0:T(8,128)S(1)}, u32[]{:S(2)}, u32[]{:S(2)}) collective-permute-start(f32[8,8,8,128]{3,2,1,0:T(8,128)S(1)} %get-tuple-element.54), channel_id=1, source_target_pairs={{0,16},{1,5},{2,18},{3,7},{4,20},{5,1},{6,22},{7,3},{8,24},{9,13},... | collective-permute-start | bytes 786440 | tf_op jit(solution)/shard_map/ppermute | solution.py:383
  46.7 0.4 collective-permute-start.12
  47.1 1.7 %collective-permute-done.11 = f32[8,8,8,128]{3,2,1,0:T(8,128)S(1)} collective-permute-done((f32[8,8,8,128]{3,2,1,0:T(8,128)S(1)}, f32[8,8,8,128]{3,2,1,0:T(8,128)S(1)}, u32[]{:S(2)}, u32[]{:S(2)}) %collective-permute-start.11) | collective-permute-done | bytes 262176 | tf_op jit(solution)/shard_map/ppermute | solution.py:383
  48.8 5.2 %collective-permute-done.13 = f32[8,8,8,128]{3,2,1,0:T(8,128)S(1)} collective-permute-done((f32[8,8,8,128]{3,2,1,0:T(8,128)S(1)}, f32[8,8,8,128]{3,2,1,0:T(8,128)S(1)}, u32[]{:S(2)}, u32[]{:S(2)}) %collective-permute-start.13) | collective-permute-done | bytes 262176 | tf_op jit(solution)/shard_map/ppermute | solution.py:383
  54.0 2.7 %collective-permute-done.12 = f32[8,8,8,128]{3,2,1,0:T(8,128)S(1)} collective-permute-done((f32[8,8,8,128]{3,2,1,0:T(8,128)S(1)}, f32[8,8,8,128]{3,2,1,0:T(8,128)S(1)}, u32[]{:S(2)}, u32[]{:S(2)}) %collective-permute-start.12) | collective-permute-done | bytes 262176 | tf_op jit(solution)/shard_map/ppermute | solution.py:383
  56.8 2.0 %collective-permute-start.14 = (f32[4,8,8,128]{3,2,0,1:T(8,128)S(1)}, f32[4,8,8,128]{3,2,0,1:T(8,128)S(1)}, u32[]{:S(2)}, u32[]{:S(2)}) collective-permute-start(f32[4,8,8,128]{3,2,0,1:T(8,128)S(1)} %slice.258), channel_id=1, source_target_pairs={{0,32},{1,33},{2,34},{3,35},{4,36},{5,37},{6,38},{7,39},{8,40},{9,... | collective-permute-start | bytes 393224 | tf_op jit(solution)/shard_map/ppermute | solution.py:383
  58.8 3.0 %collective-permute-done.14 = f32[4,8,8,128]{3,2,0,1:T(8,128)S(1)} collective-permute-done((f32[4,8,8,128]{3,2,0,1:T(8,128)S(1)}, f32[4,8,8,128]{3,2,0,1:T(8,128)S(1)}, u32[]{:S(2)}, u32[]{:S(2)}) %collective-permute-start.14) | collective-permute-done | bytes 131104 | tf_op jit(solution)/shard_map/ppermute | solution.py:383
  61.8 4.0 %collective-permute-start.15 = (f32[2,8,8,128]{3,2,0,1:T(8,128)S(1)}, f32[2,8,8,128]{3,2,0,1:T(8,128)S(1)}, u32[]{:S(2)}, u32[]{:S(2)}) collective-permute-start(f32[2,8,8,128]{3,2,0,1:T(8,128)S(1)} %get-tuple-element.57), channel_id=1, source_target_pairs={{0,64},{1,65},{2,66},{3,67},{4,68},{5,69},{6,70},{7,71},{8,72},{9,... | collective-permute-start | bytes 196616 | tf_op jit(solution)/shard_map/ppermute | solution.py:383
  65.9 2.2 %collective-permute-done.15 = f32[2,8,8,128]{3,2,0,1:T(8,128)S(1)} collective-permute-done((f32[2,8,8,128]{3,2,0,1:T(8,128)S(1)}, f32[2,8,8,128]{3,2,0,1:T(8,128)S(1)}, u32[]{:S(2)}, u32[]{:S(2)}) %collective-permute-start.15) | collective-permute-done | bytes 65568 | tf_op jit(solution)/shard_map/ppermute | solution.py:383
  68.1 7.5 %collective-permute-start.16 = (f32[1,8,8,128]{3,2,0,1:T(8,128)S(1)}, f32[1,8,8,128]{3,2,0,1:T(8,128)S(1)}, u32[]{:S(2)}, u32[]{:S(2)}) collective-permute-start(f32[1,8,8,128]{3,2,0,1:T(8,128)S(1)} %slice_add_fusion.18), channel_id=1, source_target_pairs={{0,128},{1,129},{2,130},{3,131},{4,132},{5,133},{6,134},{7,135},{8... | collective-permute-start | bytes 98312 | tf_op jit(solution)/shard_map/ppermute | solution.py:383
  75.7 1.9 %collective-permute-done.16 = f32[1,8,8,128]{3,2,0,1:T(8,128)S(1)} collective-permute-done((f32[1,8,8,128]{3,2,0,1:T(8,128)S(1)}, f32[1,8,8,128]{3,2,0,1:T(8,128)S(1)}, u32[]{:S(2)}, u32[]{:S(2)}) %collective-permute-start.16) | collective-permute-done | bytes 32800 | tf_op jit(solution)/shard_map/ppermute | solution.py:383
  77.6 0.6 fusion.16
  (33 shorter events, 1.3 us)
Async XLA Ops:
  4.3 4.2 %collective-permute-start = (f32[2,4,4,2,8,8,128]{6,5,4,3,2,1,0:T(8,128)S(1)}, f32[2,4,4,2,8,8,128]{6,5,4,3,2,1,0:T(8,128)S(1)}, u32[]{:S(2)}, u32[]{:S(2)}) collective-permute-start(f32[2,4,4,2,8,8,128]{6,5,4,3,2,1,0:T(8,128)S(1)} %get-tuple-element.38), channel_id=1, source_target_pairs={{0,1},{1,0},{2,3},{3,2},{4,5},{5,4},{6,7},{7,6},{8,9},{9,8},{10,11... | collective-permute-start | bytes 6291464 | tf_op jit(solution)/shard_map/ppermute | solution.py:383
  8.5 2.7 %copy-start = (s32[1,64]{1,0:T(1,128)S(1)}, s32[1,64]{1,0:T(1,128)}, u32[]{:S(2)}) copy-start(s32[1,64]{1,0:T(1,128)} %owner_ref.3) | copy-start | bytes 772
  8.5 2.7 %copy-start.1 = (s32[1,64]{1,0:T(1,128)S(1)}, s32[1,64]{1,0:T(1,128)}, u32[]{:S(2)}) copy-start(s32[1,64]{1,0:T(1,128)} %offset_ref.3) | copy-start | bytes 772
  8.5 2.7 %copy-start.2 = (f32[1,64]{1,0:T(1,128)S(1)}, f32[1,64]{1,0:T(1,128)}, u32[]{:S(2)}) copy-start(f32[1,64]{1,0:T(1,128)} %weight_ref.3) | copy-start | bytes 772
  8.9 13.1 %collective-permute-start.5 = (f32[2,4,2,8,8,128]{5,4,3,2,1,0:T(8,128)S(1)}, f32[2,4,2,8,8,128]{5,4,3,2,1,0:T(8,128)S(1)}, u32[]{:S(2)}, u32[]{:S(2)}) collective-permute-start(f32[2,4,2,8,8,128]{5,4,3,2,1,0:T(8,128)S(1)} %get-tuple-element.47.after_1), channel_id=1, source_target_pairs={{0,6},{1,25},{2,4},{3,27},{4,2},{5,29},{6,0},{7,31},{8,14},{9,17},... | collective-permute-start | bytes 1572872 | tf_op jit(solution)/shard_map/ppermute | solution.py:383
  11.2 10.9 %collective-permute-start.4 = (f32[2,4,2,8,8,128]{5,4,3,2,1,0:T(8,128)S(1)}, f32[2,4,2,8,8,128]{5,4,3,2,1,0:T(8,128)S(1)}, u32[]{:S(2)}, u32[]{:S(2)}) collective-permute-start(f32[2,4,2,8,8,128]{5,4,3,2,1,0:T(8,128)S(1)} %get-tuple-element.48.after_0), channel_id=1, source_target_pairs={{0,2},{1,9},{2,0},{3,11},{4,6},{5,13},{6,4},{7,15},{8,10},{9,1},{1... | collective-permute-start | bytes 1572872 | tf_op jit(solution)/shard_map/ppermute | solution.py:383
  18.9 5.2 %collective-permute-start.1 = (f32[4,4,2,8,8,128]{5,4,3,2,1,0:T(8,128)S(1)}, f32[4,4,2,8,8,128]{5,4,3,2,1,0:T(8,128)S(1)}, u32[]{:S(2)}, u32[]{:S(2)}) collective-permute-start(f32[4,4,2,8,8,128]{5,4,3,2,1,0:T(8,128)S(1)} %get-tuple-element.41), channel_id=1, source_target_pairs={{0,1},{1,0},{2,3},{3,2},{4,5},{5,4},{6,7},{7,6},{8,9},{9,8},{10,11... | collective-permute-start | bytes 3145736 | tf_op jit(solution)/shard_map/ppermute | solution.py:383
  22.2 2.7 %collective-permute-start.6 = (f32[4,4,2,8,8,128]{5,4,3,2,1,0:T(8,128)S(1)}, f32[4,4,2,8,8,128]{5,4,3,2,1,0:T(8,128)S(1)}, u32[]{:S(2)}, u32[]{:S(2)}) collective-permute-start(f32[4,4,2,8,8,128]{5,4,3,2,1,0:T(8,128)S(1)} %hold.3), channel_id=1, source_target_pairs={{0,1},{1,0},{2,3},{3,2},{4,5},{5,4},{6,7},{7,6},{8,9},{9,8},{10,11... | collective-permute-start | bytes 3145736 | tf_op jit(solution)/shard_map/ppermute | solution.py:383
  22.3 6.5 %collective-permute-start.10 = (f32[1,4,2,8,8,128]{5,4,3,2,1,0:T(8,128)S(1)}, f32[1,4,2,8,8,128]{5,4,3,2,1,0:T(8,128)S(1)}, u32[]{:S(2)}, u32[]{:S(2)}) collective-permute-start(f32[1,4,2,8,8,128]{5,4,3,2,1,0:T(8,128)S(1)} %slice_add_fusion.12.refs_2_), channel_id=1, source_target_pairs={{0,2},{1,9},{2,0},{3,11},{4,6},{5,13},{6,4},{7,15},{8,10},{9,1},{1... | collective-permute-start | bytes 786440 | tf_op jit(solution)/shard_map/ppermute | solution.py:383
  24.3 10.0 %collective-permute-start.2 = (f32[2,4,2,8,8,128]{5,4,3,2,1,0:T(8,128)S(1)}, f32[2,4,2,8,8,128]{5,4,3,2,1,0:T(8,128)S(1)}, u32[]{:S(2)}, u32[]{:S(2)}) collective-permute-start(f32[2,4,2,8,8,128]{5,4,3,2,1,0:T(8,128)S(1)} %get-tuple-element.50), channel_id=1, source_target_pairs={{0,2},{1,9},{2,0},{3,11},{4,6},{5,13},{6,4},{7,15},{8,10},{9,1},{1... | collective-permute-start | bytes 1572872 | tf_op jit(solution)/shard_map/ppermute | solution.py:383
  25.1 10.5 %collective-permute-start.7 = (f32[2,4,2,8,8,128]{5,4,3,2,1,0:T(8,128)S(1)}, f32[2,4,2,8,8,128]{5,4,3,2,1,0:T(8,128)S(1)}, u32[]{:S(2)}, u32[]{:S(2)}) collective-permute-start(f32[2,4,2,8,8,128]{5,4,3,2,1,0:T(8,128)S(1)} %get-tuple-element.52), channel_id=1, source_target_pairs={{0,6},{1,25},{2,4},{3,27},{4,2},{5,29},{6,0},{7,31},{8,14},{9,17},... | collective-permute-start | bytes 1572872 | tf_op jit(solution)/shard_map/ppermute | solution.py:383
  25.9 12.5 %collective-permute-start.9 = (f32[1,4,2,8,8,128]{5,4,3,2,1,0:T(8,128)S(1)}, f32[1,4,2,8,8,128]{5,4,3,2,1,0:T(8,128)S(1)}, u32[]{:S(2)}, u32[]{:S(2)}) collective-permute-start(f32[1,4,2,8,8,128]{5,4,3,2,1,0:T(8,128)S(1)} %slice_add_fusion.13.refs_1_), channel_id=1, source_target_pairs={{0,6},{1,25},{2,4},{3,27},{4,2},{5,29},{6,0},{7,31},{8,14},{9,17},... | collective-permute-start | bytes 786440 | tf_op jit(solution)/shard_map/ppermute | solution.py:383
  34.4 7.7 %collective-permute-start.3 = (f32[1,4,2,8,8,128]{5,4,3,2,1,0:T(8,128)S(1)}, f32[1,4,2,8,8,128]{5,4,3,2,1,0:T(8,128)S(1)}, u32[]{:S(2)}, u32[]{:S(2)}) collective-permute-start(f32[1,4,2,8,8,128]{5,4,3,2,1,0:T(8,128)S(1)} %slice_add_fusion.14), channel_id=1, source_target_pairs={{0,6},{1,25},{2,4},{3,27},{4,2},{5,29},{6,0},{7,31},{8,14},{9,17},... | collective-permute-start | bytes 786440 | tf_op jit(solution)/shard_map/ppermute | solution.py:383
  35.6 6.5 %collective-permute-start.8 = (f32[1,4,2,8,8,128]{5,4,3,2,1,0:T(8,128)S(1)}, f32[1,4,2,8,8,128]{5,4,3,2,1,0:T(8,128)S(1)}, u32[]{:S(2)}, u32[]{:S(2)}) collective-permute-start(f32[1,4,2,8,8,128]{5,4,3,2,1,0:T(8,128)S(1)} %slice_add_fusion.10), channel_id=1, source_target_pairs={{0,2},{1,9},{2,0},{3,11},{4,6},{5,13},{6,4},{7,15},{8,10},{9,1},{1... | collective-permute-start | bytes 786440 | tf_op jit(solution)/shard_map/ppermute | solution.py:383
  42.3 6.5 %collective-permute-start.11 = (f32[8,8,8,128]{3,2,1,0:T(8,128)S(1)}, f32[8,8,8,128]{3,2,1,0:T(8,128)S(1)}, u32[]{:S(2)}, u32[]{:S(2)}) collective-permute-start(f32[8,8,8,128]{3,2,1,0:T(8,128)S(1)} %get-tuple-element.53), channel_id=1, source_target_pairs={{0,8},{1,3},{2,10},{3,1},{4,12},{5,7},{6,14},{7,5},{8,0},{9,11},{1... | collective-permute-start | bytes 786440 | tf_op jit(solution)/shard_map/ppermute | solution.py:383
  44.1 9.8 %collective-permute-start.13 = (f32[8,8,8,128]{3,2,1,0:T(8,128)S(1)}, f32[8,8,8,128]{3,2,1,0:T(8,128)S(1)}, u32[]{:S(2)}, u32[]{:S(2)}) collective-permute-start(f32[8,8,8,128]{3,2,1,0:T(8,128)S(1)} %get-tuple-element.54), channel_id=1, source_target_pairs={{0,16},{1,5},{2,18},{3,7},{4,20},{5,1},{6,22},{7,3},{8,24},{9,13},... | collective-permute-start | bytes 786440 | tf_op jit(solution)/shard_map/ppermute | solution.py:383
  46.7 10.0 %collective-permute-start.12 = (f32[8,8,8,128]{3,2,1,0:T(8,128)S(1)}, f32[8,8,8,128]{3,2,1,0:T(8,128)S(1)}, u32[]{:S(2)}, u32[]{:S(2)}) collective-permute-start(f32[8,8,8,128]{3,2,1,0:T(8,128)S(1)} %get-tuple-element.55), channel_id=1, source_target_pairs={{0,24},{1,7},{2,26},{3,5},{4,28},{5,3},{6,30},{7,1},{8,16},{9,15},... | collective-permute-start | bytes 786440 | tf_op jit(solution)/shard_map/ppermute | solution.py:383
  56.8 5.1 %collective-permute-start.14 = (f32[4,8,8,128]{3,2,0,1:T(8,128)S(1)}, f32[4,8,8,128]{3,2,0,1:T(8,128)S(1)}, u32[]{:S(2)}, u32[]{:S(2)}) collective-permute-start(f32[4,8,8,128]{3,2,0,1:T(8,128)S(1)} %slice.258), channel_id=1, source_target_pairs={{0,32},{1,33},{2,34},{3,35},{4,36},{5,37},{6,38},{7,39},{8,40},{9,... | collective-permute-start | bytes 393224 | tf_op jit(solution)/shard_map/ppermute | solution.py:383
  61.8 6.3 %collective-permute-start.15 = (f32[2,8,8,128]{3,2,0,1:T(8,128)S(1)}, f32[2,8,8,128]{3,2,0,1:T(8,128)S(1)}, u32[]{:S(2)}, u32[]{:S(2)}) collective-permute-start(f32[2,8,8,128]{3,2,0,1:T(8,128)S(1)} %get-tuple-element.57), channel_id=1, source_target_pairs={{0,64},{1,65},{2,66},{3,67},{4,68},{5,69},{6,70},{7,71},{8,72},{9,... | collective-permute-start | bytes 196616 | tf_op jit(solution)/shard_map/ppermute | solution.py:383
  68.1 9.4 %collective-permute-start.16 = (f32[1,8,8,128]{3,2,0,1:T(8,128)S(1)}, f32[1,8,8,128]{3,2,0,1:T(8,128)S(1)}, u32[]{:S(2)}, u32[]{:S(2)}) collective-permute-start(f32[1,8,8,128]{3,2,0,1:T(8,128)S(1)} %slice_add_fusion.18), channel_id=1, source_target_pairs={{0,128},{1,129},{2,130},{3,131},{4,132},{5,133},{6,134},{7,135},{8... | collective-permute-start | bytes 98312 | tf_op jit(solution)/shard_map/ppermute | solution.py:383

commit v6 on v5

--- a/solution.py
+++ b/solution.py
@@ -21,6 +21,7 @@
 HALF = WIDTH // 2
 BLOCK_SEGS = 16
 BLOCK_ROWS = BLOCK_SEGS * ROWS
+EARLY = 1
 
 
 def split(value):
@@ -178,8 +179,39 @@
     return pltpu.roll(jnp.concatenate([profile] * (LANES // 8), axis=0), 0, 1, stride=1, stride_axis=0)[:, : 3 * LANES]
 
 
+def column_pass(rows, u_high, u_low, bands, y_high, y_low):
+    near_high, near_low, cross_high, cross_low = bands
+    dot = functools.partial(jnp.dot, preferred_element_type=F32)
+    part_high = u_high[:, rows, :].reshape(2 * BLOCK_ROWS, NBASIS * HALF)
+    part_low = u_low[:, rows, :].reshape(2 * BLOCK_ROWS, NBASIS * HALF)
+    near = dot(part_high, near_high[...]) + dot(part_high, near_low[...]) + dot(part_low, near_high[...])
+    border_high, border_low = (
+        jnp.concatenate(
+            [
+                u[half, rows, k * HALF + (1 - half) * LANES : k * HALF + (2 - half) * LANES]
+                for k in range(NBASIS)
+                for half in range(2)
+            ],
+            axis=1,
+        )
+        for u in (u_high, u_low)
+    )
+    cross = (
+        dot(border_high, cross_high[...]) + dot(border_high, cross_low[...]) + dot(border_low, cross_high[...])
+    )
+    left, right = near[:BLOCK_ROWS], near[BLOCK_ROWS:]
+    wide = jnp.concatenate(
+        [left[:, :LANES], left[:, LANES:] + cross[:, :LANES], right[:, :LANES] + cross[:, LANES:], right[:, LANES:]],
+        axis=1,
+    )
+    high, low = split(wide)
+    y_high[rows, :] = high
+    y_low[rows, :] = low
+
+
 def rows_kernel(
-    pixels_ref, factor_ref, blockdiag, profiles, u_high, u_low, near_high, near_low, cross_high, cross_low, done
+    pixels_ref, factor_ref, blockdiag, profiles, y_high, y_low, u_high, u_low,
+    near_high, near_low, cross_high, cross_low, done,
 ):
     cross_high[...] = jnp.zeros(cross_high.shape, BF16)
     cross_low[...] = jnp.zeros(cross_low.shape, BF16)
@@ -213,79 +245,44 @@
         return carry
 
     lax.fori_loop(0, SEGS // BLOCK_SEGS, one, 0, unroll=True)
+    for b in range(EARLY):
+        rows = slice(b * BLOCK_ROWS, (b + 1) * BLOCK_ROWS)
+        column_pass(rows, u_high, u_low, (near_high, near_low, cross_high, cross_low), y_high, y_low)
     done[...] = jnp.zeros(done.shape, F32)
 
 
-def put(place, owner_ref, offset_ref, weight_ref, lifted, first, sums):
-    def one(s, carry):
+def numer_kernel(
+    owner_ref, offset_ref, weight_ref, warp_high, warp_low, early_high, early_low, u_high, u_low,
+    near_high, near_low, cross_high, cross_low, after_0, after_1,
+    keep_0, send_0, keep_1, send_1, sums, lifted, y_high, y_low, sems,
+):
+    place = own_place()
+    sums[...] = jnp.zeros(sums.shape, F32)
+    cut = EARLY * BLOCK_ROWS
+    for b in range(EARLY, SEGS // BLOCK_SEGS):
+        rows = slice(b * BLOCK_ROWS, (b + 1) * BLOCK_ROWS)
+        column_pass(rows, u_high, u_low, (near_high, near_low, cross_high, cross_low), y_high, y_low)
+    dot = functools.partial(jnp.dot, preferred_element_type=F32)
+    for rows, high, low in ((slice(0, cut), early_high[...], early_low[...]), (slice(cut, None), y_high[cut:], y_low[cut:])):
+        for half in range(2):
+            cols = slice(half * HALF, (half + 1) * HALF)
+            warped = dot(high, warp_high[:, cols]) + dot(high, warp_low[:, cols]) + dot(low, warp_high[:, cols])
+            lifted[2 * half, rows] = warped[:, :LANES]
+            lifted[2 * half + 1, rows] = warped[:, LANES:]
+
+    def put(s, carry):
         ry, rz = relative_patch(place, owner_ref[0, s])
         rows = pl.ds(offset_ref[0, s], ROWS)
         weight = weight_ref[0, s]
         of = pl.ds(pl.multiple_of(s * ROWS, ROWS), ROWS)
-        for block in range(2):
-            sums[block, ry, rz, rows, :] += weight * lifted[first + block, of, :]
+        for block in range(BLOCKS):
+            sums[block, ry, rz, rows, :] += weight * lifted[block, of, :]
         return carry
 
-    lax.fori_loop(0, SEGS, one, 0, unroll=4)
-
-
-def numer_kernel(
-    owner_ref, offset_ref, weight_ref, warp_high, warp_low, u_high, u_low, near_high, near_low, cross_high, cross_low,
-    after_0, after_1, keep, send, lifted, sums, y_high, y_low, sems,
-):
-    place = own_place()
-    sums[...] = jnp.zeros(sums.shape, F32)
-    dot = functools.partial(jnp.dot, preferred_element_type=F32)
-
-    def one(b, carry):
-        rows = pl.ds(pl.multiple_of(b * BLOCK_ROWS, BLOCK_ROWS), BLOCK_ROWS)
-        part_high = u_high[:, rows, :].reshape(2 * BLOCK_ROWS, NBASIS * HALF)
-        part_low = u_low[:, rows, :].reshape(2 * BLOCK_ROWS, NBASIS * HALF)
-        near = dot(part_high, near_high[...]) + dot(part_high, near_low[...]) + dot(part_low, near_high[...])
-        border_high, border_low = (
-            jnp.concatenate(
-                [
-                    u[half, rows, k * HALF + (1 - half) * LANES : k * HALF + (2 - half) * LANES]
-                    for k in range(NBASIS)
-                    for half in range(2)
-                ],
-                axis=1,
-            )
-            for u in (u_high, u_low)
-        )
-        cross = (
-            dot(border_high, cross_high[...]) + dot(border_high, cross_low[...]) + dot(border_low, cross_high[...])
-        )
-        left, right = near[:BLOCK_ROWS], near[BLOCK_ROWS:]
-        wide = jnp.concatenate(
-            [left[:, :LANES], left[:, LANES:] + cross[:, :LANES], right[:, :LANES] + cross[:, LANES:], right[:, LANES:]],
-            axis=1,
-        )
-        high, low = split(wide)
-        y_high[rows, :] = high
-        y_low[rows, :] = low
-        return carry
-
-    lax.fori_loop(0, SEGS * ROWS // BLOCK_ROWS, one, 0, unroll=True)
-    for half in range(2):
-        cols = slice(half * HALF, (half + 1) * HALF)
-        warped = (
-            dot(y_high[...], warp_high[:, cols]) + dot(y_high[...], warp_low[:, cols])
-            + dot(y_low[...], warp_high[:, cols])
-        )
-        lifted[2 * half] = warped[:, :LANES]
-        lifted[2 * half + 1] = warped[:, LANES:]
-
-    put(place, owner_ref, offset_ref, weight_ref, lifted, 0, sums)
-    for copy in write_out(place, sums, keep, send, sems, U_ORDER[0]):
-        copy.wait()
-
-
-def second_kernel(owner_ref, offset_ref, weight_ref, lifted, keep, send, sums, sems):
-    place = own_place()
-    sums[...] = jnp.zeros(sums.shape, F32)
-    put(place, owner_ref, offset_ref, weight_ref, lifted, 2, sums)
-    for copy in write_out(place, sums, keep, send, sems, U_ORDER[1]):
+    lax.fori_loop(0, SEGS, put, 0, unroll=4)
+    outputs = write_out(place, sums.at[0:2], keep_0, send_0, sems.at[0], U_ORDER[0])
+    outputs += write_out(place, sums.at[2:4], keep_1, send_1, sems.at[1], U_ORDER[1])
+    for copy in outputs:
         copy.wait()
 
 
@@ -294,7 +291,7 @@
 ANY = pl.BlockSpec(memory_space=pl.ANY)
 HBM = pl.BlockSpec(memory_space=pltpu.HBM)
 TOKEN = jax.ShapeDtypeStruct((8, LANES), F32)
-PARAMS = pltpu.CompilerParams(vmem_limit_bytes=40 * 1024 * 1024)
+PARAMS = pltpu.CompilerParams(vmem_limit_bytes=24 * 1024 * 1024)
 
 
 def pinned(*values):
@@ -327,48 +324,36 @@
 
 
 def row_pass(pixels, factor, blockdiag, profiles):
+    early = jax.ShapeDtypeStruct((EARLY * BLOCK_ROWS, WIDTH), BF16)
+    wide = jax.ShapeDtypeStruct((2, SEGS * ROWS, NBASIS * HALF), BF16)
     band = jax.ShapeDtypeStruct((NBASIS * HALF, HALF), BF16)
-    wide = jax.ShapeDtypeStruct((2, SEGS * ROWS, NBASIS * HALF), BF16)
     return pl.pallas_call(
         rows_kernel,
-        out_shape=(wide, wide, band, band, band, band, TOKEN),
+        out_shape=(early, early, wide, wide, band, band, band, band, TOKEN),
         in_specs=[VMEM] * 4,
-        out_specs=(VMEM,) * 7,
+        out_specs=(VMEM,) * 9,
         compiler_params=PARAMS,
         cost_estimate=pl.CostEstimate(flops=10**3, bytes_accessed=10**3, transcendentals=0),
         name="row_pass",
     )(pixels, factor, blockdiag, profiles)
 
 
-PARTS = jax.ShapeDtypeStruct((4, 4, 2, NZ, 8, LANES), F32)
-SUMS = pltpu.VMEM((2, NY, NZ, 64, LANES), F32)
-
-
 def numer_sums(owner, offset, weight, warp, tables, after):
+    parts = jax.ShapeDtypeStruct((4, 4, 2, NZ, 8, LANES), F32)
     wide = pltpu.VMEM((SEGS * ROWS, WIDTH), BF16)
     return pl.pallas_call(
         numer_kernel,
-        out_shape=(PARTS, PARTS, jax.ShapeDtypeStruct((BLOCKS, SEGS * ROWS, LANES), F32)),
-        in_specs=[SMEM] * 3 + [VMEM] * 10,
-        out_specs=(ANY, ANY, VMEM),
-        scratch_shapes=[SUMS, wide, wide, pltpu.SemaphoreType.DMA((32,))],
+        out_shape=(parts,) * 4,
+        in_specs=[SMEM] * 3 + [VMEM] * 12,
+        out_specs=(ANY,) * 4,
+        scratch_shapes=[
+            pltpu.VMEM((BLOCKS, NY, NZ, 64, LANES), F32), pltpu.VMEM((BLOCKS, SEGS * ROWS, LANES), F32),
+            wide, wide, pltpu.SemaphoreType.DMA((2, 32)),
+        ],
         compiler_params=PARAMS,
         cost_estimate=pl.CostEstimate(flops=10**3, bytes_accessed=10**3, transcendentals=0),
         name="numer_sums",
     )(owner, offset, weight, *warp, *tables, *after)
-
-
-def second_sums(owner, offset, weight, lifted):
-    return pl.pallas_call(
-        second_kernel,
-        out_shape=(PARTS, PARTS),
-        in_specs=[SMEM] * 3 + [VMEM],
-        out_specs=(ANY, ANY),
-        scratch_shapes=[SUMS, pltpu.SemaphoreType.DMA((32,))],
-        compiler_params=PARAMS,
-        cost_estimate=pl.CostEstimate(flops=10**3, bytes_accessed=10**3, transcendentals=0),
-        name="second_sums",
-    )(owner, offset, weight, lifted)
 
 
 def permute(value, partner):
@@ -430,10 +415,9 @@
     *tables, done = row_pass(pixels, factor, blockdiag, profiles)
     (d_got,) = hold((swap_core(d_send),), (done,))
     d_parts = [halve(d_keep[half], d_got[half]) for half in range(2)]
-    keep_0, send_0, lifted = numer_sums(
+    keep_0, send_0, keep_1, send_1 = numer_sums(
         owner, row_offset, seg_weight, warp, tables, [send for _, send in d_parts]
     )
-    keep_1, send_1 = second_sums(owner, row_offset, seg_weight, lifted)
     d_parts = [halve(keep, swap_u(send, step)) for (keep, send), step in zip(d_parts, (1, 3))]
     (send_1,) = hold((send_1,), [send for _, send in d_parts])
     n_parts = [halve(keep, swap_core(send)) for keep, send in ((keep_0, send_0), (keep_1, send_1))]

time: 78.8 us -> 76.7 us (0.973)
  Pallas kernels: 16.9 us -> 15.5 us
    pallas_call x3 -> x2, Pallas kernels: 12.6 us -> 11.3 us  [the longest x1 7.64 us: numer_sums(): pl.pallas_call(numer_kernel, out_shape=(parts,) * 4, in_specs=[SMEM] * 3...]
  transfers between devices with their start and end apart: 17 -> 17, of which waited for: 13 -> 14; matrix products, arithmetic and copies ran while one was open for 1% -> 1% of each run, Pallas kernels for 16% -> 15%
where the time goes in v6:
time: 76.7 us; the launch traced here: 76.4 us
  waiting for transfers between devices  29.6 us (39%)
  starting transfers between devices  29.2 us (38%)
  Pallas kernels  15.5 us (20%)
  other arithmetic  1.89 us (2%)
    ppermute x17, waiting for transfers between devices, permute(): return lax.ppermute(value, ('sky', 'grp'), pairs)  29.6 us
    ppermute x17, starting transfers between devices, permute(): return lax.ppermute(value, ('sky', 'grp'), pairs)  29.2 us
    pallas_call x1, Pallas kernels, numer_sums(): pl.pallas_call(numer_kernel, out_shape=(parts,) * 4, in_specs=[SMEM] * 3...  7.64 us
    pallas_call x1, Pallas kernels, denom_sums(): pl.pallas_call(denom_kernel, out_shape=(parts, parts, jax.ShapeDtypeStruc...  4.27 us
    pallas_call x1, Pallas kernels, row_pass(): pl.pallas_call(rows_kernel, out_shape=(early, early, wide, wide, band, ba...  3.61 us
  transfers between devices with their start and end apart: 17, of which 14 were waited for; matrix products, arithmetic and copies ran while one was open for 1% of the time, Pallas kernels for 15%

profile of v6, /device:TPU:6, one launch (start us, length us, event | category | flops | bytes accessed | tf_op | source)
XLA Modules:
  0.0 76.4 jit_solution(7523363209867018816)
XLA Ops:
  0.0 4.3 %denom_sums.1 = (f32[2,4,4,2,8,8,128]{6,5,4,3,2,1,0:T(8,128)S(1)}, f32[2,4,4,2,8,8,128]{6,5,4,3,2,1,0:T(8,128)S(1)}, f32[1,64,16,512]{3,2,1,0:T(8,128)S(1)}, f32...) custom-call(s32[1,64]{1,0:T(1,128)} %owner_ref.1, ...), custom_call_target="tpu_custom_call" | custom-call | flops 1000 | bytes 1000 | tf_op jit(solution)/shard_map/denom_sums/pallas_call | solution.py:305
  4.4 3.6 %row_pass.1 = (bf16[256,512]{1,0:T(8,128)(2,1)S(1)}, bf16[256,512]{1,0:T(8,128)(2,1)S(1)}, bf16[2,1024,768]{2,1,0:T(8,128)(2,1)S(1)}, bf16[2,1024,768]{2,1,0:T(8...) custom-call(f32[1,64,16,512]{3,2,1,0:T(8,128)S(1)} %get-tuple-elemen, ...), custom_call_target="tpu_custom_call" | custom-call | flops 1000 | bytes 1000 | tf_op jit(solution)/shard_map/row_pass/pallas_call | solution.py:330
  8.0 0.5 collective-permute-done.refs_0_
  8.5 0.4 slice_add_fusion.3
  8.9 2.3 %collective-permute-start.5 = (f32[2,4,2,8,8,128]{5,4,3,2,1,0:T(8,128)S(1)}, f32[2,4,2,8,8,128]{5,4,3,2,1,0:T(8,128)S(1)}, u32[]{:S(2)}, u32[]{:S(2)}) collective-permute-start(f32[2,4,2,8,8,128]{5,4,3,2,1,0:T(8,128)S(1)} %get-tuple-element.49.after_1), channel_id=1, source_target_pairs={{0,6},{1,25},{2,4},{3,27},{4,2},{5,29},{6,0},{7,31},{8,14},{9,17},... | collective-permute-start | bytes 1572872 | tf_op jit(solution)/shard_map/ppermute | solution.py:368
  11.2 7.6 %numer_sums.1 = (f32[4,4,2,8,8,128]{5,4,3,2,1,0:T(8,128)S(1)}, f32[4,4,2,8,8,128]{5,4,3,2,1,0:T(8,128)S(1)}, f32[4,4,2,8,8,128]{5,4,3,2,1,0:T(8,128)S(1)}, f32[4,4,2,8,8,128]{5,4,3,2,1,0:T(8,128)S(1)}) custom-call(s32[1,64]{1,0:T(1,128)S(1)} %copy-done, s32[1,64]{1,0:T(1,128)S(1)} %copy-done.1, f32[1,64]{1,0:T(1,128)S(1)} %copy-done.2, ...), custom_call_target="tpu_custom_call" | custom-call | flops 1000 | bytes 1000 | tf_op jit(solution)/shard_map/numer_sums/pallas_call | solution.py:344
  18.9 0.7 collective-permute-start.1
  19.7 0.7 collective-permute-done.4
  20.6 1.1 %collective-permute-start.10 = (f32[1,4,2,8,8,128]{5,4,3,2,1,0:T(8,128)S(1)}, f32[1,4,2,8,8,128]{5,4,3,2,1,0:T(8,128)S(1)}, u32[]{:S(2)}, u32[]{:S(2)}) collective-permute-start(f32[1,4,2,8,8,128]{5,4,3,2,1,0:T(8,128)S(1)} %slice_add_fusion.12.refs_2_), channel_id=1, source_target_pairs={{0,2},{1,9},{2,0},{3,11},{4,6},{5,13},{6,4},{7,15},{8,10},{9,1},{1... | collective-permute-start | bytes 786440 | tf_op jit(solution)/shard_map/ppermute | solution.py:368
  21.7 0.2 collective-permute-done.1
  22.1 1.8 %collective-permute-start.2 = (f32[2,4,2,8,8,128]{5,4,3,2,1,0:T(8,128)S(1)}, f32[2,4,2,8,8,128]{5,4,3,2,1,0:T(8,128)S(1)}, u32[]{:S(2)}, u32[]{:S(2)}) collective-permute-start(f32[2,4,2,8,8,128]{5,4,3,2,1,0:T(8,128)S(1)} %get-tuple-element.52), channel_id=1, source_target_pairs={{0,2},{1,9},{2,0},{3,11},{4,6},{5,13},{6,4},{7,15},{8,10},{9,1},{1... | collective-permute-start | bytes 1572872 | tf_op jit(solution)/shard_map/ppermute | solution.py:368
  24.1 1.1 %collective-permute-start.7 = (f32[2,4,2,8,8,128]{5,4,3,2,1,0:T(8,128)S(1)}, f32[2,4,2,8,8,128]{5,4,3,2,1,0:T(8,128)S(1)}, u32[]{:S(2)}, u32[]{:S(2)}) collective-permute-start(f32[2,4,2,8,8,128]{5,4,3,2,1,0:T(8,128)S(1)} %get-tuple-element.54), channel_id=1, source_target_pairs={{0,6},{1,25},{2,4},{3,27},{4,2},{5,29},{6,0},{7,31},{8,14},{9,17},... | collective-permute-start | bytes 1572872 | tf_op jit(solution)/shard_map/ppermute | solution.py:368
  25.2 2.2 %collective-permute-start.9 = (f32[1,4,2,8,8,128]{5,4,3,2,1,0:T(8,128)S(1)}, f32[1,4,2,8,8,128]{5,4,3,2,1,0:T(8,128)S(1)}, u32[]{:S(2)}, u32[]{:S(2)}) collective-permute-start(f32[1,4,2,8,8,128]{5,4,3,2,1,0:T(8,128)S(1)} %slice_add_fusion.13.refs_1_), channel_id=1, source_target_pairs={{0,6},{1,25},{2,4},{3,27},{4,2},{5,29},{6,0},{7,31},{8,14},{9,17},... | collective-permute-start | bytes 786440 | tf_op jit(solution)/shard_map/ppermute | solution.py:368
  27.5 5.1 %collective-permute-done.2 = f32[2,4,2,8,8,128]{5,4,3,2,1,0:T(8,128)S(1)} collective-permute-done((f32[2,4,2,8,8,128]{5,4,3,2,1,0:T(8,128)S(1)}, f32[2,4,2,8,8,128]{5,4,3,2,1,0:T(8,128)S(1)}, u32[]{:S(2)}, u32[]{:S(2)}) %collective-permute-start.2) | collective-permute-done | bytes 524320 | tf_op jit(solution)/shard_map/ppermute | solution.py:368
  32.7 1.4 %collective-permute-start.3 = (f32[1,4,2,8,8,128]{5,4,3,2,1,0:T(8,128)S(1)}, f32[1,4,2,8,8,128]{5,4,3,2,1,0:T(8,128)S(1)}, u32[]{:S(2)}, u32[]{:S(2)}) collective-permute-start(f32[1,4,2,8,8,128]{5,4,3,2,1,0:T(8,128)S(1)} %slice_add_fusion.14), channel_id=1, source_target_pairs={{0,6},{1,25},{2,4},{3,27},{4,2},{5,29},{6,0},{7,31},{8,14},{9,17},... | collective-permute-start | bytes 786440 | tf_op jit(solution)/shard_map/ppermute | solution.py:368
  34.0 0.6 collective-permute-done.7
  34.7 2.7 %collective-permute-done.9 = f32[1,4,2,8,8,128]{5,4,3,2,1,0:T(8,128)S(1)} collective-permute-done((f32[1,4,2,8,8,128]{5,4,3,2,1,0:T(8,128)S(1)}, f32[1,4,2,8,8,128]{5,4,3,2,1,0:T(8,128)S(1)}, u32[]{:S(2)}, u32[]{:S(2)}) %collective-permute-start.9) | collective-permute-done | bytes 262176 | tf_op jit(solution)/shard_map/ppermute | solution.py:368
  37.4 2.9 %collective-permute-done.3 = f32[1,4,2,8,8,128]{5,4,3,2,1,0:T(8,128)S(1)} collective-permute-done((f32[1,4,2,8,8,128]{5,4,3,2,1,0:T(8,128)S(1)}, f32[1,4,2,8,8,128]{5,4,3,2,1,0:T(8,128)S(1)}, u32[]{:S(2)}, u32[]{:S(2)}) %collective-permute-start.3) | collective-permute-done | bytes 262176 | tf_op jit(solution)/shard_map/ppermute | solution.py:368
  40.4 0.7 collective-permute-done.8
  41.3 1.3 %collective-permute-start.11 = (f32[8,8,8,128]{3,2,1,0:T(8,128)S(1)}, f32[8,8,8,128]{3,2,1,0:T(8,128)S(1)}, u32[]{:S(2)}, u32[]{:S(2)}) collective-permute-start(f32[8,8,8,128]{3,2,1,0:T(8,128)S(1)} %get-tuple-element.55), channel_id=1, source_target_pairs={{0,8},{1,3},{2,10},{3,1},{4,12},{5,7},{6,14},{7,5},{8,0},{9,11},{1... | collective-permute-start | bytes 786440 | tf_op jit(solution)/shard_map/ppermute | solution.py:368
  42.6 2.4 %collective-permute-start.13 = (f32[8,8,8,128]{3,2,1,0:T(8,128)S(1)}, f32[8,8,8,128]{3,2,1,0:T(8,128)S(1)}, u32[]{:S(2)}, u32[]{:S(2)}) collective-permute-start(f32[8,8,8,128]{3,2,1,0:T(8,128)S(1)} %get-tuple-element.56), channel_id=1, source_target_pairs={{0,16},{1,5},{2,18},{3,7},{4,20},{5,1},{6,22},{7,3},{8,24},{9,13},... | collective-permute-start | bytes 786440 | tf_op jit(solution)/shard_map/ppermute | solution.py:368
  45.1 1.0 %collective-permute-start.12 = (f32[8,8,8,128]{3,2,1,0:T(8,128)S(1)}, f32[8,8,8,128]{3,2,1,0:T(8,128)S(1)}, u32[]{:S(2)}, u32[]{:S(2)}) collective-permute-start(f32[8,8,8,128]{3,2,1,0:T(8,128)S(1)} %get-tuple-element.57), channel_id=1, source_target_pairs={{0,24},{1,7},{2,26},{3,5},{4,28},{5,3},{6,30},{7,1},{8,16},{9,15},... | collective-permute-start | bytes 786440 | tf_op jit(solution)/shard_map/ppermute | solution.py:368
  46.1 1.7 %collective-permute-done.11 = f32[8,8,8,128]{3,2,1,0:T(8,128)S(1)} collective-permute-done((f32[8,8,8,128]{3,2,1,0:T(8,128)S(1)}, f32[8,8,8,128]{3,2,1,0:T(8,128)S(1)}, u32[]{:S(2)}, u32[]{:S(2)}) %collective-permute-start.11) | collective-permute-done | bytes 262176 | tf_op jit(solution)/shard_map/ppermute | solution.py:368
  47.8 4.6 %collective-permute-done.13 = f32[8,8,8,128]{3,2,1,0:T(8,128)S(1)} collective-permute-done((f32[8,8,8,128]{3,2,1,0:T(8,128)S(1)}, f32[8,8,8,128]{3,2,1,0:T(8,128)S(1)}, u32[]{:S(2)}, u32[]{:S(2)}) %collective-permute-start.13) | collective-permute-done | bytes 262176 | tf_op jit(solution)/shard_map/ppermute | solution.py:368
  52.3 2.7 %collective-permute-done.12 = f32[8,8,8,128]{3,2,1,0:T(8,128)S(1)} collective-permute-done((f32[8,8,8,128]{3,2,1,0:T(8,128)S(1)}, f32[8,8,8,128]{3,2,1,0:T(8,128)S(1)}, u32[]{:S(2)}, u32[]{:S(2)}) %collective-permute-start.12) | collective-permute-done | bytes 262176 | tf_op jit(solution)/shard_map/ppermute | solution.py:368
  55.1 2.0 %collective-permute-start.14 = (f32[4,8,8,128]{3,2,0,1:T(8,128)S(1)}, f32[4,8,8,128]{3,2,0,1:T(8,128)S(1)}, u32[]{:S(2)}, u32[]{:S(2)}) collective-permute-start(f32[4,8,8,128]{3,2,0,1:T(8,128)S(1)} %slice.258), channel_id=1, source_target_pairs={{0,32},{1,33},{2,34},{3,35},{4,36},{5,37},{6,38},{7,39},{8,40},{9,... | collective-permute-start | bytes 393224 | tf_op jit(solution)/shard_map/ppermute | solution.py:368
  57.1 3.1 %collective-permute-done.14 = f32[4,8,8,128]{3,2,0,1:T(8,128)S(1)} collective-permute-done((f32[4,8,8,128]{3,2,0,1:T(8,128)S(1)}, f32[4,8,8,128]{3,2,0,1:T(8,128)S(1)}, u32[]{:S(2)}, u32[]{:S(2)}) %collective-permute-start.14) | collective-permute-done | bytes 131104 | tf_op jit(solution)/shard_map/ppermute | solution.py:368
  60.2 4.1 %collective-permute-start.15 = (f32[2,8,8,128]{3,2,0,1:T(8,128)S(1)}, f32[2,8,8,128]{3,2,0,1:T(8,128)S(1)}, u32[]{:S(2)}, u32[]{:S(2)}) collective-permute-start(f32[2,8,8,128]{3,2,0,1:T(8,128)S(1)} %get-tuple-element.59), channel_id=1, source_target_pairs={{0,64},{1,65},{2,66},{3,67},{4,68},{5,69},{6,70},{7,71},{8,72},{9,... | collective-permute-start | bytes 196616 | tf_op jit(solution)/shard_map/ppermute | solution.py:368
  64.3 2.3 %collective-permute-done.15 = f32[2,8,8,128]{3,2,0,1:T(8,128)S(1)} collective-permute-done((f32[2,8,8,128]{3,2,0,1:T(8,128)S(1)}, f32[2,8,8,128]{3,2,0,1:T(8,128)S(1)}, u32[]{:S(2)}, u32[]{:S(2)}) %collective-permute-start.15) | collective-permute-done | bytes 65568 | tf_op jit(solution)/shard_map/ppermute | solution.py:368
  66.5 7.4 %collective-permute-start.16 = (f32[1,8,8,128]{3,2,0,1:T(8,128)S(1)}, f32[1,8,8,128]{3,2,0,1:T(8,128)S(1)}, u32[]{:S(2)}, u32[]{:S(2)}) collective-permute-start(f32[1,8,8,128]{3,2,0,1:T(8,128)S(1)} %slice_add_fusion.18), channel_id=1, source_target_pairs={{0,128},{1,129},{2,130},{3,131},{4,132},{5,133},{6,134},{7,135},{8... | collective-permute-start | bytes 98312 | tf_op jit(solution)/shard_map/ppermute | solution.py:368
  73.9 1.9 %collective-permute-done.16 = f32[1,8,8,128]{3,2,0,1:T(8,128)S(1)} collective-permute-done((f32[1,8,8,128]{3,2,0,1:T(8,128)S(1)}, f32[1,8,8,128]{3,2,0,1:T(8,128)S(1)}, u32[]{:S(2)}, u32[]{:S(2)}) %collective-permute-start.16) | collective-permute-done | bytes 32800 | tf_op jit(solution)/shard_map/ppermute | solution.py:368
  75.8 0.6 fusion.16
  (32 shorter events, 1.3 us)
Async XLA Ops:
  4.3 4.2 %collective-permute-start = (f32[2,4,4,2,8,8,128]{6,5,4,3,2,1,0:T(8,128)S(1)}, f32[2,4,4,2,8,8,128]{6,5,4,3,2,1,0:T(8,128)S(1)}, u32[]{:S(2)}, u32[]{:S(2)}) collective-permute-start(f32[2,4,4,2,8,8,128]{6,5,4,3,2,1,0:T(8,128)S(1)} %get-tuple-element.41), channel_id=1, source_target_pairs={{0,1},{1,0},{2,3},{3,2},{4,5},{5,4},{6,7},{7,6},{8,9},{9,8},{10,11... | collective-permute-start | bytes 6291464 | tf_op jit(solution)/shard_map/ppermute | solution.py:368
  8.5 2.7 %copy-start = (s32[1,64]{1,0:T(1,128)S(1)}, s32[1,64]{1,0:T(1,128)}, u32[]{:S(2)}) copy-start(s32[1,64]{1,0:T(1,128)} %owner_ref.1) | copy-start | bytes 772
  8.5 2.7 %copy-start.1 = (s32[1,64]{1,0:T(1,128)S(1)}, s32[1,64]{1,0:T(1,128)}, u32[]{:S(2)}) copy-start(s32[1,64]{1,0:T(1,128)} %offset_ref.1) | copy-start | bytes 772
  8.5 2.7 %copy-start.2 = (f32[1,64]{1,0:T(1,128)S(1)}, f32[1,64]{1,0:T(1,128)}, u32[]{:S(2)}) copy-start(f32[1,64]{1,0:T(1,128)} %weight_ref.1) | copy-start | bytes 772
  8.9 10.7 %collective-permute-start.5 = (f32[2,4,2,8,8,128]{5,4,3,2,1,0:T(8,128)S(1)}, f32[2,4,2,8,8,128]{5,4,3,2,1,0:T(8,128)S(1)}, u32[]{:S(2)}, u32[]{:S(2)}) collective-permute-start(f32[2,4,2,8,8,128]{5,4,3,2,1,0:T(8,128)S(1)} %get-tuple-element.49.after_1), channel_id=1, source_target_pairs={{0,6},{1,25},{2,4},{3,27},{4,2},{5,29},{6,0},{7,31},{8,14},{9,17},... | collective-permute-start | bytes 1572872 | tf_op jit(solution)/shard_map/ppermute | solution.py:368
  11.2 9.2 %collective-permute-start.4 = (f32[2,4,2,8,8,128]{5,4,3,2,1,0:T(8,128)S(1)}, f32[2,4,2,8,8,128]{5,4,3,2,1,0:T(8,128)S(1)}, u32[]{:S(2)}, u32[]{:S(2)}) collective-permute-start(f32[2,4,2,8,8,128]{5,4,3,2,1,0:T(8,128)S(1)} %get-tuple-element.50.after_0), channel_id=1, source_target_pairs={{0,2},{1,9},{2,0},{3,11},{4,6},{5,13},{6,4},{7,15},{8,10},{9,1},{1... | collective-permute-start | bytes 1572872 | tf_op jit(solution)/shard_map/ppermute | solution.py:368
  18.9 3.0 %collective-permute-start.1 = (f32[4,4,2,8,8,128]{5,4,3,2,1,0:T(8,128)S(1)}, f32[4,4,2,8,8,128]{5,4,3,2,1,0:T(8,128)S(1)}, u32[]{:S(2)}, u32[]{:S(2)}) collective-permute-start(f32[4,4,2,8,8,128]{5,4,3,2,1,0:T(8,128)S(1)} %get-tuple-element.44), channel_id=1, source_target_pairs={{0,1},{1,0},{2,3},{3,2},{4,5},{5,4},{6,7},{7,6},{8,9},{9,8},{10,11... | collective-permute-start | bytes 3145736 | tf_op jit(solution)/shard_map/ppermute | solution.py:368
  20.5 3.5 %collective-permute-start.6 = (f32[4,4,2,8,8,128]{5,4,3,2,1,0:T(8,128)S(1)}, f32[4,4,2,8,8,128]{5,4,3,2,1,0:T(8,128)S(1)}, u32[]{:S(2)}, u32[]{:S(2)}) collective-permute-start(f32[4,4,2,8,8,128]{5,4,3,2,1,0:T(8,128)S(1)} %hold.3), channel_id=1, source_target_pairs={{0,1},{1,0},{2,3},{3,2},{4,5},{5,4},{6,7},{7,6},{8,9},{9,8},{10,11... | collective-permute-start | bytes 3145736 | tf_op jit(solution)/shard_map/ppermute | solution.py:368
  20.6 6.9 %collective-permute-start.10 = (f32[1,4,2,8,8,128]{5,4,3,2,1,0:T(8,128)S(1)}, f32[1,4,2,8,8,128]{5,4,3,2,1,0:T(8,128)S(1)}, u32[]{:S(2)}, u32[]{:S(2)}) collective-permute-start(f32[1,4,2,8,8,128]{5,4,3,2,1,0:T(8,128)S(1)} %slice_add_fusion.12.refs_2_), channel_id=1, source_target_pairs={{0,2},{1,9},{2,0},{3,11},{4,6},{5,13},{6,4},{7,15},{8,10},{9,1},{1... | collective-permute-start | bytes 786440 | tf_op jit(solution)/shard_map/ppermute | solution.py:368
  22.1 10.5 %collective-permute-start.2 = (f32[2,4,2,8,8,128]{5,4,3,2,1,0:T(8,128)S(1)}, f32[2,4,2,8,8,128]{5,4,3,2,1,0:T(8,128)S(1)}, u32[]{:S(2)}, u32[]{:S(2)}) collective-permute-start(f32[2,4,2,8,8,128]{5,4,3,2,1,0:T(8,128)S(1)} %get-tuple-element.52), channel_id=1, source_target_pairs={{0,2},{1,9},{2,0},{3,11},{4,6},{5,13},{6,4},{7,15},{8,10},{9,1},{1... | collective-permute-start | bytes 1572872 | tf_op jit(solution)/shard_map/ppermute | solution.py:368
  24.1 10.5 %collective-permute-start.7 = (f32[2,4,2,8,8,128]{5,4,3,2,1,0:T(8,128)S(1)}, f32[2,4,2,8,8,128]{5,4,3,2,1,0:T(8,128)S(1)}, u32[]{:S(2)}, u32[]{:S(2)}) collective-permute-start(f32[2,4,2,8,8,128]{5,4,3,2,1,0:T(8,128)S(1)} %get-tuple-element.54), channel_id=1, source_target_pairs={{0,6},{1,25},{2,4},{3,27},{4,2},{5,29},{6,0},{7,31},{8,14},{9,17},... | collective-permute-start | bytes 1572872 | tf_op jit(solution)/shard_map/ppermute | solution.py:368
  25.2 12.2 %collective-permute-start.9 = (f32[1,4,2,8,8,128]{5,4,3,2,1,0:T(8,128)S(1)}, f32[1,4,2,8,8,128]{5,4,3,2,1,0:T(8,128)S(1)}, u32[]{:S(2)}, u32[]{:S(2)}) collective-permute-start(f32[1,4,2,8,8,128]{5,4,3,2,1,0:T(8,128)S(1)} %slice_add_fusion.13.refs_1_), channel_id=1, source_target_pairs={{0,6},{1,25},{2,4},{3,27},{4,2},{5,29},{6,0},{7,31},{8,14},{9,17},... | collective-permute-start | bytes 786440 | tf_op jit(solution)/shard_map/ppermute | solution.py:368
  32.7 7.7 %collective-permute-start.3 = (f32[1,4,2,8,8,128]{5,4,3,2,1,0:T(8,128)S(1)}, f32[1,4,2,8,8,128]{5,4,3,2,1,0:T(8,128)S(1)}, u32[]{:S(2)}, u32[]{:S(2)}) collective-permute-start(f32[1,4,2,8,8,128]{5,4,3,2,1,0:T(8,128)S(1)} %slice_add_fusion.14), channel_id=1, source_target_pairs={{0,6},{1,25},{2,4},{3,27},{4,2},{5,29},{6,0},{7,31},{8,14},{9,17},... | collective-permute-start | bytes 786440 | tf_op jit(solution)/shard_map/ppermute | solution.py:368
  34.6 6.5 %collective-permute-start.8 = (f32[1,4,2,8,8,128]{5,4,3,2,1,0:T(8,128)S(1)}, f32[1,4,2,8,8,128]{5,4,3,2,1,0:T(8,128)S(1)}, u32[]{:S(2)}, u32[]{:S(2)}) collective-permute-start(f32[1,4,2,8,8,128]{5,4,3,2,1,0:T(8,128)S(1)} %slice_add_fusion.10), channel_id=1, source_target_pairs={{0,2},{1,9},{2,0},{3,11},{4,6},{5,13},{6,4},{7,15},{8,10},{9,1},{1... | collective-permute-start | bytes 786440 | tf_op jit(solution)/shard_map/ppermute | solution.py:368
  41.3 6.5 %collective-permute-start.11 = (f32[8,8,8,128]{3,2,1,0:T(8,128)S(1)}, f32[8,8,8,128]{3,2,1,0:T(8,128)S(1)}, u32[]{:S(2)}, u32[]{:S(2)}) collective-permute-start(f32[8,8,8,128]{3,2,1,0:T(8,128)S(1)} %get-tuple-element.55), channel_id=1, source_target_pairs={{0,8},{1,3},{2,10},{3,1},{4,12},{5,7},{6,14},{7,5},{8,0},{9,11},{1... | collective-permute-start | bytes 786440 | tf_op jit(solution)/shard_map/ppermute | solution.py:368
  42.6 9.7 %collective-permute-start.13 = (f32[8,8,8,128]{3,2,1,0:T(8,128)S(1)}, f32[8,8,8,128]{3,2,1,0:T(8,128)S(1)}, u32[]{:S(2)}, u32[]{:S(2)}) collective-permute-start(f32[8,8,8,128]{3,2,1,0:T(8,128)S(1)} %get-tuple-element.56), channel_id=1, source_target_pairs={{0,16},{1,5},{2,18},{3,7},{4,20},{5,1},{6,22},{7,3},{8,24},{9,13},... | collective-permute-start | bytes 786440 | tf_op jit(solution)/shard_map/ppermute | solution.py:368
  45.1 10.0 %collective-permute-start.12 = (f32[8,8,8,128]{3,2,1,0:T(8,128)S(1)}, f32[8,8,8,128]{3,2,1,0:T(8,128)S(1)}, u32[]{:S(2)}, u32[]{:S(2)}) collective-permute-start(f32[8,8,8,128]{3,2,1,0:T(8,128)S(1)} %get-tuple-element.57), channel_id=1, source_target_pairs={{0,24},{1,7},{2,26},{3,5},{4,28},{5,3},{6,30},{7,1},{8,16},{9,15},... | collective-permute-start | bytes 786440 | tf_op jit(solution)/shard_map/ppermute | solution.py:368
  55.1 5.1 %collective-permute-start.14 = (f32[4,8,8,128]{3,2,0,1:T(8,128)S(1)}, f32[4,8,8,128]{3,2,0,1:T(8,128)S(1)}, u32[]{:S(2)}, u32[]{:S(2)}) collective-permute-start(f32[4,8,8,128]{3,2,0,1:T(8,128)S(1)} %slice.258), channel_id=1, source_target_pairs={{0,32},{1,33},{2,34},{3,35},{4,36},{5,37},{6,38},{7,39},{8,40},{9,... | collective-permute-start | bytes 393224 | tf_op jit(solution)/shard_map/ppermute | solution.py:368
  60.2 6.3 %collective-permute-start.15 = (f32[2,8,8,128]{3,2,0,1:T(8,128)S(1)}, f32[2,8,8,128]{3,2,0,1:T(8,128)S(1)}, u32[]{:S(2)}, u32[]{:S(2)}) collective-permute-start(f32[2,8,8,128]{3,2,0,1:T(8,128)S(1)} %get-tuple-element.59), channel_id=1, source_target_pairs={{0,64},{1,65},{2,66},{3,67},{4,68},{5,69},{6,70},{7,71},{8,72},{9,... | collective-permute-start | bytes 196616 | tf_op jit(solution)/shard_map/ppermute | solution.py:368
  66.5 9.3 %collective-permute-start.16 = (f32[1,8,8,128]{3,2,0,1:T(8,128)S(1)}, f32[1,8,8,128]{3,2,0,1:T(8,128)S(1)}, u32[]{:S(2)}, u32[]{:S(2)}) collective-permute-start(f32[1,8,8,128]{3,2,0,1:T(8,128)S(1)} %slice_add_fusion.18), channel_id=1, source_target_pairs={{0,128},{1,129},{2,130},{3,131},{4,132},{5,133},{6,134},{7,135},{8... | collective-permute-start | bytes 98312 | tf_op jit(solution)/shard_map/ppermute | solution.py:368

commit v7 on v6

--- a/solution.py
+++ b/solution.py
@@ -185,12 +185,12 @@
     part_high = u_high[:, rows, :].reshape(2 * BLOCK_ROWS, NBASIS * HALF)
     part_low = u_low[:, rows, :].reshape(2 * BLOCK_ROWS, NBASIS * HALF)
     near = dot(part_high, near_high[...]) + dot(part_high, near_low[...]) + dot(part_low, near_high[...])
+    upper = lax.broadcasted_iota(jnp.int32, (BLOCK_ROWS, LANES), 1) < LANES // 2
     border_high, border_low = (
         jnp.concatenate(
             [
-                u[half, rows, k * HALF + (1 - half) * LANES : k * HALF + (2 - half) * LANES]
+                jnp.where(upper, u[1, rows, k * HALF : k * HALF + LANES], u[0, rows, k * HALF + LANES : (k + 1) * HALF])
                 for k in range(NBASIS)
-                for half in range(2)
             ],
             axis=1,
         )
@@ -213,21 +213,17 @@
     pixels_ref, factor_ref, blockdiag, profiles, y_high, y_low, u_high, u_low,
     near_high, near_low, cross_high, cross_low, done,
 ):
-    cross_high[...] = jnp.zeros(cross_high.shape, BF16)
-    cross_low[...] = jnp.zeros(cross_low.shape, BF16)
+    upper = lax.broadcasted_iota(jnp.int32, (LANES, LANES), 0) < LANES // 2
     for k in range(NBASIS):
-        for near, cross, band in zip(
-            (near_high, near_low), (cross_high, cross_low), split(band_tables(profiles[k]))
-        ):
-            top = slice(k * HALF, k * HALF + LANES)
-            bottom = slice(k * HALF + LANES, (k + 1) * HALF)
-            left, middle, right = (band[:, i * LANES : (i + 1) * LANES] for i in range(3))
-            near[top, :LANES] = middle
-            near[top, LANES:] = right
-            near[bottom, :LANES] = left
-            near[bottom, LANES:] = middle
-            cross[top, LANES:] = right
-            cross[bottom, :LANES] = left
+        band = band_tables(profiles[k])
+        left, middle, right = (band[:, i * LANES : (i + 1) * LANES] for i in range(3))
+        rows = slice(k * HALF, (k + 1) * HALF)
+        whole = jnp.concatenate([jnp.concatenate([middle, right], axis=1), jnp.concatenate([left, middle], axis=1)])
+        near_high[rows, :], near_low[rows, :] = split(whole)
+        rows = slice(k * LANES, (k + 1) * LANES)
+        border = jnp.concatenate([jnp.where(upper, left, 0.0), jnp.where(upper, 0.0, right)], axis=1)
+        cross_high[rows, :], cross_low[rows, :] = split(border)
+
     def one(b, carry):
         segs = pl.ds(b * BLOCK_SEGS, BLOCK_SEGS)
         masked = (pixels_ref[0, segs] * factor_ref[segs, :][:, None, :]).reshape(BLOCK_ROWS, WIDTH)
@@ -327,9 +323,10 @@
     early = jax.ShapeDtypeStruct((EARLY * BLOCK_ROWS, WIDTH), BF16)
     wide = jax.ShapeDtypeStruct((2, SEGS * ROWS, NBASIS * HALF), BF16)
     band = jax.ShapeDtypeStruct((NBASIS * HALF, HALF), BF16)
+    cross = jax.ShapeDtypeStruct((NBASIS * LANES, HALF), BF16)
     return pl.pallas_call(
         rows_kernel,
-        out_shape=(early, early, wide, wide, band, band, band, band, TOKEN),
+        out_shape=(early, early, wide, wide, band, band, cross, cross, TOKEN),
         in_specs=[VMEM] * 4,
         out_specs=(VMEM,) * 9,
         compiler_params=PARAMS,

time: 76.7 us -> 76.6 us (level)
  transfers between devices with their start and end apart: 17 -> 17, of which waited for: 14 -> 14; matrix products, arithmetic and copies ran while one was open for 1% -> 1% of each run, Pallas kernels for 15% -> 14%
where the time goes in v7:
time: 76.6 us; the launch traced here: 76.4 us
  waiting for transfers between devices  30 us (39%)
  starting transfers between devices  29.3 us (38%)
  Pallas kernels  15.1 us (20%)
  other arithmetic  1.89 us (2%)
    ppermute x17, waiting for transfers between devices, permute(): return lax.ppermute(value, ('sky', 'grp'), pairs)  30 us
    ppermute x17, starting transfers between devices, permute(): return lax.ppermute(value, ('sky', 'grp'), pairs)  29.3 us
    pallas_call x1, Pallas kernels, numer_sums(): pl.pallas_call(numer_kernel, out_shape=(parts,) * 4, in_specs=[SMEM] * 3...  7.35 us
    pallas_call x1, Pallas kernels, denom_sums(): pl.pallas_call(denom_kernel, out_shape=(parts, parts, jax.ShapeDtypeStruc...  4.27 us
    pallas_call x1, Pallas kernels, row_pass(): pl.pallas_call(rows_kernel, out_shape=(early, early, wide, wide, band, ba...  3.47 us
  transfers between devices with their start and end apart: 17, of which 14 were waited for; matrix products, arithmetic and copies ran while one was open for 1% of the time, Pallas kernels for 14%

profile of v7, /device:TPU:6, one launch (start us, length us, event | category | flops | bytes accessed | tf_op | source)
XLA Modules:
  0.0 76.4 jit_solution(12012317340730088123)
XLA Ops:
  0.0 4.3 %denom_sums.1 = (f32[2,4,4,2,8,8,128]{6,5,4,3,2,1,0:T(8,128)S(1)}, f32[2,4,4,2,8,8,128]{6,5,4,3,2,1,0:T(8,128)S(1)}, f32[1,64,16,512]{3,2,1,0:T(8,128)S(1)}, f32...) custom-call(s32[1,64]{1,0:T(1,128)} %owner_ref.1, ...), custom_call_target="tpu_custom_call" | custom-call | flops 1000 | bytes 1000 | tf_op jit(solution)/shard_map/denom_sums/pallas_call | solution.py:301
  4.4 3.5 %row_pass.1 = (bf16[256,512]{1,0:T(8,128)(2,1)S(1)}, bf16[256,512]{1,0:T(8,128)(2,1)S(1)}, bf16[2,1024,768]{2,1,0:T(8,128)(2,1)S(1)}, bf16[2,1024,768]{2,1,0:T(8...) custom-call(f32[1,64,16,512]{3,2,1,0:T(8,128)S(1)} %get-tuple-elemen, ...), custom_call_target="tpu_custom_call" | custom-call | flops 1000 | bytes 1000 | tf_op jit(solution)/shard_map/row_pass/pallas_call | solution.py:327
  7.9 0.7 collective-permute-done.refs_0_
  8.5 0.4 slice_add_fusion.3
  8.9 2.3 %collective-permute-start.5 = (f32[2,4,2,8,8,128]{5,4,3,2,1,0:T(8,128)S(1)}, f32[2,4,2,8,8,128]{5,4,3,2,1,0:T(8,128)S(1)}, u32[]{:S(2)}, u32[]{:S(2)}) collective-permute-start(f32[2,4,2,8,8,128]{5,4,3,2,1,0:T(8,128)S(1)} %get-tuple-element.49.after_1), channel_id=1, source_target_pairs={{0,6},{1,25},{2,4},{3,27},{4,2},{5,29},{6,0},{7,31},{8,14},{9,17},... | collective-permute-start | bytes 1572872 | tf_op jit(solution)/shard_map/ppermute | solution.py:365
  11.2 7.3 %numer_sums.1 = (f32[4,4,2,8,8,128]{5,4,3,2,1,0:T(8,128)S(1)}, f32[4,4,2,8,8,128]{5,4,3,2,1,0:T(8,128)S(1)}, f32[4,4,2,8,8,128]{5,4,3,2,1,0:T(8,128)S(1)}, f32[4,4,2,8,8,128]{5,4,3,2,1,0:T(8,128)S(1)}) custom-call(s32[1,64]{1,0:T(1,128)S(1)} %copy-done, s32[1,64]{1,0:T(1,128)S(1)} %copy-done.1, f32[1,64]{1,0:T(1,128)S(1)} %copy-done.2, ...), custom_call_target="tpu_custom_call" | custom-call | flops 1000 | bytes 1000 | tf_op jit(solution)/shard_map/numer_sums/pallas_call | solution.py:341
  18.6 0.9 %collective-permute-start.1 = (f32[4,4,2,8,8,128]{5,4,3,2,1,0:T(8,128)S(1)}, f32[4,4,2,8,8,128]{5,4,3,2,1,0:T(8,128)S(1)}, u32[]{:S(2)}, u32[]{:S(2)}) collective-permute-start(f32[4,4,2,8,8,128]{5,4,3,2,1,0:T(8,128)S(1)} %get-tuple-element.44), channel_id=1, source_target_pairs={{0,1},{1,0},{2,3},{3,2},{4,5},{5,4},{6,7},{7,6},{8,9},{9,8},{10,11... | collective-permute-start | bytes 3145736 | tf_op jit(solution)/shard_map/ppermute | solution.py:365
  19.6 0.8 %collective-permute-done.4 = f32[2,4,2,8,8,128]{5,4,3,2,1,0:T(8,128)S(1)} collective-permute-done((f32[2,4,2,8,8,128]{5,4,3,2,1,0:T(8,128)S(1)}, f32[2,4,2,8,8,128]{5,4,3,2,1,0:T(8,128)S(1)}, u32[]{:S(2)}, u32[]{:S(2)}) %collective-permute-start.4) | collective-permute-done | bytes 524320 | tf_op jit(solution)/shard_map/ppermute | solution.py:365
  20.6 1.0 %collective-permute-start.10 = (f32[1,4,2,8,8,128]{5,4,3,2,1,0:T(8,128)S(1)}, f32[1,4,2,8,8,128]{5,4,3,2,1,0:T(8,128)S(1)}, u32[]{:S(2)}, u32[]{:S(2)}) collective-permute-start(f32[1,4,2,8,8,128]{5,4,3,2,1,0:T(8,128)S(1)} %slice_add_fusion.12.refs_2_), channel_id=1, source_target_pairs={{0,2},{1,9},{2,0},{3,11},{4,6},{5,13},{6,4},{7,15},{8,10},{9,1},{1... | collective-permute-start | bytes 786440 | tf_op jit(solution)/shard_map/ppermute | solution.py:365
  21.6 0.2 collective-permute-done.1
  22.0 1.8 %collective-permute-start.2 = (f32[2,4,2,8,8,128]{5,4,3,2,1,0:T(8,128)S(1)}, f32[2,4,2,8,8,128]{5,4,3,2,1,0:T(8,128)S(1)}, u32[]{:S(2)}, u32[]{:S(2)}) collective-permute-start(f32[2,4,2,8,8,128]{5,4,3,2,1,0:T(8,128)S(1)} %get-tuple-element.52), channel_id=1, source_target_pairs={{0,2},{1,9},{2,0},{3,11},{4,6},{5,13},{6,4},{7,15},{8,10},{9,1},{1... | collective-permute-start | bytes 1572872 | tf_op jit(solution)/shard_map/ppermute | solution.py:365
  24.0 1.1 %collective-permute-start.7 = (f32[2,4,2,8,8,128]{5,4,3,2,1,0:T(8,128)S(1)}, f32[2,4,2,8,8,128]{5,4,3,2,1,0:T(8,128)S(1)}, u32[]{:S(2)}, u32[]{:S(2)}) collective-permute-start(f32[2,4,2,8,8,128]{5,4,3,2,1,0:T(8,128)S(1)} %get-tuple-element.54), channel_id=1, source_target_pairs={{0,6},{1,25},{2,4},{3,27},{4,2},{5,29},{6,0},{7,31},{8,14},{9,17},... | collective-permute-start | bytes 1572872 | tf_op jit(solution)/shard_map/ppermute | solution.py:365
  25.1 2.2 %collective-permute-start.9 = (f32[1,4,2,8,8,128]{5,4,3,2,1,0:T(8,128)S(1)}, f32[1,4,2,8,8,128]{5,4,3,2,1,0:T(8,128)S(1)}, u32[]{:S(2)}, u32[]{:S(2)}) collective-permute-start(f32[1,4,2,8,8,128]{5,4,3,2,1,0:T(8,128)S(1)} %slice_add_fusion.13.refs_1_), channel_id=1, source_target_pairs={{0,6},{1,25},{2,4},{3,27},{4,2},{5,29},{6,0},{7,31},{8,14},{9,17},... | collective-permute-start | bytes 786440 | tf_op jit(solution)/shard_map/ppermute | solution.py:365
  27.4 5.3 %collective-permute-done.2 = f32[2,4,2,8,8,128]{5,4,3,2,1,0:T(8,128)S(1)} collective-permute-done((f32[2,4,2,8,8,128]{5,4,3,2,1,0:T(8,128)S(1)}, f32[2,4,2,8,8,128]{5,4,3,2,1,0:T(8,128)S(1)}, u32[]{:S(2)}, u32[]{:S(2)}) %collective-permute-start.2) | collective-permute-done | bytes 524320 | tf_op jit(solution)/shard_map/ppermute | solution.py:365
  32.7 1.4 %collective-permute-start.3 = (f32[1,4,2,8,8,128]{5,4,3,2,1,0:T(8,128)S(1)}, f32[1,4,2,8,8,128]{5,4,3,2,1,0:T(8,128)S(1)}, u32[]{:S(2)}, u32[]{:S(2)}) collective-permute-start(f32[1,4,2,8,8,128]{5,4,3,2,1,0:T(8,128)S(1)} %slice_add_fusion.14), channel_id=1, source_target_pairs={{0,6},{1,25},{2,4},{3,27},{4,2},{5,29},{6,0},{7,31},{8,14},{9,17},... | collective-permute-start | bytes 786440 | tf_op jit(solution)/shard_map/ppermute | solution.py:365
  34.0 0.4 collective-permute-done.7
  34.6 2.7 %collective-permute-done.9 = f32[1,4,2,8,8,128]{5,4,3,2,1,0:T(8,128)S(1)} collective-permute-done((f32[1,4,2,8,8,128]{5,4,3,2,1,0:T(8,128)S(1)}, f32[1,4,2,8,8,128]{5,4,3,2,1,0:T(8,128)S(1)}, u32[]{:S(2)}, u32[]{:S(2)}) %collective-permute-start.9) | collective-permute-done | bytes 262176 | tf_op jit(solution)/shard_map/ppermute | solution.py:365
  37.3 3.0 %collective-permute-done.3 = f32[1,4,2,8,8,128]{5,4,3,2,1,0:T(8,128)S(1)} collective-permute-done((f32[1,4,2,8,8,128]{5,4,3,2,1,0:T(8,128)S(1)}, f32[1,4,2,8,8,128]{5,4,3,2,1,0:T(8,128)S(1)}, u32[]{:S(2)}, u32[]{:S(2)}) %collective-permute-start.3) | collective-permute-done | bytes 262176 | tf_op jit(solution)/shard_map/ppermute | solution.py:365
  40.4 0.6 collective-permute-done.8
  41.2 1.3 %collective-permute-start.11 = (f32[8,8,8,128]{3,2,1,0:T(8,128)S(1)}, f32[8,8,8,128]{3,2,1,0:T(8,128)S(1)}, u32[]{:S(2)}, u32[]{:S(2)}) collective-permute-start(f32[8,8,8,128]{3,2,1,0:T(8,128)S(1)} %get-tuple-element.55), channel_id=1, source_target_pairs={{0,8},{1,3},{2,10},{3,1},{4,12},{5,7},{6,14},{7,5},{8,0},{9,11},{1... | collective-permute-start | bytes 786440 | tf_op jit(solution)/shard_map/ppermute | solution.py:365
  42.5 2.6 %collective-permute-start.13 = (f32[8,8,8,128]{3,2,1,0:T(8,128)S(1)}, f32[8,8,8,128]{3,2,1,0:T(8,128)S(1)}, u32[]{:S(2)}, u32[]{:S(2)}) collective-permute-start(f32[8,8,8,128]{3,2,1,0:T(8,128)S(1)} %get-tuple-element.56), channel_id=1, source_target_pairs={{0,16},{1,5},{2,18},{3,7},{4,20},{5,1},{6,22},{7,3},{8,24},{9,13},... | collective-permute-start | bytes 786440 | tf_op jit(solution)/shard_map/ppermute | solution.py:365
  45.1 0.9 %collective-permute-start.12 = (f32[8,8,8,128]{3,2,1,0:T(8,128)S(1)}, f32[8,8,8,128]{3,2,1,0:T(8,128)S(1)}, u32[]{:S(2)}, u32[]{:S(2)}) collective-permute-start(f32[8,8,8,128]{3,2,1,0:T(8,128)S(1)} %get-tuple-element.57), channel_id=1, source_target_pairs={{0,24},{1,7},{2,26},{3,5},{4,28},{5,3},{6,30},{7,1},{8,16},{9,15},... | collective-permute-start | bytes 786440 | tf_op jit(solution)/shard_map/ppermute | solution.py:365
  46.0 1.7 %collective-permute-done.11 = f32[8,8,8,128]{3,2,1,0:T(8,128)S(1)} collective-permute-done((f32[8,8,8,128]{3,2,1,0:T(8,128)S(1)}, f32[8,8,8,128]{3,2,1,0:T(8,128)S(1)}, u32[]{:S(2)}, u32[]{:S(2)}) %collective-permute-start.11) | collective-permute-done | bytes 262176 | tf_op jit(solution)/shard_map/ppermute | solution.py:365
  47.6 4.7 %collective-permute-done.13 = f32[8,8,8,128]{3,2,1,0:T(8,128)S(1)} collective-permute-done((f32[8,8,8,128]{3,2,1,0:T(8,128)S(1)}, f32[8,8,8,128]{3,2,1,0:T(8,128)S(1)}, u32[]{:S(2)}, u32[]{:S(2)}) %collective-permute-start.13) | collective-permute-done | bytes 262176 | tf_op jit(solution)/shard_map/ppermute | solution.py:365
  52.3 2.7 %collective-permute-done.12 = f32[8,8,8,128]{3,2,1,0:T(8,128)S(1)} collective-permute-done((f32[8,8,8,128]{3,2,1,0:T(8,128)S(1)}, f32[8,8,8,128]{3,2,1,0:T(8,128)S(1)}, u32[]{:S(2)}, u32[]{:S(2)}) %collective-permute-start.12) | collective-permute-done | bytes 262176 | tf_op jit(solution)/shard_map/ppermute | solution.py:365
  55.1 2.0 %collective-permute-start.14 = (f32[4,8,8,128]{3,2,0,1:T(8,128)S(1)}, f32[4,8,8,128]{3,2,0,1:T(8,128)S(1)}, u32[]{:S(2)}, u32[]{:S(2)}) collective-permute-start(f32[4,8,8,128]{3,2,0,1:T(8,128)S(1)} %slice.258), channel_id=1, source_target_pairs={{0,32},{1,33},{2,34},{3,35},{4,36},{5,37},{6,38},{7,39},{8,40},{9,... | collective-permute-start | bytes 393224 | tf_op jit(solution)/shard_map/ppermute | solution.py:365
  57.1 3.1 %collective-permute-done.14 = f32[4,8,8,128]{3,2,0,1:T(8,128)S(1)} collective-permute-done((f32[4,8,8,128]{3,2,0,1:T(8,128)S(1)}, f32[4,8,8,128]{3,2,0,1:T(8,128)S(1)}, u32[]{:S(2)}, u32[]{:S(2)}) %collective-permute-start.14) | collective-permute-done | bytes 131104 | tf_op jit(solution)/shard_map/ppermute | solution.py:365
  60.2 4.1 %collective-permute-start.15 = (f32[2,8,8,128]{3,2,0,1:T(8,128)S(1)}, f32[2,8,8,128]{3,2,0,1:T(8,128)S(1)}, u32[]{:S(2)}, u32[]{:S(2)}) collective-permute-start(f32[2,8,8,128]{3,2,0,1:T(8,128)S(1)} %get-tuple-element.59), channel_id=1, source_target_pairs={{0,64},{1,65},{2,66},{3,67},{4,68},{5,69},{6,70},{7,71},{8,72},{9,... | collective-permute-start | bytes 196616 | tf_op jit(solution)/shard_map/ppermute | solution.py:365
  64.2 2.3 %collective-permute-done.15 = f32[2,8,8,128]{3,2,0,1:T(8,128)S(1)} collective-permute-done((f32[2,8,8,128]{3,2,0,1:T(8,128)S(1)}, f32[2,8,8,128]{3,2,0,1:T(8,128)S(1)}, u32[]{:S(2)}, u32[]{:S(2)}) %collective-permute-start.15) | collective-permute-done | bytes 65568 | tf_op jit(solution)/shard_map/ppermute | solution.py:365
  66.5 7.4 %collective-permute-start.16 = (f32[1,8,8,128]{3,2,0,1:T(8,128)S(1)}, f32[1,8,8,128]{3,2,0,1:T(8,128)S(1)}, u32[]{:S(2)}, u32[]{:S(2)}) collective-permute-start(f32[1,8,8,128]{3,2,0,1:T(8,128)S(1)} %slice_add_fusion.18), channel_id=1, source_target_pairs={{0,128},{1,129},{2,130},{3,131},{4,132},{5,133},{6,134},{7,135},{8... | collective-permute-start | bytes 98312 | tf_op jit(solution)/shard_map/ppermute | solution.py:365
  73.9 1.9 %collective-permute-done.16 = f32[1,8,8,128]{3,2,0,1:T(8,128)S(1)} collective-permute-done((f32[1,8,8,128]{3,2,0,1:T(8,128)S(1)}, f32[1,8,8,128]{3,2,0,1:T(8,128)S(1)}, u32[]{:S(2)}, u32[]{:S(2)}) %collective-permute-start.16) | collective-permute-done | bytes 32800 | tf_op jit(solution)/shard_map/ppermute | solution.py:365
  75.8 0.6 fusion.16
  (32 shorter events, 1.3 us)
Async XLA Ops:
  4.3 4.2 %collective-permute-start = (f32[2,4,4,2,8,8,128]{6,5,4,3,2,1,0:T(8,128)S(1)}, f32[2,4,4,2,8,8,128]{6,5,4,3,2,1,0:T(8,128)S(1)}, u32[]{:S(2)}, u32[]{:S(2)}) collective-permute-start(f32[2,4,4,2,8,8,128]{6,5,4,3,2,1,0:T(8,128)S(1)} %get-tuple-element.41), channel_id=1, source_target_pairs={{0,1},{1,0},{2,3},{3,2},{4,5},{5,4},{6,7},{7,6},{8,9},{9,8},{10,11... | collective-permute-start | bytes 6291464 | tf_op jit(solution)/shard_map/ppermute | solution.py:365
  8.5 2.7 %copy-start = (s32[1,64]{1,0:T(1,128)S(1)}, s32[1,64]{1,0:T(1,128)}, u32[]{:S(2)}) copy-start(s32[1,64]{1,0:T(1,128)} %owner_ref.1) | copy-start | bytes 772
  8.5 2.7 %copy-start.1 = (s32[1,64]{1,0:T(1,128)S(1)}, s32[1,64]{1,0:T(1,128)}, u32[]{:S(2)}) copy-start(s32[1,64]{1,0:T(1,128)} %offset_ref.1) | copy-start | bytes 772
  8.5 2.7 %copy-start.2 = (f32[1,64]{1,0:T(1,128)S(1)}, f32[1,64]{1,0:T(1,128)}, u32[]{:S(2)}) copy-start(f32[1,64]{1,0:T(1,128)} %weight_ref.1) | copy-start | bytes 772
  8.9 10.6 %collective-permute-start.5 = (f32[2,4,2,8,8,128]{5,4,3,2,1,0:T(8,128)S(1)}, f32[2,4,2,8,8,128]{5,4,3,2,1,0:T(8,128)S(1)}, u32[]{:S(2)}, u32[]{:S(2)}) collective-permute-start(f32[2,4,2,8,8,128]{5,4,3,2,1,0:T(8,128)S(1)} %get-tuple-element.49.after_1), channel_id=1, source_target_pairs={{0,6},{1,25},{2,4},{3,27},{4,2},{5,29},{6,0},{7,31},{8,14},{9,17},... | collective-permute-start | bytes 1572872 | tf_op jit(solution)/shard_map/ppermute | solution.py:365
  11.2 9.2 %collective-permute-start.4 = (f32[2,4,2,8,8,128]{5,4,3,2,1,0:T(8,128)S(1)}, f32[2,4,2,8,8,128]{5,4,3,2,1,0:T(8,128)S(1)}, u32[]{:S(2)}, u32[]{:S(2)}) collective-permute-start(f32[2,4,2,8,8,128]{5,4,3,2,1,0:T(8,128)S(1)} %get-tuple-element.50.after_0), channel_id=1, source_target_pairs={{0,2},{1,9},{2,0},{3,11},{4,6},{5,13},{6,4},{7,15},{8,10},{9,1},{1... | collective-permute-start | bytes 1572872 | tf_op jit(solution)/shard_map/ppermute | solution.py:365
  18.6 3.2 %collective-permute-start.1 = (f32[4,4,2,8,8,128]{5,4,3,2,1,0:T(8,128)S(1)}, f32[4,4,2,8,8,128]{5,4,3,2,1,0:T(8,128)S(1)}, u32[]{:S(2)}, u32[]{:S(2)}) collective-permute-start(f32[4,4,2,8,8,128]{5,4,3,2,1,0:T(8,128)S(1)} %get-tuple-element.44), channel_id=1, source_target_pairs={{0,1},{1,0},{2,3},{3,2},{4,5},{5,4},{6,7},{7,6},{8,9},{9,8},{10,11... | collective-permute-start | bytes 3145736 | tf_op jit(solution)/shard_map/ppermute | solution.py:365
  20.5 3.4 %collective-permute-start.6 = (f32[4,4,2,8,8,128]{5,4,3,2,1,0:T(8,128)S(1)}, f32[4,4,2,8,8,128]{5,4,3,2,1,0:T(8,128)S(1)}, u32[]{:S(2)}, u32[]{:S(2)}) collective-permute-start(f32[4,4,2,8,8,128]{5,4,3,2,1,0:T(8,128)S(1)} %hold.3), channel_id=1, source_target_pairs={{0,1},{1,0},{2,3},{3,2},{4,5},{5,4},{6,7},{7,6},{8,9},{9,8},{10,11... | collective-permute-start | bytes 3145736 | tf_op jit(solution)/shard_map/ppermute | solution.py:365
  20.6 6.8 %collective-permute-start.10 = (f32[1,4,2,8,8,128]{5,4,3,2,1,0:T(8,128)S(1)}, f32[1,4,2,8,8,128]{5,4,3,2,1,0:T(8,128)S(1)}, u32[]{:S(2)}, u32[]{:S(2)}) collective-permute-start(f32[1,4,2,8,8,128]{5,4,3,2,1,0:T(8,128)S(1)} %slice_add_fusion.12.refs_2_), channel_id=1, source_target_pairs={{0,2},{1,9},{2,0},{3,11},{4,6},{5,13},{6,4},{7,15},{8,10},{9,1},{1... | collective-permute-start | bytes 786440 | tf_op jit(solution)/shard_map/ppermute | solution.py:365
  22.0 10.6 %collective-permute-start.2 = (f32[2,4,2,8,8,128]{5,4,3,2,1,0:T(8,128)S(1)}, f32[2,4,2,8,8,128]{5,4,3,2,1,0:T(8,128)S(1)}, u32[]{:S(2)}, u32[]{:S(2)}) collective-permute-start(f32[2,4,2,8,8,128]{5,4,3,2,1,0:T(8,128)S(1)} %get-tuple-element.52), channel_id=1, source_target_pairs={{0,2},{1,9},{2,0},{3,11},{4,6},{5,13},{6,4},{7,15},{8,10},{9,1},{1... | collective-permute-start | bytes 1572872 | tf_op jit(solution)/shard_map/ppermute | solution.py:365
  24.0 10.5 %collective-permute-start.7 = (f32[2,4,2,8,8,128]{5,4,3,2,1,0:T(8,128)S(1)}, f32[2,4,2,8,8,128]{5,4,3,2,1,0:T(8,128)S(1)}, u32[]{:S(2)}, u32[]{:S(2)}) collective-permute-start(f32[2,4,2,8,8,128]{5,4,3,2,1,0:T(8,128)S(1)} %get-tuple-element.54), channel_id=1, source_target_pairs={{0,6},{1,25},{2,4},{3,27},{4,2},{5,29},{6,0},{7,31},{8,14},{9,17},... | collective-permute-start | bytes 1572872 | tf_op jit(solution)/shard_map/ppermute | solution.py:365
  25.1 12.2 %collective-permute-start.9 = (f32[1,4,2,8,8,128]{5,4,3,2,1,0:T(8,128)S(1)}, f32[1,4,2,8,8,128]{5,4,3,2,1,0:T(8,128)S(1)}, u32[]{:S(2)}, u32[]{:S(2)}) collective-permute-start(f32[1,4,2,8,8,128]{5,4,3,2,1,0:T(8,128)S(1)} %slice_add_fusion.13.refs_1_), channel_id=1, source_target_pairs={{0,6},{1,25},{2,4},{3,27},{4,2},{5,29},{6,0},{7,31},{8,14},{9,17},... | collective-permute-start | bytes 786440 | tf_op jit(solution)/shard_map/ppermute | solution.py:365
  32.7 7.7 %collective-permute-start.3 = (f32[1,4,2,8,8,128]{5,4,3,2,1,0:T(8,128)S(1)}, f32[1,4,2,8,8,128]{5,4,3,2,1,0:T(8,128)S(1)}, u32[]{:S(2)}, u32[]{:S(2)}) collective-permute-start(f32[1,4,2,8,8,128]{5,4,3,2,1,0:T(8,128)S(1)} %slice_add_fusion.14), channel_id=1, source_target_pairs={{0,6},{1,25},{2,4},{3,27},{4,2},{5,29},{6,0},{7,31},{8,14},{9,17},... | collective-permute-start | bytes 786440 | tf_op jit(solution)/shard_map/ppermute | solution.py:365
  34.5 6.5 %collective-permute-start.8 = (f32[1,4,2,8,8,128]{5,4,3,2,1,0:T(8,128)S(1)}, f32[1,4,2,8,8,128]{5,4,3,2,1,0:T(8,128)S(1)}, u32[]{:S(2)}, u32[]{:S(2)}) collective-permute-start(f32[1,4,2,8,8,128]{5,4,3,2,1,0:T(8,128)S(1)} %slice_add_fusion.10), channel_id=1, source_target_pairs={{0,2},{1,9},{2,0},{3,11},{4,6},{5,13},{6,4},{7,15},{8,10},{9,1},{1... | collective-permute-start | bytes 786440 | tf_op jit(solution)/shard_map/ppermute | solution.py:365
  41.2 6.5 %collective-permute-start.11 = (f32[8,8,8,128]{3,2,1,0:T(8,128)S(1)}, f32[8,8,8,128]{3,2,1,0:T(8,128)S(1)}, u32[]{:S(2)}, u32[]{:S(2)}) collective-permute-start(f32[8,8,8,128]{3,2,1,0:T(8,128)S(1)} %get-tuple-element.55), channel_id=1, source_target_pairs={{0,8},{1,3},{2,10},{3,1},{4,12},{5,7},{6,14},{7,5},{8,0},{9,11},{1... | collective-permute-start | bytes 786440 | tf_op jit(solution)/shard_map/ppermute | solution.py:365
  42.5 9.8 %collective-permute-start.13 = (f32[8,8,8,128]{3,2,1,0:T(8,128)S(1)}, f32[8,8,8,128]{3,2,1,0:T(8,128)S(1)}, u32[]{:S(2)}, u32[]{:S(2)}) collective-permute-start(f32[8,8,8,128]{3,2,1,0:T(8,128)S(1)} %get-tuple-element.56), channel_id=1, source_target_pairs={{0,16},{1,5},{2,18},{3,7},{4,20},{5,1},{6,22},{7,3},{8,24},{9,13},... | collective-permute-start | bytes 786440 | tf_op jit(solution)/shard_map/ppermute | solution.py:365
  45.1 10.0 %collective-permute-start.12 = (f32[8,8,8,128]{3,2,1,0:T(8,128)S(1)}, f32[8,8,8,128]{3,2,1,0:T(8,128)S(1)}, u32[]{:S(2)}, u32[]{:S(2)}) collective-permute-start(f32[8,8,8,128]{3,2,1,0:T(8,128)S(1)} %get-tuple-element.57), channel_id=1, source_target_pairs={{0,24},{1,7},{2,26},{3,5},{4,28},{5,3},{6,30},{7,1},{8,16},{9,15},... | collective-permute-start | bytes 786440 | tf_op jit(solution)/shard_map/ppermute | solution.py:365
  55.1 5.1 %collective-permute-start.14 = (f32[4,8,8,128]{3,2,0,1:T(8,128)S(1)}, f32[4,8,8,128]{3,2,0,1:T(8,128)S(1)}, u32[]{:S(2)}, u32[]{:S(2)}) collective-permute-start(f32[4,8,8,128]{3,2,0,1:T(8,128)S(1)} %slice.258), channel_id=1, source_target_pairs={{0,32},{1,33},{2,34},{3,35},{4,36},{5,37},{6,38},{7,39},{8,40},{9,... | collective-permute-start | bytes 393224 | tf_op jit(solution)/shard_map/ppermute | solution.py:365
  60.2 6.3 %collective-permute-start.15 = (f32[2,8,8,128]{3,2,0,1:T(8,128)S(1)}, f32[2,8,8,128]{3,2,0,1:T(8,128)S(1)}, u32[]{:S(2)}, u32[]{:S(2)}) collective-permute-start(f32[2,8,8,128]{3,2,0,1:T(8,128)S(1)} %get-tuple-element.59), channel_id=1, source_target_pairs={{0,64},{1,65},{2,66},{3,67},{4,68},{5,69},{6,70},{7,71},{8,72},{9,... | collective-permute-start | bytes 196616 | tf_op jit(solution)/shard_map/ppermute | solution.py:365
  66.5 9.3 %collective-permute-start.16 = (f32[1,8,8,128]{3,2,0,1:T(8,128)S(1)}, f32[1,8,8,128]{3,2,0,1:T(8,128)S(1)}, u32[]{:S(2)}, u32[]{:S(2)}) collective-permute-start(f32[1,8,8,128]{3,2,0,1:T(8,128)S(1)} %slice_add_fusion.18), channel_id=1, source_target_pairs={{0,128},{1,129},{2,130},{3,131},{4,132},{5,133},{6,134},{7,135},{8... | collective-permute-start | bytes 98312 | tf_op jit(solution)/shard_map/ppermute | solution.py:365
